TPU v7x, 256 devices: a whole 4x4x8 slice. The times are simulated.
256 devices in a mesh: frame: 32 (over z, x_hi, core), chan: 8 (over y, x_lo).
Axes of the slice: x: 4 (x_hi: 2, x_lo: 2; x = x_hi * 2 + x_lo), y: 4, z: 8, core: 2. Of those that a mesh axis runs over, the one named last changes fastest.
Arguments:
- inputs: bfloat16 [32, 128, 32, 1024], P('frame', None, None, 'chan'), may hold values from -6 to 6
- cotangent: bfloat16 [32, 128, 32, 1024], P('frame', None, None, 'chan'), may hold values from -6 to 6
- spatial_weight: bfloat16 [9, 128, 128], replicated, may hold values from -0.1875 to 0.1875
- temporal_weight: bfloat16 [3, 128, 128], replicated, may hold values from -0.3125 to 0.3125
- norm_gain: float32 [128], replicated, may hold values from 0.1 to 1.9
- norm_shift: float32 [128], replicated, may hold values from -3 to 3
- spatial_bias: float32 [128], replicated, may hold values from -3 to 3
Outputs:
- output: bfloat16 [32, 128, 32, 1024], P('frame', None, None, 'chan')
- input_grad: bfloat16 [32, 128, 32, 1024], P('frame', None, None, 'chan')
- spatial_grad: float32 [9, 128, 128], replicated
- temporal_grad: float32 [3, 128, 128], replicated
All inputs are finite; a program needn't handle non-finite values.
Results may differ from a plain program's by a relative error of at most 0.00105.
The roundings to bfloat16 on the way count: a program that leaves them out, or rounds other values in their place, can miss the bound.
Values may be sent and summed in bfloat16 or wider, within the bound.
No kernel may reach another device: no remote copies, remote signals or barrier semaphores. Data moves between devices by JAX's collectives and lax.ppermute only.
A program may use at most 128 MiB of HBM per device.

v0:
```python
import functools

import jax
import jax.numpy as jnp
from jax import lax
from jax.experimental import pallas as pl
from jax.experimental.pallas import tpu as pltpu
from jax.sharding import PartitionSpec as P

GROUPS = 32
LANES = 128
TILE = 512
MIB = 1024 * 1024
CONTRACT_LAST = (((1,), (1,)), ((), ()))
F32, BF16 = jnp.float32, jnp.bfloat16


def partner(bits, frames):
    return [(f, f ^ bits) for f in range(frames)]


def both(frame_bits, chan_bits, frames, peers):
    return [(f * peers + c, (f ^ frame_bits) * peers + (c ^ chan_bits)) for f in range(frames) for c in range(peers)]


def neighbour(frames):
    pairs = []
    for f in range(frames):
        target = f + 1 if f % 2 else f - 1
        if 0 <= target < frames:
            pairs.append((f, target))
    return pairs


def call(kernel, outs, ins, scratch=(), cost=(0, 0), limit=24):
    smem = pl.BlockSpec(memory_space=pltpu.SMEM)
    vmem = pl.BlockSpec(memory_space=pltpu.VMEM)
    is_place = lambda v: v.dtype == jnp.int32
    flops, moved = cost
    return pl.pallas_call(
        kernel,
        out_shape=[jax.ShapeDtypeStruct(s, d) for s, d in outs],
        in_specs=[smem if is_place(v) else vmem for v in ins],
        out_specs=[vmem] * len(outs),
        scratch_shapes=list(scratch),
        cost_estimate=pl.CostEstimate(flops=flops, bytes_accessed=moved, transcendentals=0),
        compiler_params=pltpu.CompilerParams(vmem_limit_bytes=limit * MIB),
    )(*ins)


def lane_index(shape=(LANES, LANES)):
    return lax.broadcasted_iota(jnp.int32, shape, len(shape) - 1)


def row_at(r):
    return pl.ds(pl.multiple_of(r * LANES, LANES), LANES)


def tile_at(n, extra=0):
    return pl.ds(pl.multiple_of(n * TILE, LANES) + extra, TILE)


def group_sum(v):
    lane = lax.broadcasted_iota(jnp.int32, v.shape, 1)
    for step in (1, 2):
        up, down = pltpu.roll(v, LANES - step, 1), pltpu.roll(v, step, 1)
        v = v + jnp.where((lane // step) % 2 == 0, up, down)
    return v


def sigmoid(v):
    return 1.0 / (1.0 + jnp.exp(-v))


def selector(n, rows):
    pixel = lax.broadcasted_iota(jnp.int32, (LANES, TILE), 1) + n * TILE
    at = lax.broadcasted_iota(jnp.int32, (LANES, TILE), 0)
    low = (at < rows) & (pixel == at * LANES)
    high = (at >= 64) & (pixel == (at - 64) * LANES + (LANES - 1))
    return jnp.where(low | high | (at == 32), 1.0, 0.0).astype(BF16)


def turn(raw):
    return jnp.swapaxes(raw, 0, 1)


def store_shifts(ref, row, halo, r, lane, order):
    left = jnp.where(lane == 0, pltpu.roll(halo, LANES - 32 - r, 1), pltpu.roll(row, 1, 1))
    right = jnp.where(lane == LANES - 1, pltpu.roll(halo, 63 - r, 1), pltpu.roll(row, LANES - 1, 1))
    shifts = (left, row, right)
    for slot, which in enumerate(order):
        ref[slot * LANES : (slot + 1) * LANES, row_at(r + 1)] = shifts[which].astype(BF16)


def turn_kernel(raw_ref, low_ref, high_ref):
    channels, rows, _ = raw_ref.shape
    for c in range(0, channels, 16):
        block = turn(raw_ref[c : c + 16])
        for r in range(rows):
            ref, at = (low_ref, r) if r < rows // 2 else (high_ref, r - rows // 2)
            ref[c : c + 16, at * LANES : (at + 1) * LANES] = block[r]


def sums_kernel(me_ref, raw_ref, out_ref, payload_ref):
    channels, rows, _ = raw_ref.shape
    me = me_ref[0]
    for c in range(0, channels, 16):
        block = turn(raw_ref[c : c + 16])
        for r in range(rows):
            out_ref[c : c + 16, r * LANES : (r + 1) * LANES] = block[r]
    packed = jnp.zeros((LANES, channels), F32)
    for n in range(rows * LANES // TILE):
        packed += lax.dot_general(selector(n, rows), out_ref[:, n * TILE : (n + 1) * TILE], CONTRACT_LAST, preferred_element_type=F32)
    mean = packed[32:33] / (rows * LANES)
    mean_all = jnp.broadcast_to(mean, (LANES, channels)).T

    def square(r, acc):
        off = out_ref[:, row_at(r)].astype(F32) - mean_all
        return acc + off * off

    squares = lax.fori_loop(0, rows, square, jnp.zeros((channels, LANES), F32), unroll=4)
    squares = jnp.sum(squares.T, axis=0, keepdims=True)
    head = jnp.concatenate([mean, squares, jnp.zeros((6, channels), F32)], axis=0)
    for peer in range(payload_ref.shape[0]):
        payload_ref[peer, 0:8, :] = head
        payload_ref[peer, 8 : 8 + rows, :] = jnp.where(peer < me, packed[0:rows], packed[64 : 64 + rows])


def forward_kernel(me_ref, plane_ref, received_ref, table_ref, weight_ref, act_ref, hidden_ref, slope_ref, columns_ref):
    channels, pixels = plane_ref.shape
    rows = pixels // LANES
    peers = received_ref.shape[0]
    me = me_ref[0]
    lane = lane_index()
    count = (channels // GROUPS) * pixels * peers
    means, squares = received_ref[:, 0, :], received_ref[:, 1, :]
    center = group_sum(jnp.sum(means, axis=0, keepdims=True)) * (GROUPS / (channels * peers))
    off = means - center
    spread = group_sum(jnp.sum(squares + pixels * (off * off), axis=0, keepdims=True)) / count
    inverse = lax.rsqrt(spread + 1e-05)
    low = received_ref[jnp.maximum(me - 1, 0), 8 : 8 + rows, :]
    high = received_ref[jnp.minimum(me + 1, peers - 1), 8 : 8 + rows, :]
    head = jnp.concatenate([center, inverse, table_ref[0:6, :]], axis=0)
    gap = jnp.zeros((24, LANES), F32)
    columns = jnp.concatenate([head, gap, low, high, jnp.zeros((32, LANES), F32)], axis=0).T
    columns_ref[...] = columns
    wide = lambda at: jnp.broadcast_to(columns[:, at : at + 1], (channels, LANES))
    center_w, inverse_w, gain_w, shift_w, bias_w = [wide(at) for at in range(5)]

    def activate(v):
        v = (v - center_w) * inverse_w * gain_w + shift_w
        return v * sigmoid(v)

    inside = ((lane < 64) & (me > 0)) | ((lane >= 64) & (me < peers - 1))
    halo = jnp.where(inside, activate(columns), 0.0)
    nothing = jnp.zeros((3 * channels, LANES), BF16)
    act_ref[:, 0:LANES] = nothing
    act_ref[:, (rows + 1) * LANES : (rows + 2) * LANES] = nothing

    def shape_row(r, carry):
        row = activate(plane_ref[:, row_at(r)].astype(F32))
        store_shifts(act_ref, row, halo, r, lane, (0, 1, 2))
        return carry

    lax.fori_loop(0, rows, shape_row, 0, unroll=2)
    weights = [jnp.concatenate([weight_ref[3 * dy + dx] for dx in range(3)], axis=1) for dy in range(3)]
    bias = jnp.broadcast_to(bias_w[:, 0:1], (channels, TILE))

    def conv(n, carry):
        value = bias
        for dy in range(3):
            value = value + jnp.dot(weights[dy], act_ref[:, tile_at(n, dy * LANES)], preferred_element_type=F32)
        logistic = sigmoid(value)
        hidden_ref[:, tile_at(n)] = (value * logistic).astype(BF16)
        slope_ref[:, tile_at(n)] = logistic * (1.0 + value * (1.0 - logistic))
        return carry

    lax.fori_loop(0, pixels // TILE, conv, 0)


def backward_kernel(last, me_ref, act_ref, hidden_ref, slope_ref, grad_ref, mate_ref, cross_ref, weight_ref, *rest):
    if last:
        early_in, late_in, packed_in, pre_ref, terms_ref, low_ref, high_ref, early, late = rest
    else:
        pre_ref, early, late, packed_ref = rest
    channels, pixels = grad_ref.shape
    rows = 2 * pixels // LANES
    core, spot = me_ref[1], me_ref[2]
    first = pixels // TILE if last else 0
    turned = [weight_ref[k].astype(F32).T for k in range(3)]
    even = core == 0
    ahead = jnp.where(even, turned[0], turned[2])
    behind = jnp.where(even, turned[2], turned[0])
    weights = jnp.concatenate([turned[1], ahead, behind], axis=1).astype(BF16)
    early[...] = early_in[...] if last else jnp.zeros(early.shape, F32)
    late[...] = late_in[...] if last else jnp.zeros(late.shape, F32)

    def step(n, packed):
        whole = n + first
        grads = jnp.concatenate([ref[:, tile_at(n)] for ref in (grad_ref, mate_ref, cross_ref)], axis=0)
        back = jnp.dot(weights, grads, preferred_element_type=F32)
        pre = (back * slope_ref[:, tile_at(whole)]).astype(BF16)
        pre_ref[:, tile_at(n)] = pre
        early[...] += lax.dot_general(grads, hidden_ref[:, tile_at(whole)], CONTRACT_LAST, preferred_element_type=F32)
        for dy in range(3):
            late[dy] += lax.dot_general(pre, act_ref[:, tile_at(whole, dy * LANES)], CONTRACT_LAST, preferred_element_type=F32)
        return packed + lax.dot_general(selector(whole, rows), pre, CONTRACT_LAST, preferred_element_type=F32)

    packed = lax.fori_loop(0, pixels // TILE, step, packed_in[...] if last else jnp.zeros((LANES, channels), F32))
    if not last:
        packed_ref[...] = packed
        return
    low_ref[...] = packed[0:rows]
    high_ref[...] = packed[64 : 64 + rows]
    own, mate, cross = [early[i * channels : (i + 1) * channels, :] for i in range(3)]
    blocks = [late[t // 3, :, (t % 3) * LANES : (t % 3 + 1) * LANES] for t in range(9)]
    blocks += [jnp.where(even, mate, cross), own, jnp.where(even, cross, mate)]
    part = terms_ref.shape[2]
    for t, block in enumerate(blocks):
        for v in range(channels // 64):
            at = (t * channels + v * 64) // part
            offset = (t * channels + v * 64) % part
            half = jnp.where(core == at % 2, 0, 1)
            terms_ref[half, at // 2 ^ spot, offset : offset + 64, :] = block[v * 64 : (v + 1) * 64]


def input_kernel(early_ref, late_ref, low_ref, high_ref, weight_ref, plane_ref, columns_ref, scaled_ref, sums_ref, padded):
    channels, pixels = plane_ref.shape
    rows = pixels // LANES
    lane = lane_index()
    blank = jnp.zeros((32, LANES), F32)
    halo = jnp.concatenate([blank, low_ref[...], high_ref[...], blank], axis=0).T
    nothing = jnp.zeros((3 * channels, LANES), BF16)
    padded[:, 0:LANES] = nothing
    padded[:, (rows + 1) * LANES : (rows + 2) * LANES] = nothing

    for first, ref in ((0, early_ref), (rows // 2, late_ref)):

        def shift_row(r, carry, ref=ref, first=first):
            store_shifts(padded, ref[:, row_at(r)].astype(F32), halo, r + first, lane, (2, 1, 0))
            return carry

        lax.fori_loop(0, rows // 2, shift_row, 0, unroll=2)
    weights = [
        jnp.concatenate([weight_ref[3 * dy + dx].astype(F32).T for dx in range(3)], axis=1).astype(BF16) for dy in range(3)
    ]
    columns = columns_ref[...]
    wide = lambda at: jnp.broadcast_to(columns[:, at : at + 1], (channels, LANES))
    center, inverse, gain, shift = [wide(at) for at in range(4)]

    def step(n, carry):
        plain, crossed = carry
        value = jnp.zeros((channels, TILE), F32)
        for dy in range(3):
            value = value + jnp.dot(weights[dy], padded[:, tile_at(n, (2 - dy) * LANES)], preferred_element_type=F32)
        for i in range(TILE // LANES):
            at = row_at(n * (TILE // LANES) + i)
            normed = (plane_ref[:, at].astype(F32) - center) * inverse
            shaped = normed * gain + shift
            logistic = sigmoid(shaped)
            field = value[:, i * LANES : (i + 1) * LANES] * (logistic * (1.0 + shaped * (1.0 - logistic)))
            scaled = field * gain
            scaled_ref[:, at] = scaled
            plain, crossed = plain + scaled, crossed + scaled * normed
        return plain, crossed

    zero = jnp.zeros((channels, LANES), F32)
    plain, crossed = lax.fori_loop(0, pixels // TILE, step, (zero, zero))
    plain, crossed = [jnp.sum(v, axis=1, keepdims=True) for v in (plain, crossed)]
    sums_ref[...] = jnp.where(lane == 0, plain, jnp.where(lane == 1, crossed, 0.0)).T[0:8]


def output_kernel(me_ref, hidden_ref, mate_ref, cross_ref, weight_ref, raw_ref, out_ref, flat):
    channels, rows, _ = raw_ref.shape
    even = me_ref[1] == 0
    pick = lambda a, b: jnp.where(even, weight_ref[a].astype(F32), weight_ref[b].astype(F32)).astype(BF16)
    weights = jnp.concatenate([weight_ref[1], pick(2, 0), pick(0, 2)], axis=1)
    each = TILE // LANES

    def step(n, carry):
        frames = jnp.concatenate([ref[:, tile_at(n)] for ref in (hidden_ref, mate_ref, cross_ref)], axis=0)
        mixed = jnp.dot(weights, frames, preferred_element_type=F32)
        for i in range(each):
            flat[n * each + i] = mixed[:, i * LANES : (i + 1) * LANES]
        return carry

    lax.fori_loop(0, rows // each, step, 0)
    for c in range(0, channels, 16):
        out_ref[c : c + 16] = (raw_ref[c : c + 16].astype(F32) + turn(flat[:, c : c + 16, :])).astype(BF16)


def final_kernel(own_ref, one_ref, two_ref, three_ref, scaled_ref, plane_ref, columns_ref, raw_ref, out_ref, flat):
    channels, rows, _ = raw_ref.shape
    count = (channels // GROUPS) * rows * LANES * 8
    at = own_ref.shape[0] - 8
    totals = (own_ref[at:, :] + one_ref[at:, :]) + (two_ref[at:, :] + three_ref[at:, :])
    totals = group_sum(totals) / count
    turned = jnp.concatenate([totals, jnp.zeros((LANES - 8, LANES), F32)], axis=0).T
    wide = lambda v, at: jnp.broadcast_to(v[:, at : at + 1], (channels, LANES))
    mean_grad, second = wide(turned, 0), wide(turned, 1)
    columns = columns_ref[...]
    center, inverse = wide(columns, 0), wide(columns, 1)

    def step(r, carry):
        normed = (plane_ref[:, row_at(r)].astype(F32) - center) * inverse
        flat[r] = inverse * (scaled_ref[:, row_at(r)] - mean_grad - normed * second)
        return carry

    lax.fori_loop(0, rows, step, 0, unroll=2)
    for c in range(0, channels, 16):
        out_ref[c : c + 16] = (raw_ref[c : c + 16].astype(F32) + turn(flat[:, c : c + 16, :])).astype(BF16)


def place_kernel(me_ref, own_ref, mate_ref, spatial_ref, temporal_ref, whole):
    core, spot = me_ref[1], me_ref[2]
    part = whole.shape[1]
    for slot in range(4):
        at = 2 * (slot ^ spot)
        whole[at + core] = own_ref[slot, 0:part]
        whole[at + 1 - core] = mate_ref[slot, 0:part]
    split = spatial_ref.shape[0] // part
    spatial_ref[...] = whole[0:split].reshape(spatial_ref.shape)
    temporal_ref[...] = whole[split:].reshape(temporal_ref.shape)


def body(inputs, cotangent, spatial_weight, temporal_weight, norm_gain, norm_shift, spatial_bias):
    frames = lax.axis_size("frame")
    peers = lax.axis_size("chan")
    core = lax.axis_index("frame") % 2
    me = lax.axis_index("chan")
    channels, rows, cols = inputs.shape[1:]
    pixels = rows * cols
    plane, half = (channels, pixels), (channels, pixels // 2)
    tied = lax.optimization_barrier
    place = jnp.stack([me, core, me // 2]).astype(jnp.int32)
    table = jnp.pad(jnp.stack([norm_gain, norm_shift, spatial_bias]), ((0, 5), (0, 0)))
    raw_in, raw_grad = inputs[0], cotangent[0]
    cross = lambda v: lax.ppermute(v, "frame", neighbour(frames))
    mate = lambda v: lax.ppermute(v, "frame", partner(1, frames))

    def meet(v, frame_bits, chan_bits):
        return lax.ppermute(v, ("frame", "chan"), both(frame_bits, chan_bits, frames, peers))

    def total(v, steps):
        got = [v] + [meet(v, *step) for step in steps]
        return got[0] + got[1] if len(got) == 2 else (got[0] + got[1]) + (got[2] + got[3])

    grads = call(turn_kernel, [(half, BF16)] * 2, [raw_grad], cost=(0, 2 * MIB), limit=8)
    raw_in, early_grad, table, place = tied((raw_in, grads[0], table, place))
    crossed = [cross(early_grad)]
    turned, payload = call(
        sums_kernel, [(plane, BF16), ((peers, 8 + rows, channels), F32)], [place, raw_in], cost=(0, 2 * MIB), limit=8
    )
    received = lax.all_to_all(payload, "chan", 0, 0, tiled=True)
    early_grad, late_grad, received = tied((early_grad, grads[1], received))
    grads = [early_grad, late_grad]
    crossed.append(cross(late_grad))
    mates = [mate(v) for v in grads]

    padded = (3 * channels, pixels + 2 * cols)
    act, hidden, slope, columns = call(
        forward_kernel,
        [(padded, BF16), (plane, BF16), (plane, F32), ((channels, LANES), F32)],
        [place, turned, received, table, spatial_weight],
        cost=(1000, MIB),
        limit=16,
    )
    early_shape, late_shape = (3 * channels, channels), (3, channels, 3 * channels)
    pre_early, *sums = call(
        functools.partial(backward_kernel, False),
        [(half, BF16), (early_shape, F32), (late_shape, F32), ((LANES, channels), F32)],
        [place, act, hidden, slope, grads[0], mates[0], crossed[0], temporal_weight],
        cost=(1000, MIB),
        limit=16,
    )
    sent, late_cross = tied((hidden, crossed[1]))
    hidden_cross, hidden_mate = cross(sent), mate(sent)
    part = 12 * channels // 8
    edge = ((rows, channels), F32)
    pre_late, terms, low, high = call(
        functools.partial(backward_kernel, True),
        [(half, BF16), ((2, 4, part, channels), F32), edge, edge],
        [place, act, hidden, slope, grads[1], mates[1], late_cross, temporal_weight, *sums],
        [pltpu.VMEM(early_shape, F32), pltpu.VMEM(late_shape, F32)],
        cost=(1000, MIB),
        limit=16,
    )
    terms = terms[0] + mate(terms[1])
    got = [terms[0]] + [meet(terms[b], 0, 2 * b) for b in (1, 2, 3)]
    piece = (got[0] + got[1]) + (got[2] + got[3])
    ups, downs = [(c, c + 1) for c in range(peers - 1)], [(c + 1, c) for c in range(peers - 1)]
    halo_low, halo_high = lax.ppermute(high, "chan", ups), lax.ppermute(low, "chan", downs)
    piece = total(piece, [(4, 0), (8, 0), (12, 0)])
    piece = total(piece, [(16, 0)])
    piece, hidden_cross, hidden_mate = tied((piece, hidden_cross, hidden_mate))
    scaled, sums = call(
        input_kernel,
        [(plane, F32), ((8, channels), F32)],
        [pre_early, pre_late, halo_low, halo_high, spatial_weight, turned, columns],
        [pltpu.VMEM(padded, BF16)],
        cost=(18 * channels * channels * pixels, 6 * MIB),
        limit=16,
    )
    sums = total(sums, [(0, 1)])
    piece = total(piece, [(2, 0), (0, 1), (2, 1)])
    flat = pltpu.VMEM((rows, channels, cols), F32)
    (output,) = call(
        output_kernel,
        [(raw_in.shape, BF16)],
        [place, hidden, hidden_mate, hidden_cross, temporal_weight, raw_in],
        [flat],
        cost=(6 * channels * channels * pixels, 5 * MIB),
        limit=16,
    )
    piece = jnp.concatenate([piece, sums])
    got = [piece] + [meet(piece, 0, 2 * b) for b in (1, 2, 3)]
    own = jnp.stack(got)
    other = mate(own)
    (input_grad,) = call(
        final_kernel,
        [(raw_in.shape, BF16)],
        [*got, scaled, turned, columns, raw_grad],
        [flat],
        cost=(0, 5 * MIB),
        limit=16,
    )
    spatial_grad, temporal_grad = call(
        place_kernel,
        [((9 * channels, channels), F32), ((3 * channels, channels), F32)],
        [place, own, other],
        [pltpu.VMEM((8, part, channels), F32)],
        cost=(0, MIB),
        limit=8,
    )
    square = (-1, channels, channels)
    return (output[None], input_grad[None], spatial_grad.reshape(square), temporal_grad.reshape(square))


def solution(mesh):
    banded = P("frame", None, None, "chan")
    return jax.shard_map(
        body,
        mesh=mesh,
        in_specs=(banded, banded, P(), P(), P(), P(), P()),
        out_specs=(banded, banded, P(), P()),
        check_vma=False,
    )
```

profile of v0, /device:TPU:1, one launch (start us, length us, event | category | flops | bytes accessed | tf_op | source)
XLA Modules:
  0.0 121.4 jit_solution(3817904111356499271)
XLA Ops:
  4.2 2.5 %shard_map.103 = (bf16[128,4096]{1,0:T(8,128)(2,1)S(1)}, f32[8,40,128]{2,1,0:T(8,128)}) custom-call(s32[3]{0:T(128)S(1)} %pad_add_fusion.me_ref, bf16[128,32,128]{2,1,0:T(8,128)(2,1)S(1)} %bitcast.33), custom_call_target="tpu_custom_call" | custom-call | bytes 2097152 | tf_op jit(solution)/shard_map/pallas_call | solution.py:40
  6.7 5.9 %all-to-all-start = ((f32[8,40,128]{2,1,0:T(8,128)}), f32[8,40,128]{2,1,0:T(8,128)S(1)}, u32[]{:S(2)}, u32[]{:S(2)}) async-start(f32[8,40,128]{2,1,0:T(8,128)} %get-tuple-element.42), calls=%async_computation | async-start | bytes 327680 | tf_op jit(solution)/shard_map/all_to_all | solution.py:354
  12.7 5.2 %collective-permute-start.3 = (bf16[128,2048]{1,0:T(8,128)(2,1)S(1)}, bf16[128,2048]{1,0:T(8,128)(2,1)S(1)}, u32[]{:S(2)}, u32[]{:S(2)}) collective-permute-start(bf16[128,2048]{1,0:T(8,128)(2,1)S(1)} %get-tuple-element.50.grad_ref), channel_id=1, source_target_pairs={{8,16},{16,8},{24,32},{32,24},{40,48},{48,40},{56,64},{64,56},{72,... | collective-permute-start | bytes 1572872 | tf_op jit(solution)/shard_map/ppermute | solution.py:338
  18.4 2.1 %collective-permute-start.2 = (bf16[128,2048]{1,0:T(8,128)(2,1)S(1)}, bf16[128,2048]{1,0:T(8,128)(2,1)S(1)}, u32[]{:S(2)}, u32[]{:S(2)}) collective-permute-start(bf16[128,2048]{1,0:T(8,128)(2,1)S(1)} %get-tuple-element.50.grad_ref), channel_id=1, source_target_pairs={{0,8},{8,0},{16,24},{24,16},{32,40},{40,32},{48,56},{56,48},{64,72... | collective-permute-start | bytes 1572872 | tf_op jit(solution)/shard_map/ppermute | solution.py:339
  20.4 4.2 %collective-permute-start.1 = (bf16[128,2048]{1,0:T(8,128)(2,1)S(1)}, bf16[128,2048]{1,0:T(8,128)(2,1)S(1)}, u32[]{:S(2)}, u32[]{:S(2)}) collective-permute-start(bf16[128,2048]{1,0:T(8,128)(2,1)S(1)} %get-tuple-element.48.grad_ref), channel_id=1, source_target_pairs={{8,16},{16,8},{24,32},{32,24},{40,48},{48,40},{56,64},{64,56},{72,... | collective-permute-start | bytes 1572872 | tf_op jit(solution)/shard_map/ppermute | solution.py:338
  24.8 7.6 %shard_map.104 = (bf16[384,4352]{1,0:T(8,128)(2,1)S(1)}, bf16[128,4096]{1,0:T(8,128)(2,1)S(1)}, f32[128,4096]{1,0:T(8,128)S(1)}, f32[128,128]{1,0:T(8,128)S(1)}) custom-call(s32[3]{0:T(128)S(1)} %pad_add_fusion.me_ref, bf16[128,4096]{1,0:T(8,128)(2,1)S(1)} %get-tuple-element.39.plane_ref, f32[8,40,128]{2,1,0:T(8,128)S(1)} %all-to-all-done.received_ref, ...), custom_call_target="tpu_custom_call" | custom-call | flops 1000 | bytes 1048576 | tf_op jit(solution)/shard_map/pallas_call | solution.py:40
  32.4 2.8 %collective-permute-done.3.cross_ref = bf16[128,2048]{1,0:T(8,128)(2,1)S(1)} collective-permute-done((bf16[128,2048]{1,0:T(8,128)(2,1)S(1)}, bf16[128,2048]{1,0:T(8,128)(2,1)S(1)}, u32[]{:S(2)}, u32[]{:S(2)}) %collective-permute-start.3) | collective-permute-done | bytes 524320 | tf_op jit(solution)/shard_map/ppermute | solution.py:338
  35.2 3.4 %shard_map.105 = (bf16[128,2048]{1,0:T(8,128)(2,1)S(1)}, f32[384,128]{1,0:T(8,128)S(1)}, f32[3,128,384]{2,1,0:T(8,128)S(1)}, f32[128,128]{1,0:T(8,128)S(1)}) custom-call(s32[3]{0:T(128)S(1)} %pad_add_fusion.me_ref, bf16[384,4352]{1,0:T(8,128)(2,1)S(1)} %get-tuple-element.46.act_ref, bf16[128,4096]{1,0:T(8,128)(2,1)S(1)} %get-tuple-element.55.hidden_ref, ...), custom_call_target="tpu_custom_call" | custom-call | flops 1000 | bytes 1048576 | tf_op jit(solution)/shard_map/pallas_call | solution.py:40
  38.6 2.2 %collective-permute-done.1.cross_ref = bf16[128,2048]{1,0:T(8,128)(2,1)S(1)} collective-permute-done((bf16[128,2048]{1,0:T(8,128)(2,1)S(1)}, bf16[128,2048]{1,0:T(8,128)(2,1)S(1)}, u32[]{:S(2)}, u32[]{:S(2)}) %collective-permute-start.1) | collective-permute-done | bytes 524320 | tf_op jit(solution)/shard_map/ppermute | solution.py:338
  40.8 3.4 %shard_map.106 = (bf16[128,2048]{1,0:T(8,128)(2,1)S(1)}, f32[2,4,192,128]{3,2,1,0:T(8,128)S(1)}, f32[32,128]{1,0:T(8,128)S(1)}, f32[32,128]{1,0:T(8,128)S(1)}) custom-call(s32[3]{0:T(128)S(1)} %pad_add_fusion.me_ref, bf16[384,4352]{1,0:T(8,128)(2,1)S(1)} %get-tuple-element.46.act_ref, bf16[128,4096]{1,0:T(8,128)(2,1)S(1)} %get-tuple-element.55.hidden_ref, ...), custom_call_target="tpu_custom_call" | custom-call | flops 1000 | bytes 1048576 | tf_op jit(solution)/shard_map/pallas_call | solution.py:40
  44.4 5.9 %collective-permute-start.12 = (bf16[128,4096]{1,0:T(8,128)(2,1)S(1)}, bf16[128,4096]{1,0:T(8,128)(2,1)S(1)}, u32[]{:S(2)}, u32[]{:S(2)}) collective-permute-start(bf16[128,4096]{1,0:T(8,128)(2,1)S(1)} %get-tuple-element.55.hidden_ref), channel_id=1, source_target_pairs={{8,16},{16,8},{24,32},{32,24},{40,48},{48,40},{56,64},{64,56},{72,... | collective-permute-start | bytes 3145736 | tf_op jit(solution)/shard_map/ppermute | solution.py:338
  50.5 1.8 %collective-permute-start.5 = (f32[192,128]{1,0:T(8,128)S(1)}, f32[192,128]{1,0:T(8,128)S(1)}, u32[]{:S(2)}, u32[]{:S(2)}) collective-permute-start(f32[192,128]{1,0:T(8,128)S(1)} %get-tuple-element.70), channel_id=1, source_target_pairs={{0,2},{1,3},{2,0},{3,1},{4,6},{5,7},{6,4},{7,5},{8,10},{9,11},{10,... | collective-permute-start | bytes 294920 | tf_op jit(solution)/shard_map/ppermute | solution.py:342
  52.3 2.4 %collective-permute-start.6 = (f32[192,128]{1,0:T(8,128)S(1)}, f32[192,128]{1,0:T(8,128)S(1)}, u32[]{:S(2)}, u32[]{:S(2)}) collective-permute-start(f32[192,128]{1,0:T(8,128)S(1)} %get-tuple-element.69), channel_id=1, source_target_pairs={{0,4},{1,5},{2,6},{3,7},{4,0},{5,1},{6,2},{7,3},{8,12},{9,13},{10,... | collective-permute-start | bytes 294920 | tf_op jit(solution)/shard_map/ppermute | solution.py:342
  55.0 4.2 %collective-permute-done.6 = f32[192,128]{1,0:T(8,128)S(1)} collective-permute-done((f32[192,128]{1,0:T(8,128)S(1)}, f32[192,128]{1,0:T(8,128)S(1)}, u32[]{:S(2)}, u32[]{:S(2)}) %collective-permute-start.6) | collective-permute-done | bytes 98336 | tf_op jit(solution)/shard_map/ppermute | solution.py:342
  59.2 2.6 %collective-permute-done.7 = f32[192,128]{1,0:T(8,128)S(1)} collective-permute-done((f32[192,128]{1,0:T(8,128)S(1)}, f32[192,128]{1,0:T(8,128)S(1)}, u32[]{:S(2)}, u32[]{:S(2)}) %collective-permute-start.7) | collective-permute-done | bytes 98336 | tf_op jit(solution)/shard_map/ppermute | solution.py:342
  61.8 4.4 %collective-permute-start.10 = (f32[192,128]{1,0:T(8,128)S(1)}, f32[192,128]{1,0:T(8,128)S(1)}, u32[]{:S(2)}, u32[]{:S(2)}) collective-permute-start(f32[192,128]{1,0:T(8,128)S(1)} %fusion.1), channel_id=1, source_target_pairs={{0,96},{1,97},{2,98},{3,99},{4,100},{5,101},{6,102},{7,103},{8,104... | collective-permute-start | bytes 294920 | tf_op jit(solution)/shard_map/ppermute | solution.py:342
  66.7 2.2 %collective-permute-done.10 = f32[192,128]{1,0:T(8,128)S(1)} collective-permute-done((f32[192,128]{1,0:T(8,128)S(1)}, f32[192,128]{1,0:T(8,128)S(1)}, u32[]{:S(2)}, u32[]{:S(2)}) %collective-permute-start.10) | collective-permute-done | bytes 98336 | tf_op jit(solution)/shard_map/ppermute | solution.py:342
  68.9 3.8 %collective-permute-done.8 = f32[192,128]{1,0:T(8,128)S(1)} collective-permute-done((f32[192,128]{1,0:T(8,128)S(1)}, f32[192,128]{1,0:T(8,128)S(1)}, u32[]{:S(2)}, u32[]{:S(2)}) %collective-permute-start.8) | collective-permute-done | bytes 98336 | tf_op jit(solution)/shard_map/ppermute | solution.py:342
  72.7 8.9 %collective-permute-start.11 = (f32[192,128]{1,0:T(8,128)S(1)}, f32[192,128]{1,0:T(8,128)S(1)}, u32[]{:S(2)}, u32[]{:S(2)}) collective-permute-start(f32[192,128]{1,0:T(8,128)S(1)} %add_add_fusion.1), channel_id=1, source_target_pairs={{0,128},{1,129},{2,130},{3,131},{4,132},{5,133},{6,134},{7,135},{8... | collective-permute-start | bytes 294920 | tf_op jit(solution)/shard_map/ppermute | solution.py:342
  81.6 2.5 %collective-permute-start.17 = (f32[32,128]{1,0:T(8,128)S(1)}, f32[32,128]{1,0:T(8,128)S(1)}, u32[]{:S(2)}, u32[]{:S(2)}) collective-permute-start(f32[32,128]{1,0:T(8,128)S(1)} %get-tuple-element.61), channel_id=1, source_target_pairs={{0,1},{1,2},{2,3},{3,4},{4,5},{5,6},{6,7},{8,9},{9,10},{10,11},{11... | collective-permute-start | bytes 49160 | tf_op jit(solution)/shard_map/ppermute | solution.py:392
  84.1 1.3 %collective-permute-start.18 = (f32[32,128]{1,0:T(8,128)S(1)}, f32[32,128]{1,0:T(8,128)S(1)}, u32[]{:S(2)}, u32[]{:S(2)}) collective-permute-start(f32[32,128]{1,0:T(8,128)S(1)} %get-tuple-element.62), channel_id=1, source_target_pairs={{1,0},{2,1},{3,2},{4,3},{5,4},{6,5},{7,6},{9,8},{10,9},{11,10},{12... | collective-permute-start | bytes 49160 | tf_op jit(solution)/shard_map/ppermute | solution.py:392
  85.6 2.2 %collective-permute-start.15 = (f32[192,128]{1,0:T(8,128)S(1)}, f32[192,128]{1,0:T(8,128)S(1)}, u32[]{:S(2)}, u32[]{:S(2)}) collective-permute-start(f32[192,128]{1,0:T(8,128)S(1)} %add.51), channel_id=1, source_target_pairs={{0,1},{1,0},{2,3},{3,2},{4,5},{5,4},{6,7},{7,6},{8,9},{9,8},{10,11... | collective-permute-start | bytes 294920 | tf_op jit(solution)/shard_map/ppermute | solution.py:342
  87.7 2.3 %collective-permute-start.16 = (f32[192,128]{1,0:T(8,128)S(1)}, f32[192,128]{1,0:T(8,128)S(1)}, u32[]{:S(2)}, u32[]{:S(2)}) collective-permute-start(f32[192,128]{1,0:T(8,128)S(1)} %add.51), channel_id=1, source_target_pairs={{0,17},{1,16},{2,19},{3,18},{4,21},{5,20},{6,23},{7,22},{8,25},{9,... | collective-permute-start | bytes 294920 | tf_op jit(solution)/shard_map/ppermute | solution.py:342
  90.0 6.3 %shard_map.108 = (f32[128,4096]{1,0:T(8,128)S(1)}, f32[8,128]{1,0:T(8,128)S(1)}) custom-call(bf16[128,2048]{1,0:T(8,128)(2,1)S(1)} %get-tuple-element.59.early_ref, bf16[128,2048]{1,0:T(8,128)(2,1)S(1)} %get-tuple-element.60.late_ref, f32[32,128]{1,0:T(8,128)S(1)} %collective-permute-done.17.low_ref, f32[32,128]{1,0:T(8,128)S(1)} %collective-permute-done.18.high_ref, ...), custom_call_target="tpu_custom_call" | custom-call | flops 1207959552 | bytes 6291456 | tf_op jit(solution)/shard_map/pallas_call | solution.py:40
  97.3 1.6 %collective-permute-done.19 = f32[8,128]{1,0:T(8,128)S(1)} collective-permute-done((f32[8,128]{1,0:T(8,128)S(1)}, f32[8,128]{1,0:T(8,128)S(1)}, u32[]{:S(2)}, u32[]{:S(2)}) %collective-permute-start.19) | collective-permute-done | bytes 4128 | tf_op jit(solution)/shard_map/ppermute | solution.py:342
  99.6 2.0 %collective-permute-start.21 = (f32[200,128]{1,0:T(8,128)S(1)}, f32[200,128]{1,0:T(8,128)S(1)}, u32[]{:S(2)}, u32[]{:S(2)}) collective-permute-start(f32[200,128]{1,0:T(8,128)S(1)} %get-tuple-element.72.own_ref), channel_id=1, source_target_pairs={{0,4},{1,5},{2,6},{3,7},{4,0},{5,1},{6,2},{7,3},{8,12},{9,13},{10,... | collective-permute-start | bytes 307208 | tf_op jit(solution)/shard_map/ppermute | solution.py:342
  102.9 1.9 %collective-permute-done.21.two_ref = f32[200,128]{1,0:T(8,128)S(1)} collective-permute-done((f32[200,128]{1,0:T(8,128)S(1)}, f32[200,128]{1,0:T(8,128)S(1)}, u32[]{:S(2)}, u32[]{:S(2)}) %collective-permute-start.21) | collective-permute-done | bytes 102432 | tf_op jit(solution)/shard_map/ppermute | solution.py:342
  104.8 1.6 %collective-permute-done.22.three_ref = f32[200,128]{1,0:T(8,128)S(1)} collective-permute-done((f32[200,128]{1,0:T(8,128)S(1)}, f32[200,128]{1,0:T(8,128)S(1)}, u32[]{:S(2)}, u32[]{:S(2)}) %collective-permute-start.22) | collective-permute-done | bytes 102432 | tf_op jit(solution)/shard_map/ppermute | solution.py:342
  106.4 6.8 %collective-permute-start.23 = (f32[4,200,128]{2,1,0:T(8,128)S(1)}, f32[4,200,128]{2,1,0:T(8,128)S(1)}, u32[]{:S(2)}, u32[]{:S(2)}) collective-permute-start(f32[4,200,128]{2,1,0:T(8,128)S(1)} %pad_maximum_fusion.own_ref), channel_id=1, source_target_pairs={{0,8},{8,0},{16,24},{24,16},{32,40},{40,32},{48,56},{56,48},{64,72... | collective-permute-start | bytes 1228808 | tf_op jit(solution)/shard_map/ppermute | solution.py:339
  113.2 4.0 %shard_map.107 = bf16[128,32,128]{2,1,0:T(8,128)(2,1)} custom-call(s32[3]{0:T(128)S(1)} %pad_add_fusion.me_ref, bf16[128,4096]{1,0:T(8,128)(2,1)S(1)} %get-tuple-element.55.hidden_ref, bf16[128,4096]{1,0:T(8,128)(2,1)S(1)} %collective-permute-done.13.mate_ref, bf16[128,4096]{1,0:T(8,128)(2,1)S(1)} %collective-permute-done.12.cross_ref, ...), custom_call_target="tpu_custom_call" | custom-call | flops 402653184 | bytes 5242880 | tf_op jit(solution)/shard_map/pallas_call | solution.py:40
  117.1 2.7 %shard_map.109 = bf16[128,32,128]{2,1,0:T(8,128)(2,1)} custom-call(f32[200,128]{1,0:T(8,128)S(1)} %get-tuple-element.72.own_ref, f32[200,128]{1,0:T(8,128)S(1)} %collective-permute-done.20.one_ref, f32[200,128]{1,0:T(8,128)S(1)} %collective-permute-done.21.two_ref, f32[200,128]{1,0:T(8,128)S(1)} %collective-permute-done.22.three_ref, ...), custom_call_target="tpu_custom_call" | custom-call | bytes 5242880 | tf_op jit(solution)/shard_map/pallas_call | solution.py:40
  119.9 1.5 %shard_map.110 = (f32[1152,128]{1,0:T(8,128)}, f32[384,128]{1,0:T(8,128)}) custom-call(s32[3]{0:T(128)S(1)} %pad_add_fusion.me_ref, f32[4,200,128]{2,1,0:T(8,128)S(1)} %pad_maximum_fusion.own_ref, f32[4,200,128]{2,1,0:T(8,128)S(1)} %collective-permute-done.23.mate_ref), custom_call_target="tpu_custom_call" | custom-call | bytes 1048576 | tf_op jit(solution)/shard_map/pallas_call | solution.py:40
  (51 shorter events, 8.3 us)
Async XLA Ops:
  0.6 1.2 %copy-start.2 = (bf16[1,128,32,128]{3,2,1,0:T(8,128)(2,1)S(1)}, bf16[1,128,32,128]{3,2,1,0:T(8,128)(2,1)}, u32[]{:S(2)}) copy-start(bf16[1,128,32,128]{3,2,1,0:T(8,128)(2,1)} %param.8) | copy-start | bytes 3145732
  1.9 22.9 %copy-start.5 = (bf16[9,128,128]{2,1,0:T(8,128)(2,1)S(1)}, bf16[9,128,128]{2,1,0:T(8,128)(2,1)}, u32[]{:S(2)}) copy-start(bf16[9,128,128]{2,1,0:T(8,128)(2,1)} %weight_ref.9) | copy-start | bytes 884740
  1.9 33.3 %copy-start.4 = (bf16[3,128,128]{2,1,0:T(8,128)(2,1)S(1)}, bf16[3,128,128]{2,1,0:T(8,128)(2,1)}, u32[]{:S(2)}) copy-start(bf16[3,128,128]{2,1,0:T(8,128)(2,1)} %weight_ref.8) | copy-start | bytes 294916
  3.0 1.2 %copy-start = (bf16[1,128,32,128]{3,2,1,0:T(8,128)(2,1)S(1)}, bf16[1,128,32,128]{3,2,1,0:T(8,128)(2,1)}, u32[]{:S(2)}) copy-start(bf16[1,128,32,128]{3,2,1,0:T(8,128)(2,1)} %param.7) | copy-start | bytes 3145732
  6.7 11.7 %all-to-all-start = ((f32[8,40,128]{2,1,0:T(8,128)}), f32[8,40,128]{2,1,0:T(8,128)S(1)}, u32[]{:S(2)}, u32[]{:S(2)}) async-start(f32[8,40,128]{2,1,0:T(8,128)} %get-tuple-element.42), calls=%async_computation | async-start | bytes 327680 | tf_op jit(solution)/shard_map/all_to_all | solution.py:354
  12.7 22.5 %collective-permute-start.3 = (bf16[128,2048]{1,0:T(8,128)(2,1)S(1)}, bf16[128,2048]{1,0:T(8,128)(2,1)S(1)}, u32[]{:S(2)}, u32[]{:S(2)}) collective-permute-start(bf16[128,2048]{1,0:T(8,128)(2,1)S(1)} %get-tuple-element.50.grad_ref), channel_id=1, source_target_pairs={{8,16},{16,8},{24,32},{32,24},{40,48},{48,40},{56,64},{64,56},{72,... | collective-permute-start | bytes 1572872 | tf_op jit(solution)/shard_map/ppermute | solution.py:338
  18.4 16.8 %collective-permute-start.2 = (bf16[128,2048]{1,0:T(8,128)(2,1)S(1)}, bf16[128,2048]{1,0:T(8,128)(2,1)S(1)}, u32[]{:S(2)}, u32[]{:S(2)}) collective-permute-start(bf16[128,2048]{1,0:T(8,128)(2,1)S(1)} %get-tuple-element.50.grad_ref), channel_id=1, source_target_pairs={{0,8},{8,0},{16,24},{24,16},{32,40},{40,32},{48,56},{56,48},{64,72... | collective-permute-start | bytes 1572872 | tf_op jit(solution)/shard_map/ppermute | solution.py:339
  20.4 20.4 %collective-permute-start.1 = (bf16[128,2048]{1,0:T(8,128)(2,1)S(1)}, bf16[128,2048]{1,0:T(8,128)(2,1)S(1)}, u32[]{:S(2)}, u32[]{:S(2)}) collective-permute-start(bf16[128,2048]{1,0:T(8,128)(2,1)S(1)} %get-tuple-element.48.grad_ref), channel_id=1, source_target_pairs={{8,16},{16,8},{24,32},{32,24},{40,48},{48,40},{56,64},{64,56},{72,... | collective-permute-start | bytes 1572872 | tf_op jit(solution)/shard_map/ppermute | solution.py:338
  24.7 16.1 %collective-permute-start = (bf16[128,2048]{1,0:T(8,128)(2,1)S(1)}, bf16[128,2048]{1,0:T(8,128)(2,1)S(1)}, u32[]{:S(2)}, u32[]{:S(2)}) collective-permute-start(bf16[128,2048]{1,0:T(8,128)(2,1)S(1)} %get-tuple-element.48.grad_ref), channel_id=1, source_target_pairs={{0,8},{8,0},{16,24},{24,16},{32,40},{40,32},{48,56},{56,48},{64,72... | collective-permute-start | bytes 1572872 | tf_op jit(solution)/shard_map/ppermute | solution.py:339
  44.3 6.1 %collective-permute-start.4 = (f32[4,192,128]{2,1,0:T(8,128)S(1)}, f32[4,192,128]{2,1,0:T(8,128)S(1)}, u32[]{:S(2)}, u32[]{:S(2)}) collective-permute-start(f32[4,192,128]{2,1,0:T(8,128)S(1)} %slice_bitcast_fusion), channel_id=1, source_target_pairs={{0,8},{8,0},{16,24},{24,16},{32,40},{40,32},{48,56},{56,48},{64,72... | collective-permute-start | bytes 1179656 | tf_op jit(solution)/shard_map/ppermute | solution.py:339
  44.4 41.0 %collective-permute-start.12 = (bf16[128,4096]{1,0:T(8,128)(2,1)S(1)}, bf16[128,4096]{1,0:T(8,128)(2,1)S(1)}, u32[]{:S(2)}, u32[]{:S(2)}) collective-permute-start(bf16[128,4096]{1,0:T(8,128)(2,1)S(1)} %get-tuple-element.55.hidden_ref), channel_id=1, source_target_pairs={{8,16},{16,8},{24,32},{32,24},{40,48},{48,40},{56,64},{64,56},{72,... | collective-permute-start | bytes 3145736 | tf_op jit(solution)/shard_map/ppermute | solution.py:338
  50.3 35.1 %collective-permute-start.13 = (bf16[128,4096]{1,0:T(8,128)(2,1)S(1)}, bf16[128,4096]{1,0:T(8,128)(2,1)S(1)}, u32[]{:S(2)}, u32[]{:S(2)}) collective-permute-start(bf16[128,4096]{1,0:T(8,128)(2,1)S(1)} %get-tuple-element.55.hidden_ref), channel_id=1, source_target_pairs={{0,8},{8,0},{16,24},{24,16},{32,40},{40,32},{48,56},{56,48},{64,72... | collective-permute-start | bytes 3145736 | tf_op jit(solution)/shard_map/ppermute | solution.py:339
  50.5 4.6 %collective-permute-start.5 = (f32[192,128]{1,0:T(8,128)S(1)}, f32[192,128]{1,0:T(8,128)S(1)}, u32[]{:S(2)}, u32[]{:S(2)}) collective-permute-start(f32[192,128]{1,0:T(8,128)S(1)} %get-tuple-element.70), channel_id=1, source_target_pairs={{0,2},{1,3},{2,0},{3,1},{4,6},{5,7},{6,4},{7,5},{8,10},{9,11},{10,... | collective-permute-start | bytes 294920 | tf_op jit(solution)/shard_map/ppermute | solution.py:342
  52.3 6.9 %collective-permute-start.6 = (f32[192,128]{1,0:T(8,128)S(1)}, f32[192,128]{1,0:T(8,128)S(1)}, u32[]{:S(2)}, u32[]{:S(2)}) collective-permute-start(f32[192,128]{1,0:T(8,128)S(1)} %get-tuple-element.69), channel_id=1, source_target_pairs={{0,4},{1,5},{2,6},{3,7},{4,0},{5,1},{6,2},{7,3},{8,12},{9,13},{10,... | collective-permute-start | bytes 294920 | tf_op jit(solution)/shard_map/ppermute | solution.py:342
  54.7 7.1 %collective-permute-start.7 = (f32[192,128]{1,0:T(8,128)S(1)}, f32[192,128]{1,0:T(8,128)S(1)}, u32[]{:S(2)}, u32[]{:S(2)}) collective-permute-start(f32[192,128]{1,0:T(8,128)S(1)} %get-tuple-element.68), channel_id=1, source_target_pairs={{0,6},{1,7},{2,4},{3,5},{4,2},{5,3},{6,0},{7,1},{8,14},{9,15},{10,... | collective-permute-start | bytes 294920 | tf_op jit(solution)/shard_map/ppermute | solution.py:342
  61.8 7.0 %collective-permute-start.10 = (f32[192,128]{1,0:T(8,128)S(1)}, f32[192,128]{1,0:T(8,128)S(1)}, u32[]{:S(2)}, u32[]{:S(2)}) collective-permute-start(f32[192,128]{1,0:T(8,128)S(1)} %fusion.1), channel_id=1, source_target_pairs={{0,96},{1,97},{2,98},{3,99},{4,100},{5,101},{6,102},{7,103},{8,104... | collective-permute-start | bytes 294920 | tf_op jit(solution)/shard_map/ppermute | solution.py:342
  66.3 6.4 %collective-permute-start.8 = (f32[192,128]{1,0:T(8,128)S(1)}, f32[192,128]{1,0:T(8,128)S(1)}, u32[]{:S(2)}, u32[]{:S(2)}) collective-permute-start(f32[192,128]{1,0:T(8,128)S(1)} %fusion.1), channel_id=1, source_target_pairs={{0,32},{1,33},{2,34},{3,35},{4,36},{5,37},{6,38},{7,39},{8,40},{9,... | collective-permute-start | bytes 294920 | tf_op jit(solution)/shard_map/ppermute | solution.py:342
  66.3 6.4 %collective-permute-start.9 = (f32[192,128]{1,0:T(8,128)S(1)}, f32[192,128]{1,0:T(8,128)S(1)}, u32[]{:S(2)}, u32[]{:S(2)}) collective-permute-start(f32[192,128]{1,0:T(8,128)S(1)} %fusion.1), channel_id=1, source_target_pairs={{0,64},{1,65},{2,66},{3,67},{4,68},{5,69},{6,70},{7,71},{8,72},{9,... | collective-permute-start | bytes 294920 | tf_op jit(solution)/shard_map/ppermute | solution.py:342
  72.7 12.7 %collective-permute-start.11 = (f32[192,128]{1,0:T(8,128)S(1)}, f32[192,128]{1,0:T(8,128)S(1)}, u32[]{:S(2)}, u32[]{:S(2)}) collective-permute-start(f32[192,128]{1,0:T(8,128)S(1)} %add_add_fusion.1), channel_id=1, source_target_pairs={{0,128},{1,129},{2,130},{3,131},{4,132},{5,133},{6,134},{7,135},{8... | collective-permute-start | bytes 294920 | tf_op jit(solution)/shard_map/ppermute | solution.py:342
  81.6 8.4 %collective-permute-start.17 = (f32[32,128]{1,0:T(8,128)S(1)}, f32[32,128]{1,0:T(8,128)S(1)}, u32[]{:S(2)}, u32[]{:S(2)}) collective-permute-start(f32[32,128]{1,0:T(8,128)S(1)} %get-tuple-element.61), channel_id=1, source_target_pairs={{0,1},{1,2},{2,3},{3,4},{4,5},{5,6},{6,7},{8,9},{9,10},{10,11},{11... | collective-permute-start | bytes 49160 | tf_op jit(solution)/shard_map/ppermute | solution.py:392
  84.1 5.9 %collective-permute-start.18 = (f32[32,128]{1,0:T(8,128)S(1)}, f32[32,128]{1,0:T(8,128)S(1)}, u32[]{:S(2)}, u32[]{:S(2)}) collective-permute-start(f32[32,128]{1,0:T(8,128)S(1)} %get-tuple-element.62), channel_id=1, source_target_pairs={{1,0},{2,1},{3,2},{4,3},{5,4},{6,5},{7,6},{9,8},{10,9},{11,10},{12... | collective-permute-start | bytes 49160 | tf_op jit(solution)/shard_map/ppermute | solution.py:392
  85.5 13.4 %collective-permute-start.14 = (f32[192,128]{1,0:T(8,128)S(1)}, f32[192,128]{1,0:T(8,128)S(1)}, u32[]{:S(2)}, u32[]{:S(2)}) collective-permute-start(f32[192,128]{1,0:T(8,128)S(1)} %add.51), channel_id=1, source_target_pairs={{0,16},{1,17},{2,18},{3,19},{4,20},{5,21},{6,22},{7,23},{8,24},{9,... | collective-permute-start | bytes 294920 | tf_op jit(solution)/shard_map/ppermute | solution.py:342
  85.6 13.3 %collective-permute-start.15 = (f32[192,128]{1,0:T(8,128)S(1)}, f32[192,128]{1,0:T(8,128)S(1)}, u32[]{:S(2)}, u32[]{:S(2)}) collective-permute-start(f32[192,128]{1,0:T(8,128)S(1)} %add.51), channel_id=1, source_target_pairs={{0,1},{1,0},{2,3},{3,2},{4,5},{5,4},{6,7},{7,6},{8,9},{9,8},{10,11... | collective-permute-start | bytes 294920 | tf_op jit(solution)/shard_map/ppermute | solution.py:342
  87.7 11.2 %collective-permute-start.16 = (f32[192,128]{1,0:T(8,128)S(1)}, f32[192,128]{1,0:T(8,128)S(1)}, u32[]{:S(2)}, u32[]{:S(2)}) collective-permute-start(f32[192,128]{1,0:T(8,128)S(1)} %add.51), channel_id=1, source_target_pairs={{0,17},{1,16},{2,19},{3,18},{4,21},{5,20},{6,23},{7,22},{8,25},{9,... | collective-permute-start | bytes 294920 | tf_op jit(solution)/shard_map/ppermute | solution.py:342
  90.0 23.1 %copy-start.1 = (bf16[1,128,32,128]{3,2,1,0:T(8,128)(2,1)S(1)}, bf16[1,128,32,128]{3,2,1,0:T(8,128)(2,1)}, u32[]{:S(2)}) copy-start(bf16[1,128,32,128]{3,2,1,0:T(8,128)(2,1)} %param.7) | copy-start | bytes 3145732
  96.4 2.5 %collective-permute-start.19 = (f32[8,128]{1,0:T(8,128)S(1)}, f32[8,128]{1,0:T(8,128)S(1)}, u32[]{:S(2)}, u32[]{:S(2)}) collective-permute-start(f32[8,128]{1,0:T(8,128)S(1)} %get-tuple-element.64), channel_id=1, source_target_pairs={{0,1},{1,0},{2,3},{3,2},{4,5},{5,4},{6,7},{7,6},{8,9},{9,8},{10,11... | collective-permute-start | bytes 12296 | tf_op jit(solution)/shard_map/ppermute | solution.py:342
  98.9 3.9 %collective-permute-start.20 = (f32[200,128]{1,0:T(8,128)S(1)}, f32[200,128]{1,0:T(8,128)S(1)}, u32[]{:S(2)}, u32[]{:S(2)}) collective-permute-start(f32[200,128]{1,0:T(8,128)S(1)} %get-tuple-element.72.own_ref), channel_id=1, source_target_pairs={{0,2},{1,3},{2,0},{3,1},{4,6},{5,7},{6,4},{7,5},{8,10},{9,11},{10,... | collective-permute-start | bytes 307208 | tf_op jit(solution)/shard_map/ppermute | solution.py:342
  99.6 5.1 %collective-permute-start.21 = (f32[200,128]{1,0:T(8,128)S(1)}, f32[200,128]{1,0:T(8,128)S(1)}, u32[]{:S(2)}, u32[]{:S(2)}) collective-permute-start(f32[200,128]{1,0:T(8,128)S(1)} %get-tuple-element.72.own_ref), channel_id=1, source_target_pairs={{0,4},{1,5},{2,6},{3,7},{4,0},{5,1},{6,2},{7,3},{8,12},{9,13},{10,... | collective-permute-start | bytes 307208 | tf_op jit(solution)/shard_map/ppermute | solution.py:342
  101.6 4.7 %collective-permute-start.22 = (f32[200,128]{1,0:T(8,128)S(1)}, f32[200,128]{1,0:T(8,128)S(1)}, u32[]{:S(2)}, u32[]{:S(2)}) collective-permute-start(f32[200,128]{1,0:T(8,128)S(1)} %get-tuple-element.72.own_ref), channel_id=1, source_target_pairs={{0,6},{1,7},{2,4},{3,5},{4,2},{5,3},{6,0},{7,1},{8,14},{9,15},{10,... | collective-permute-start | bytes 307208 | tf_op jit(solution)/shard_map/ppermute | solution.py:342
  106.4 10.7 %copy-start.3 = (bf16[1,128,32,128]{3,2,1,0:T(8,128)(2,1)S(1)}, bf16[1,128,32,128]{3,2,1,0:T(8,128)(2,1)}, u32[]{:S(2)}) copy-start(bf16[1,128,32,128]{3,2,1,0:T(8,128)(2,1)} %param.8) | copy-start | bytes 3145732
  106.4 13.5 %collective-permute-start.23 = (f32[4,200,128]{2,1,0:T(8,128)S(1)}, f32[4,200,128]{2,1,0:T(8,128)S(1)}, u32[]{:S(2)}, u32[]{:S(2)}) collective-permute-start(f32[4,200,128]{2,1,0:T(8,128)S(1)} %pad_maximum_fusion.own_ref), channel_id=1, source_target_pairs={{0,8},{8,0},{16,24},{24,16},{32,40},{40,32},{48,56},{56,48},{64,72... | collective-permute-start | bytes 1228808 | tf_op jit(solution)/shard_map/ppermute | solution.py:339
where the time goes:
time: 122 us; the launch traced here: 121 us
  starting transfers between devices  61.6 us (50%)
  Pallas kernels  31.8 us (26%)
  waiting for transfers between devices  23.6 us (19%)
  local copies, waits for them, and re-layouts  2.51 us (2%)
    pallas_call x9, Pallas kernels, call(): pl.pallas_call(kernel, out_shape=[jax.ShapeDtypeStruct(s, d) for s, d in...  31.8 us
    ppermute x14, starting transfers between devices, meet(): lax.ppermute(v, ('frame', 'chan'), both(frame_bits, chan_bits, frames, pe...  27.5 us
    ppermute x14, waiting for transfers between devices, meet(): lax.ppermute(v, ('frame', 'chan'), both(frame_bits, chan_bits, frames, pe...  18.1 us
    ppermute x3, starting transfers between devices, body(): cross = lambda v: lax.ppermute(v, 'frame', neighbour(frames))  15.3 us
    ppermute x5, starting transfers between devices, body(): mate = lambda v: lax.ppermute(v, 'frame', partner(1, frames))  9.11 us
    all_to_all x1, starting transfers between devices, body(): received = lax.all_to_all(payload, 'chan', 0, 0, tiled=True)  5.94 us
    ppermute x3, waiting for transfers between devices, body(): cross = lambda v: lax.ppermute(v, 'frame', neighbour(frames))  5 us
    ppermute x1, starting transfers between devices, body(): lax.ppermute(high, 'chan', ups)  2.47 us
  transfers between devices with their start and end apart: 25, of which 11 were waited for; matrix products, arithmetic and copies ran while one was open for 0% of the time, Pallas kernels for 20%

commit v1 on v0

v1 whole, which is shorter than its diff:
```python
import functools

import jax
import jax.numpy as jnp
from jax import lax
from jax.experimental import pallas as pl
from jax.experimental.pallas import tpu as pltpu
from jax.sharding import PartitionSpec as P

GROUPS = 32
LANES = 128
TILE = 1024
MIB = 1024 * 1024
CONTRACT_LAST = (((1,), (1,)), ((), ()))
F32, BF16 = jnp.float32, jnp.bfloat16


def partner(bits, frames):
    return [(f, f ^ bits) for f in range(frames)]


def both(frame_bits, chan_bits, frames, peers):
    return [(f * peers + c, (f ^ frame_bits) * peers + (c ^ chan_bits)) for f in range(frames) for c in range(peers)]


def crossing(frames, inside):
    return [(f, t) for f, t in neighbour(frames) if (f // 4 == t // 4) == inside]


def neighbour(frames):
    pairs = []
    for f in range(frames):
        target = f + 1 if f % 2 else f - 1
        if 0 <= target < frames:
            pairs.append((f, target))
    return pairs


def call(kernel, outs, ins, scratch=(), cost=(0, 0), limit=24):
    smem = pl.BlockSpec(memory_space=pltpu.SMEM)
    vmem = pl.BlockSpec(memory_space=pltpu.VMEM)
    is_place = lambda v: v.dtype == jnp.int32
    flops, moved = cost
    return pl.pallas_call(
        kernel,
        out_shape=[jax.ShapeDtypeStruct(s, d) for s, d in outs],
        in_specs=[smem if is_place(v) else vmem for v in ins],
        out_specs=[vmem] * len(outs),
        scratch_shapes=list(scratch),
        cost_estimate=pl.CostEstimate(flops=flops, bytes_accessed=moved, transcendentals=0),
        compiler_params=pltpu.CompilerParams(vmem_limit_bytes=limit * MIB),
    )(*ins)


def lane_index(shape=(LANES, LANES)):
    return lax.broadcasted_iota(jnp.int32, shape, len(shape) - 1)


def row_at(r):
    return pl.ds(pl.multiple_of(r * LANES, LANES), LANES)


def span(row, rows):
    return slice(row * LANES, (row + rows) * LANES)


def side(parts):
    return jnp.concatenate(parts, axis=1)


def tile_at(n, extra=0):
    return pl.ds(pl.multiple_of(n * TILE, LANES) + extra, TILE)


def group_sum(v):
    lane = lax.broadcasted_iota(jnp.int32, v.shape, 1)
    for step in (1, 2):
        up, down = pltpu.roll(v, LANES - step, 1), pltpu.roll(v, step, 1)
        v = v + jnp.where((lane // step) % 2 == 0, up, down)
    return v


def sigmoid(v):
    return 1.0 / (1.0 + jnp.exp(-v))


def selector(n, rows):
    pixel = lax.broadcasted_iota(jnp.int32, (LANES, TILE), 1) + n * TILE
    at = lax.broadcasted_iota(jnp.int32, (LANES, TILE), 0)
    low = (at < rows) & (pixel == at * LANES)
    high = (at >= 64) & (pixel == (at - 64) * LANES + (LANES - 1))
    return jnp.where(low | high | (at == 32), 1.0, 0.0).astype(BF16)


def turn(raw):
    return jnp.swapaxes(raw, 0, 1)


def store_shifts(ref, row, halo, r, lane, order, offset=1):
    row = row.astype(BF16)
    left = jnp.where(lane == 0, pltpu.roll(halo, LANES - 32 - r, 1), pltpu.roll(row, 1, 1))
    right = jnp.where(lane == LANES - 1, pltpu.roll(halo, 63 - r, 1), pltpu.roll(row, LANES - 1, 1))
    shifts = (left, row, right)
    for slot, which in enumerate(order):
        ref[slot * LANES : (slot + 1) * LANES, row_at(r + offset)] = shifts[which].astype(BF16)


def turn_kernel(raw_ref, low_ref, high_ref):
    channels, rows, _ = raw_ref.shape
    for c in range(0, channels, 16):
        block = turn(raw_ref[c : c + 16])
        for r in range(rows):
            ref, at = (low_ref, r) if r < rows // 2 else (high_ref, r - rows // 2)
            ref[c : c + 16, at * LANES : (at + 1) * LANES] = block[r]


def sums_kernel(me_ref, raw_ref, out_ref, payload_ref):
    channels, rows, _ = raw_ref.shape
    me = me_ref[0]
    for c in range(0, channels, 16):
        block = turn(raw_ref[c : c + 16])
        for r in range(rows):
            out_ref[c : c + 16, r * LANES : (r + 1) * LANES] = block[r]
    packed = jnp.zeros((LANES, channels), F32)
    for n in range(rows * LANES // TILE):
        packed += lax.dot_general(selector(n, rows), out_ref[:, n * TILE : (n + 1) * TILE], CONTRACT_LAST, preferred_element_type=F32)
    mean = packed[32:33] / (rows * LANES)
    mean_all = jnp.broadcast_to(mean, (LANES, channels)).T

    def square(r, acc):
        off = out_ref[:, row_at(r)].astype(F32) - mean_all
        return acc + off * off

    squares = lax.fori_loop(0, rows, square, jnp.zeros((channels, LANES), F32), unroll=4)
    squares = jnp.sum(squares.T, axis=0, keepdims=True)
    head = jnp.concatenate([mean, squares, jnp.zeros((6, channels), F32)], axis=0)
    for peer in range(payload_ref.shape[0]):
        payload_ref[peer, 0:8, :] = head
        payload_ref[peer, 8 : 8 + rows, :] = jnp.where(peer < me, packed[0:rows], packed[64 : 64 + rows])


def forward_kernel(me_ref, plane_ref, received_ref, table_ref, weight_ref, act_ref, hidden_ref, slope_ref, columns_ref):
    channels, pixels = plane_ref.shape
    rows = pixels // LANES
    peers = received_ref.shape[0]
    me = me_ref[0]
    lane = lane_index()
    count = (channels // GROUPS) * pixels * peers
    means, squares = received_ref[:, 0, :], received_ref[:, 1, :]
    center = group_sum(jnp.sum(means, axis=0, keepdims=True)) * (GROUPS / (channels * peers))
    off = means - center
    spread = group_sum(jnp.sum(squares + pixels * (off * off), axis=0, keepdims=True)) / count
    inverse = lax.rsqrt(spread + 1e-05)
    low = received_ref[jnp.maximum(me - 1, 0), 8 : 8 + rows, :]
    high = received_ref[jnp.minimum(me + 1, peers - 1), 8 : 8 + rows, :]
    head = jnp.concatenate([center, inverse, table_ref[...], jnp.zeros((3, LANES), F32)], axis=0)
    gap = jnp.zeros((24, LANES), F32)
    columns = jnp.concatenate([head, gap, low, high, jnp.zeros((32, LANES), F32)], axis=0).T
    columns_ref[...] = columns
    wide = lambda at: jnp.broadcast_to(columns[:, at : at + 1], (channels, LANES))
    center_w, inverse_w, gain_w, shift_w, bias_w = [wide(at) for at in range(5)]

    def activate(v):
        v = (v - center_w) * inverse_w * gain_w + shift_w
        return v * sigmoid(v)

    inside = ((lane < 64) & (me > 0)) | ((lane >= 64) & (me < peers - 1))
    halo = jnp.where(inside, activate(columns), 0.0).astype(BF16)
    nothing = jnp.zeros((3 * channels, LANES), BF16)
    act_ref[:, 0:LANES] = nothing
    act_ref[:, (rows + 1) * LANES : (rows + 2) * LANES] = nothing

    def shape_row(r, carry):
        row = activate(plane_ref[:, row_at(r)].astype(F32))
        store_shifts(act_ref, row, halo, r, lane, (0, 1, 2))
        return carry

    lax.fori_loop(0, rows, shape_row, 0, unroll=8)
    weights = side([weight_ref[t] for t in range(9)])
    each = TILE // LANES
    bias = jnp.broadcast_to(bias_w[:, 0:1], (channels, TILE))
    for n in range(rows // each):
        window = jnp.concatenate([act_ref[:, span(n * each + dy, each)] for dy in range(3)], axis=0)
        value = jnp.dot(weights, window, preferred_element_type=F32) + bias
        logistic = sigmoid(value)
        hidden_ref[:, span(n * each, each)] = (value * logistic).astype(BF16)
        slope_ref[:, span(n * each, each)] = logistic * (1.0 + value * (1.0 - logistic))


def backward_kernel(last, me_ref, act_ref, hidden_ref, slope_ref, grad_ref, mate_ref, cross_ref, *rest):
    if last:
        weight_ref, early_in, late_in, packed_in, *rest = rest
        pre_ref, keep_ref, send_ref, edges_ref, early, late, shifted = rest
    else:
        weight_ref, pre_ref, early, late, packed_ref, shifted = rest
    channels, pixels = grad_ref.shape
    rows = 2 * pixels // LANES
    core, spot = me_ref[1], me_ref[2]
    turned = [weight_ref[k].astype(F32).T for k in range(3)]
    even = core == 0
    ahead = jnp.where(even, turned[0], turned[2])
    behind = jnp.where(even, turned[2], turned[0])
    weights = jnp.concatenate([turned[1], ahead, behind], axis=1).astype(BF16)
    own_rows = rows // 2
    start = own_rows if last else 0
    blank = jnp.zeros((channels, 2 * LANES), BF16)
    shifted[:, span(0, 2)] = blank
    shifted[:, span(own_rows + 2, 2)] = blank
    each = TILE // LANES
    fresh = jnp.zeros((3 * channels, channels), F32)
    packed = jnp.zeros((LANES, channels), F32)
    for n in range(own_rows // each):
        at, whole = span(n * each, each), span(n * each + start, each)
        grads = jnp.concatenate([ref[:, at] for ref in (grad_ref, mate_ref, cross_ref)], axis=0)
        back = jnp.dot(weights, grads, preferred_element_type=F32)
        pre = (back * slope_ref[:, whole]).astype(BF16)
        pre_ref[:, at] = pre
        shifted[:, span(n * each + 2, each)] = pre
        fresh += lax.dot_general(grads, hidden_ref[:, whole], CONTRACT_LAST, preferred_element_type=F32)
        packed += lax.dot_general(selector(n + start // each, rows), pre, CONTRACT_LAST, preferred_element_type=F32)
    lhs = jnp.concatenate([shifted[:, span(2 - dy, own_rows + 2)] for dy in range(3)], axis=0)
    rhs = act_ref[:, span(start, own_rows + 2)]
    latest = lax.dot_general(lhs, rhs, CONTRACT_LAST, preferred_element_type=F32)
    early[...] = fresh + early_in[...] if last else fresh
    late[...] = latest + late_in[...] if last else latest
    packed = packed + packed_in[...] if last else packed
    if not last:
        packed_ref[...] = packed
        return
    low, high = packed[0:rows], packed[64 : 64 + rows]
    left = me_ref[0] % 2 == 0
    edges_ref[0:rows, :] = jnp.where(left, high, low)
    edges_ref[rows:, :] = jnp.where(left, low, high)
    own, mate, cross = [early[i * channels : (i + 1) * channels, :] for i in range(3)]
    blocks = [late[t // 3 * channels : (t // 3 + 1) * channels, span(t % 3, 1)] for t in range(9)]
    blocks += [jnp.where(even, mate, cross), own, jnp.where(even, cross, mate)]
    part = keep_ref.shape[1]

    def rows_at(at):
        return blocks[at // channels][at % channels : at % channels + 64]

    for y in range(4):
        slot = y ^ spot
        for v in range(0, part, 64):
            one, two = rows_at(2 * y * part + v), rows_at((2 * y + 1) * part + v)
            keep_ref[slot, v : v + 64, :] = jnp.where(even, one, two)
            send_ref[slot, v : v + 64, :] = jnp.where(even, two, one)


def input_kernel(me_ref, early_ref, late_ref, near_ref, one_ref, three_ref, *refs):
    weight_ref, plane_ref, columns_ref, scaled_ref, sums_ref, padded, total = refs
    channels, pixels = plane_ref.shape
    rows = pixels // LANES
    lane = lane_index()
    blank = jnp.zeros((32, LANES), F32)
    me = me_ref[0]
    left = me % 2 == 0
    near = near_ref[0:rows, :]
    at = one_ref.shape[0] - rows
    far = jnp.where((me // 2 % 2 == 0) != left, one_ref[at:, :], three_ref[at:, :])
    far = jnp.where((me > 0) & (me < 7), far, 0.0)
    low, high = jnp.where(left, far, near), jnp.where(left, near, far)
    halo = jnp.concatenate([blank, low, high, blank], axis=0).T.astype(BF16)
    for first, ref in ((0, early_ref), (rows // 2, late_ref)):

        def shift_row(r, carry, ref=ref, first=first):
            store_shifts(padded, ref[:, row_at(r)], halo, r + first, lane, (2, 1, 0))
            return carry

        lax.fori_loop(0, rows // 2, shift_row, 0, unroll=8)
    flipped = lambda t: weight_ref[t].astype(F32).T.astype(BF16)
    weights = side([flipped(3 * dy + dx) for dy in (2, 1, 0) for dx in range(3)])
    each = TILE // LANES
    padded[:, span(0, 1)] = jnp.zeros((3 * channels, LANES), BF16)
    padded[:, span(rows + 1, 1)] = jnp.zeros((3 * channels, LANES), BF16)
    for n in range(rows // each):
        window = jnp.concatenate([padded[:, span(n * each + dy, each)] for dy in range(3)], axis=0)
        total[:, span(n * each + 1, each)] = jnp.dot(weights, window, preferred_element_type=F32)
    columns = columns_ref[...]
    wide = lambda at: jnp.broadcast_to(columns[:, at : at + 1], (channels, LANES))
    center, inverse, gain, shift = [wide(at) for at in range(4)]

    def step(r, carry):
        plain, crossed = carry
        normed = (plane_ref[:, row_at(r)].astype(F32) - center) * inverse
        shaped = normed * gain + shift
        logistic = sigmoid(shaped)
        scaled = total[:, row_at(r + 1)] * (logistic * (1.0 + shaped * (1.0 - logistic))) * gain
        scaled_ref[:, row_at(r)] = scaled
        return plain + scaled, crossed + scaled * normed

    zero = jnp.zeros((channels, LANES), F32)
    plain, crossed = lax.fori_loop(0, rows, step, (zero, zero), unroll=4)
    plain, crossed = [jnp.sum(v, axis=1, keepdims=True) for v in (plain, crossed)]
    sums_ref[...] = jnp.where(lane == 0, plain, jnp.where(lane == 1, crossed, 0.0)).T[0:8]


def output_kernel(me_ref, hidden_ref, mate_ref, inside_ref, outside_ref, weight_ref, raw_ref, out_ref, flat):
    channels, rows, _ = raw_ref.shape
    inside = me_ref[3] == 1
    even = me_ref[1] == 0
    pick = lambda a, b: jnp.where(even, weight_ref[a].astype(F32), weight_ref[b].astype(F32)).astype(BF16)
    weights = jnp.concatenate([weight_ref[1], pick(2, 0), pick(0, 2)], axis=1)
    each = TILE // LANES

    def step(n, carry):
        across = jnp.where(inside, inside_ref[:, tile_at(n)], outside_ref[:, tile_at(n)])
        frames = jnp.concatenate([hidden_ref[:, tile_at(n)], mate_ref[:, tile_at(n)], across], axis=0)
        mixed = jnp.dot(weights, frames, preferred_element_type=F32)
        for i in range(each):
            flat[n * each + i] = mixed[:, i * LANES : (i + 1) * LANES]
        return carry

    lax.fori_loop(0, rows // each, step, 0, unroll=2)
    for c in range(0, channels, 16):
        out_ref[c : c + 16] = (raw_ref[c : c + 16].astype(F32) + turn(flat[:, c : c + 16, :])).astype(BF16)


def final_kernel(own_ref, one_ref, two_ref, three_ref, scaled_ref, plane_ref, columns_ref, raw_ref, out_ref, flat):
    channels, rows, _ = raw_ref.shape
    count = (channels // GROUPS) * rows * LANES * 8
    at = own_ref.shape[0] - 8
    totals = (own_ref[at:, :] + one_ref[at:, :]) + (two_ref[at:, :] + three_ref[at:, :])
    totals = group_sum(totals) / count
    turned = jnp.concatenate([totals, jnp.zeros((LANES - 8, LANES), F32)], axis=0).T
    wide = lambda v, at: jnp.broadcast_to(v[:, at : at + 1], (channels, LANES))
    mean_grad, second = wide(turned, 0), wide(turned, 1)
    columns = columns_ref[...]
    center, inverse = wide(columns, 0), wide(columns, 1)

    def step(r, carry):
        normed = (plane_ref[:, row_at(r)].astype(F32) - center) * inverse
        flat[r] = inverse * (scaled_ref[:, row_at(r)] - mean_grad - normed * second)
        return carry

    lax.fori_loop(0, rows, step, 0, unroll=2)
    for c in range(0, channels, 16):
        out_ref[c : c + 16] = (raw_ref[c : c + 16].astype(F32) + turn(flat[:, c : c + 16, :])).astype(BF16)


def place_kernel(me_ref, *refs):
    spatial_ref, temporal_ref, whole = refs[8:]
    core, spot = me_ref[1], me_ref[2]
    part = whole.shape[1]
    for slot in range(4):
        at = 2 * (slot ^ spot)
        whole[at + core] = refs[slot][0:part]
        whole[at + 1 - core] = refs[4 + slot][0:part]
    split = spatial_ref.shape[0] // part
    spatial_ref[...] = whole[0:split].reshape(spatial_ref.shape)
    temporal_ref[...] = whole[split:].reshape(temporal_ref.shape)


def body(inputs, cotangent, spatial_weight, temporal_weight, norm_gain, norm_shift, spatial_bias):
    frames = lax.axis_size("frame")
    peers = lax.axis_size("chan")
    core = lax.axis_index("frame") % 2
    me = lax.axis_index("chan")
    channels, rows, cols = inputs.shape[1:]
    pixels = rows * cols
    plane, half = (channels, pixels), (channels, pixels // 2)
    tied = lax.optimization_barrier
    at = lax.axis_index("frame")
    place = jnp.stack([me, core, me // 2, (at // 2 % 2) ^ core]).astype(jnp.int32)
    table = jnp.concatenate([v[None] for v in (norm_gain, norm_shift, spatial_bias)])
    raw_in, raw_grad = inputs[0], cotangent[0]
    cross = lambda v: lax.ppermute(v, "frame", neighbour(frames))
    mate = lambda v: lax.ppermute(v, "frame", partner(1, frames))

    def meet(v, frame_bits, chan_bits):
        return lax.ppermute(v, ("frame", "chan"), both(frame_bits, chan_bits, frames, peers))

    def total(v, steps):
        got = [v] + [meet(v, *step) for step in steps]
        return got[0] + got[1] if len(got) == 2 else (got[0] + got[1]) + (got[2] + got[3])

    turned, payload = call(
        sums_kernel, [(plane, BF16), ((peers, 8 + rows, channels), F32)], [place, raw_in], cost=(0, 2 * MIB), limit=8
    )
    payload, later_grad, table = tied((payload, raw_grad, table))
    received = lax.all_to_all(payload, "chan", 0, 0, tiled=True)
    early_grad, late_grad = call(turn_kernel, [(half, BF16)] * 2, [later_grad], cost=(0, 1000), limit=8)
    crossed = [cross(early_grad)]
    received, early_grad, late_grad = tied((received, early_grad, late_grad))
    grads = [early_grad, late_grad]
    crossed.append(cross(late_grad))
    mates = [mate(v) for v in grads]

    padded = (3 * channels, pixels + 2 * cols)
    act, hidden, slope, columns = call(
        forward_kernel,
        [(padded, BF16), (plane, BF16), (plane, F32), ((channels, LANES), F32)],
        [place, turned, received, table, spatial_weight],
        cost=(1000, MIB),
        limit=16,
    )
    early_shape, late_shape = (3 * channels, channels), (3 * channels, 3 * channels)
    shifted = pltpu.VMEM((channels, pixels // 2 + 4 * cols), BF16)
    pre_early, *sums = call(
        functools.partial(backward_kernel, False),
        [(half, BF16), (early_shape, F32), (late_shape, F32), ((LANES, channels), F32)],
        [place, act, hidden, slope, grads[0], mates[0], crossed[0], temporal_weight],
        [shifted],
        cost=(1000, MIB),
        limit=20,
    )
    part = 12 * channels // 8
    slots = ((4, part, channels), F32)
    pre_late, keep, send, edges = call(
        functools.partial(backward_kernel, True),
        [(half, BF16), slots, slots, ((2 * rows, channels), F32)],
        [place, act, hidden, slope, grads[1], mates[1], crossed[1], temporal_weight, *sums],
        [pltpu.VMEM(early_shape, F32), pltpu.VMEM(late_shape, F32), shifted],
        cost=(1000, MIB),
        limit=20,
    )
    near = meet(edges, 0, 1)
    terms = keep + mate(send)
    terms, near, hidden = tied((terms, near, hidden))
    hidden_inside, hidden_mate = lax.ppermute(hidden, "frame", crossing(frames, True)), mate(hidden)
    far = near[rows:]
    one, two, three = [
        meet(jnp.concatenate([terms[b], far]) if b != 2 else terms[b], 0, 2 * b) for b in (1, 2, 3)
    ]
    piece = (terms[0] + one[:part]) + (two + three[:part])
    piece, one, three, hidden_mate = tied((piece, one, three, hidden_mate))
    scaled, sums = call(
        input_kernel,
        [(plane, F32), ((8, channels), F32)],
        [place, pre_early, pre_late, near, one, three, spatial_weight, turned, columns],
        [pltpu.VMEM(padded, BF16), pltpu.VMEM((channels, pixels + 2 * cols), F32)],
        cost=(1000, MIB),
        limit=16,
    )
    piece = total(piece, [(4, 0), (8, 0), (12, 0)])
    piece, sums = tied((piece, sums))
    sums = total(sums, [(0, 1)])
    piece = total(piece, [(16, 0)])
    piece = total(piece, [(2, 0), (0, 1), (2, 1)])
    piece, hidden, hidden_inside = tied((jnp.concatenate([piece, sums]), hidden, hidden_inside))
    flat = pltpu.VMEM((rows, channels, cols), F32)
    got = [piece] + [meet(piece, 0, 2 * b) for b in (1, 2, 3)]
    hidden_outside = lax.ppermute(hidden, "frame", crossing(frames, False))
    others = [mate(v) for v in got]
    (input_grad,) = call(
        final_kernel,
        [(raw_in.shape, BF16)],
        [*got, scaled, turned, columns, raw_grad],
        [flat],
        cost=(1000, MIB),
        limit=16,
    )
    spatial_grad, temporal_grad = call(
        place_kernel,
        [((9 * channels, channels), F32), ((3 * channels, channels), F32)],
        [place, *got, *others],
        [pltpu.VMEM((8, part, channels), F32)],
        cost=(1000, MIB),
        limit=8,
    )
    hidden_outside, input_grad, spatial_grad = tied((hidden_outside, input_grad, spatial_grad))
    (output,) = call(
        output_kernel,
        [(raw_in.shape, BF16)],
        [place, hidden, hidden_mate, hidden_inside, hidden_outside, temporal_weight, raw_in],
        [flat],
        cost=(1000, MIB),
        limit=16,
    )
    square = (-1, channels, channels)
    return (output[None], input_grad[None], spatial_grad.reshape(square), temporal_grad.reshape(square))


def solution(mesh):
    banded = P("frame", None, None, "chan")
    return jax.shard_map(
        body,
        mesh=mesh,
        in_specs=(banded, banded, P(), P(), P(), P(), P()),
        out_specs=(banded, banded, P(), P()),
        check_vma=False,
    )
```

time: 122 us -> 111 us (0.910)
  the two profiles are of different devices: /device:TPU:1 before, /device:TPU:32 now
where the time goes in v1:
time: 111 us
  starting transfers between devices  51.7 us (47%)
  waiting for transfers between devices  30.1 us (27%)
  Pallas kernels  26.1 us (24%)
  local copies, waits for them, and re-layouts  1.26 us (1%)
    ppermute x15, starting transfers between devices, meet(): lax.ppermute(v, ('frame', 'chan'), both(frame_bits, chan_bits, frames, pe...  26.1 us
    pallas_call x9, Pallas kernels, call(): pl.pallas_call(kernel, out_shape=[jax.ShapeDtypeStruct(s, d) for s, d in...  26.1 us
    ppermute x15, waiting for transfers between devices, meet(): lax.ppermute(v, ('frame', 'chan'), both(frame_bits, chan_bits, frames, pe...  23.5 us
    ppermute x8, starting transfers between devices, body(): mate = lambda v: lax.ppermute(v, 'frame', partner(1, frames))  10.4 us
    ppermute x2, starting transfers between devices, body(): cross = lambda v: lax.ppermute(v, 'frame', neighbour(frames))  7.11 us
    all_to_all x1, starting transfers between devices, body(): received = lax.all_to_all(payload, 'chan', 0, 0, tiled=True)  5.4 us
    all_to_all x1, waiting for transfers between devices, body(): received = lax.all_to_all(payload, 'chan', 0, 0, tiled=True)  2.52 us
    ppermute x1, waiting for transfers between devices, body(): hidden_outside = lax.ppermute(hidden, 'frame', crossing(frames, False))  2.42 us
  transfers between devices with their start and end apart: 28, of which 13 were waited for; matrix products, arithmetic and copies ran while one was open for 0% of the time, Pallas kernels for 16%

profile of v1, /device:TPU:32, one launch (start us, length us, event | category | flops | bytes accessed | tf_op | source)
XLA Modules:
  0.0 111.0 jit_solution(4059954367423389745)
XLA Ops:
  0.8 1.2 %copy-done = bf16[1,128,32,128]{3,2,1,0:T(8,128)(2,1)S(1)} copy-done((bf16[1,128,32,128]{3,2,1,0:T(8,128)(2,1)S(1)}, bf16[1,128,32,128]{3,2,1,0:T(8,128)(2,1)}, u32[]{:S(2)}) %copy-start) | copy-done | bytes 1048600
  2.0 2.5 %shard_map.102 = (bf16[128,4096]{1,0:T(8,128)(2,1)S(1)}, f32[8,40,128]{2,1,0:T(8,128)}) custom-call(s32[4]{0:T(128)S(1)} %pad_add_fusion.me_ref, bf16[128,32,128]{2,1,0:T(8,128)(2,1)S(1)} %bitcast.21), custom_call_target="tpu_custom_call" | custom-call | bytes 2097152 | tf_op jit(solution)/shard_map/pallas_call | solution.py:44
  5.2 5.4 %all-to-all-start = ((f32[8,40,128]{2,1,0:T(8,128)}), f32[8,40,128]{2,1,0:T(8,128)S(1)}, u32[]{:S(2)}, u32[]{:S(2)}) async-start(f32[8,40,128]{2,1,0:T(8,128)} %get-tuple-element.47), calls=%async_computation | async-start | bytes 327680 | tf_op jit(solution)/shard_map/all_to_all | solution.py:381
  11.6 3.3 %collective-permute-start.3 = (bf16[128,2048]{1,0:T(8,128)(2,1)}, bf16[128,2048]{1,0:T(8,128)(2,1)}, u32[]{:S(2)}, u32[]{:S(2)}) collective-permute-start(bf16[128,2048]{1,0:T(8,128)(2,1)} %get-tuple-element.57.grad_ref), channel_id=1, source_target_pairs={{8,16},{16,8},{24,32},{32,24},{40,48},{48,40},{56,64},{64,56},{72,... | collective-permute-start | bytes 1572872 | tf_op jit(solution)/shard_map/ppermute | solution.py:367
  14.9 2.5 %all-to-all-done.received_ref = f32[8,40,128]{2,1,0:T(8,128)S(1)} async-done(((f32[8,40,128]{2,1,0:T(8,128)}), f32[8,40,128]{2,1,0:T(8,128)S(1)}, u32[]{:S(2)}, u32[]{:S(2)}) %all-to-all-start) | async-done | bytes 163872 | tf_op jit(solution)/shard_map/all_to_all | solution.py:381
  17.9 3.8 %collective-permute-start.1 = (bf16[128,2048]{1,0:T(8,128)(2,1)S(1)}, bf16[128,2048]{1,0:T(8,128)(2,1)S(1)}, u32[]{:S(2)}, u32[]{:S(2)}) collective-permute-start(bf16[128,2048]{1,0:T(8,128)(2,1)S(1)} %get-tuple-element.56.grad_ref), channel_id=1, source_target_pairs={{8,16},{16,8},{24,32},{32,24},{40,48},{48,40},{56,64},{64,56},{72,... | collective-permute-start | bytes 1572872 | tf_op jit(solution)/shard_map/ppermute | solution.py:367
  21.7 4.4 %shard_map.104 = (bf16[384,4352]{1,0:T(8,128)(2,1)S(1)}, bf16[128,4096]{1,0:T(8,128)(2,1)S(1)}, f32[128,4096]{1,0:T(8,128)S(1)}, f32[128,128]{1,0:T(8,128)S(1)}) custom-call(s32[4]{0:T(128)S(1)} %pad_add_fusion.me_ref, bf16[128,4096]{1,0:T(8,128)(2,1)S(1)} %get-tuple-element.45.plane_ref.refs_1_, f32[8,40,128]{2,1,0:T(8,128)S(1)} %all-to-all-done.received_ref, ...), custom_call_target="tpu_custom_call" | custom-call | flops 1000 | bytes 1048576 | tf_op jit(solution)/shard_map/pallas_call | solution.py:44
  26.1 3.2 %shard_map.105 = (bf16[128,2048]{1,0:T(8,128)(2,1)S(1)}, f32[384,128]{1,0:T(8,128)S(1)}, f32[384,384]{1,0:T(8,128)S(1)}, f32[128,128]{1,0:T(8,128)S(1)}) custom-call(s32[4]{0:T(128)S(1)} %pad_add_fusion.me_ref, bf16[384,4352]{1,0:T(8,128)(2,1)S(1)} %get-tuple-element.53.act_ref, bf16[128,4096]{1,0:T(8,128)(2,1)S(1)} %get-tuple-element.76.hidden_ref, ...), custom_call_target="tpu_custom_call" | custom-call | flops 1000 | bytes 1048576 | tf_op jit(solution)/shard_map/pallas_call | solution.py:44
  29.3 1.6 %collective-permute-done.1.cross_ref = bf16[128,2048]{1,0:T(8,128)(2,1)S(1)} collective-permute-done((bf16[128,2048]{1,0:T(8,128)(2,1)S(1)}, bf16[128,2048]{1,0:T(8,128)(2,1)S(1)}, u32[]{:S(2)}, u32[]{:S(2)}) %collective-permute-start.1) | collective-permute-done | bytes 524320 | tf_op jit(solution)/shard_map/ppermute | solution.py:367
  30.9 2.6 %shard_map.106 = (bf16[128,2048]{1,0:T(8,128)(2,1)S(1)}, f32[4,192,128]{2,1,0:T(8,128)S(1)}, f32[4,192,128]{2,1,0:T(8,128)S(1)}, f32[64,128]{1,0:T(8,128)S(1)}) custom-call(s32[4]{0:T(128)S(1)} %pad_add_fusion.me_ref, bf16[384,4352]{1,0:T(8,128)(2,1)S(1)} %get-tuple-element.53.act_ref, bf16[128,4096]{1,0:T(8,128)(2,1)S(1)} %get-tuple-element.76.hidden_ref, ...), custom_call_target="tpu_custom_call" | custom-call | flops 1000 | bytes 1048576 | tf_op jit(solution)/shard_map/pallas_call | solution.py:44
  33.5 9.4 %collective-permute-start.4 = (f32[4,192,128]{2,1,0:T(8,128)S(1)}, f32[4,192,128]{2,1,0:T(8,128)S(1)}, u32[]{:S(2)}, u32[]{:S(2)}) collective-permute-start(f32[4,192,128]{2,1,0:T(8,128)S(1)} %get-tuple-element.62), channel_id=1, source_target_pairs={{0,8},{8,0},{16,24},{24,16},{32,40},{40,32},{48,56},{56,48},{64,72... | collective-permute-start | bytes 1179656 | tf_op jit(solution)/shard_map/ppermute | solution.py:368
  42.9 1.7 %collective-permute-start.5 = (f32[64,128]{1,0:T(8,128)S(1)}, f32[64,128]{1,0:T(8,128)S(1)}, u32[]{:S(2)}, u32[]{:S(2)}) collective-permute-start(f32[64,128]{1,0:T(8,128)S(1)} %get-tuple-element.63), channel_id=1, source_target_pairs={{0,1},{1,0},{2,3},{3,2},{4,5},{5,4},{6,7},{7,6},{8,9},{9,8},{10,11... | collective-permute-start | bytes 98312 | tf_op jit(solution)/shard_map/ppermute | solution.py:371
  44.6 2.2 %collective-permute-done.5.near_ref = f32[64,128]{1,0:T(8,128)S(1)} collective-permute-done((f32[64,128]{1,0:T(8,128)S(1)}, f32[64,128]{1,0:T(8,128)S(1)}, u32[]{:S(2)}, u32[]{:S(2)}) %collective-permute-start.5) | collective-permute-done | bytes 32800 | tf_op jit(solution)/shard_map/ppermute | solution.py:371
  46.8 2.1 %collective-permute-start.6 = (f32[224,128]{1,0:T(8,128)S(1)}, f32[224,128]{1,0:T(8,128)S(1)}, u32[]{:S(2)}, u32[]{:S(2)}) collective-permute-start(f32[224,128]{1,0:T(8,128)S(1)} %get-tuple-element.89), channel_id=1, source_target_pairs={{0,2},{1,3},{2,0},{3,1},{4,6},{5,7},{6,4},{7,5},{8,10},{9,11},{10,... | collective-permute-start | bytes 344072 | tf_op jit(solution)/shard_map/ppermute | solution.py:371
  48.9 2.1 %collective-permute-start.8 = (f32[224,128]{1,0:T(8,128)S(1)}, f32[224,128]{1,0:T(8,128)S(1)}, u32[]{:S(2)}, u32[]{:S(2)}) collective-permute-start(f32[224,128]{1,0:T(8,128)S(1)} %get-tuple-element.90), channel_id=1, source_target_pairs={{0,6},{1,7},{2,4},{3,5},{4,2},{5,3},{6,0},{7,1},{8,14},{9,15},{10,... | collective-permute-start | bytes 344072 | tf_op jit(solution)/shard_map/ppermute | solution.py:371
  52.4 5.0 %collective-permute-done.7 = f32[192,128]{1,0:T(8,128)S(1)} collective-permute-done((f32[192,128]{1,0:T(8,128)S(1)}, f32[192,128]{1,0:T(8,128)S(1)}, u32[]{:S(2)}, u32[]{:S(2)}) %collective-permute-start.7) | collective-permute-done | bytes 98336 | tf_op jit(solution)/shard_map/ppermute | solution.py:371
  57.9 3.4 %collective-permute-start.11 = (f32[192,128]{1,0:T(8,128)S(1)}, f32[192,128]{1,0:T(8,128)S(1)}, u32[]{:S(2)}, u32[]{:S(2)}) collective-permute-start(f32[192,128]{1,0:T(8,128)S(1)} %fusion), channel_id=1, source_target_pairs={{0,64},{1,65},{2,66},{3,67},{4,68},{5,69},{6,70},{7,71},{8,72},{9,... | collective-permute-start | bytes 294920 | tf_op jit(solution)/shard_map/ppermute | solution.py:371
  61.7 5.3 %shard_map.107 = (f32[128,4096]{1,0:T(8,128)S(1)}, f32[8,128]{1,0:T(8,128)S(1)}) custom-call(s32[4]{0:T(128)S(1)} %pad_add_fusion.me_ref, bf16[128,2048]{1,0:T(8,128)(2,1)S(1)} %get-tuple-element.68.early_ref, bf16[128,2048]{1,0:T(8,128)(2,1)S(1)} %get-tuple-element.69.late_ref, f32[64,128]{1,0:T(8,128)S(1)} %collective-permute-done.5.near_ref, ...), custom_call_target="tpu_custom_call" | custom-call | flops 1000 | bytes 1048576 | tf_op jit(solution)/shard_map/pallas_call | solution.py:44
  68.1 2.0 %collective-permute-done.12 = f32[192,128]{1,0:T(8,128)S(1)} collective-permute-done((f32[192,128]{1,0:T(8,128)S(1)}, f32[192,128]{1,0:T(8,128)S(1)}, u32[]{:S(2)}, u32[]{:S(2)}) %collective-permute-start.12) | collective-permute-done | bytes 98336 | tf_op jit(solution)/shard_map/ppermute | solution.py:371
  70.1 5.8 %collective-permute-start.13 = (f32[192,128]{1,0:T(8,128)S(1)}, f32[192,128]{1,0:T(8,128)S(1)}, u32[]{:S(2)}, u32[]{:S(2)}) collective-permute-start(f32[192,128]{1,0:T(8,128)S(1)} %add_add_fusion.1), channel_id=1, source_target_pairs={{0,128},{1,129},{2,130},{3,131},{4,132},{5,133},{6,134},{7,135},{8... | collective-permute-start | bytes 294920 | tf_op jit(solution)/shard_map/ppermute | solution.py:371
  75.8 4.0 %collective-permute-done.13 = f32[192,128]{1,0:T(8,128)S(1)} collective-permute-done((f32[192,128]{1,0:T(8,128)S(1)}, f32[192,128]{1,0:T(8,128)S(1)}, u32[]{:S(2)}, u32[]{:S(2)}) %collective-permute-start.13) | collective-permute-done | bytes 98336 | tf_op jit(solution)/shard_map/ppermute | solution.py:371
  79.8 2.9 %collective-permute-start.14 = (f32[192,128]{1,0:T(8,128)S(1)}, f32[192,128]{1,0:T(8,128)S(1)}, u32[]{:S(2)}, u32[]{:S(2)}) collective-permute-start(f32[192,128]{1,0:T(8,128)S(1)} %add.54), channel_id=1, source_target_pairs={{0,16},{1,17},{2,18},{3,19},{4,20},{5,21},{6,22},{7,23},{8,24},{9,... | collective-permute-start | bytes 294920 | tf_op jit(solution)/shard_map/ppermute | solution.py:371
  84.8 2.7 %collective-permute-done.17 = f32[8,128]{1,0:T(8,128)S(1)} collective-permute-done((f32[8,128]{1,0:T(8,128)S(1)}, f32[8,128]{1,0:T(8,128)S(1)}, u32[]{:S(2)}, u32[]{:S(2)}) %collective-permute-start.17) | collective-permute-done | bytes 4128 | tf_op jit(solution)/shard_map/ppermute | solution.py:371
  87.6 1.8 %collective-permute-done.16 = f32[192,128]{1,0:T(8,128)S(1)} collective-permute-done((f32[192,128]{1,0:T(8,128)S(1)}, f32[192,128]{1,0:T(8,128)S(1)}, u32[]{:S(2)}, u32[]{:S(2)}) %collective-permute-start.16) | collective-permute-done | bytes 98336 | tf_op jit(solution)/shard_map/ppermute | solution.py:371
  89.4 1.9 %collective-permute-start.19 = (bf16[128,4096]{1,0:T(8,128)(2,1)S(1)}, bf16[128,4096]{1,0:T(8,128)(2,1)S(1)}, u32[]{:S(2)}, u32[]{:S(2)}) collective-permute-start(bf16[128,4096]{1,0:T(8,128)(2,1)S(1)} %get-tuple-element.76.hidden_ref), channel_id=1, source_target_pairs={{24,32},{32,24},{56,64},{64,56},{88,96},{96,88},{120,128},{128,120... | collective-permute-start | bytes 3145736 | tf_op jit(solution)/shard_map/ppermute | solution.py:443
  92.2 3.2 %collective-permute-start.21 = (f32[200,128]{1,0:T(8,128)S(1)}, f32[200,128]{1,0:T(8,128)S(1)}, u32[]{:S(2)}, u32[]{:S(2)}) collective-permute-start(f32[200,128]{1,0:T(8,128)S(1)} %pad_maximum_fusion.2.own_ref.refs_0_), channel_id=1, source_target_pairs={{0,4},{1,5},{2,6},{3,7},{4,0},{5,1},{6,2},{7,3},{8,12},{9,13},{10,... | collective-permute-start | bytes 307208 | tf_op jit(solution)/shard_map/ppermute | solution.py:371
  96.7 2.5 %collective-permute-done.21.two_ref.refs_2_ = f32[200,128]{1,0:T(8,128)S(1)} collective-permute-done((f32[200,128]{1,0:T(8,128)S(1)}, f32[200,128]{1,0:T(8,128)S(1)}, u32[]{:S(2)}, u32[]{:S(2)}) %collective-permute-start.21) | collective-permute-done | bytes 102432 | tf_op jit(solution)/shard_map/ppermute | solution.py:371
  99.2 2.1 %collective-permute-done.22.three_ref.refs_3_ = f32[200,128]{1,0:T(8,128)S(1)} collective-permute-done((f32[200,128]{1,0:T(8,128)S(1)}, f32[200,128]{1,0:T(8,128)S(1)}, u32[]{:S(2)}, u32[]{:S(2)}) %collective-permute-start.22) | collective-permute-done | bytes 102432 | tf_op jit(solution)/shard_map/ppermute | solution.py:371
  101.3 2.7 %shard_map.108 = bf16[128,32,128]{2,1,0:T(8,128)(2,1)} custom-call(f32[200,128]{1,0:T(8,128)S(1)} %pad_maximum_fusion.2.own_ref.refs_0_, f32[200,128]{1,0:T(8,128)S(1)} %collective-permute-done.20.one_ref.refs_1_, f32[200,128]{1,0:T(8,128)S(1)} %collective-permute-done.21.two_ref.refs_2_, f32[200,128]{1,0:T(8,128)S(1)} %collective-permute-done.22.three_ref.refs_3_, ...), custom_call_target="tpu_custom_call" | custom-call | flops 1000 | bytes 1048576 | tf_op jit(solution)/shard_map/pallas_call | solution.py:44
  104.0 1.5 %shard_map.109 = (f32[1152,128]{1,0:T(8,128)}, f32[384,128]{1,0:T(8,128)}) custom-call(s32[4]{0:T(128)S(1)} %pad_add_fusion.me_ref, f32[200,128]{1,0:T(8,128)S(1)} %pad_maximum_fusion.2.own_ref.refs_0_, f32[200,128]{1,0:T(8,128)S(1)} %collective-permute-done.20.one_ref.refs_1_, f32[200,128]{1,0:T(8,128)S(1)} %collective-permute-done.21.two_ref.refs_2_, ...), custom_call_target="tpu_custom_call" | custom-call | flops 1000 | bytes 1048576 | tf_op jit(solution)/shard_map/pallas_call | solution.py:44
  105.5 2.4 %collective-permute-done.19.outside_ref = bf16[128,4096]{1,0:T(8,128)(2,1)S(1)} collective-permute-done((bf16[128,4096]{1,0:T(8,128)(2,1)S(1)}, bf16[128,4096]{1,0:T(8,128)(2,1)S(1)}, u32[]{:S(2)}, u32[]{:S(2)}) %collective-permute-start.19) | collective-permute-done | bytes 1048608 | tf_op jit(solution)/shard_map/ppermute | solution.py:443
  108.0 3.0 %shard_map.110 = bf16[128,32,128]{2,1,0:T(8,128)(2,1)} custom-call(s32[4]{0:T(128)S(1)} %pad_add_fusion.me_ref, bf16[128,4096]{1,0:T(8,128)(2,1)S(1)} %get-tuple-element.76.hidden_ref, bf16[128,4096]{1,0:T(8,128)(2,1)S(1)} %collective-permute-done.9.mate_ref, bf16[128,4096]{1,0:T(8,128)(2,1)S(1)} %collective-permute-done.18.inside_ref, ...), custom_call_target="tpu_custom_call" | custom-call | flops 1000 | bytes 1048576 | tf_op jit(solution)/shard_map/pallas_call | solution.py:44
  (55 shorter events, 10.0 us)
Async XLA Ops:
  0.6 25.5 %copy-start.4 = (bf16[3,128,128]{2,1,0:T(8,128)(2,1)S(1)}, bf16[3,128,128]{2,1,0:T(8,128)(2,1)}, u32[]{:S(2)}) copy-start(bf16[3,128,128]{2,1,0:T(8,128)(2,1)} %weight_ref.3) | copy-start | bytes 294916
  2.0 8.6 %copy-start.2 = (bf16[1,128,32,128]{3,2,1,0:T(8,128)(2,1)S(1)}, bf16[1,128,32,128]{3,2,1,0:T(8,128)(2,1)}, u32[]{:S(2)}) copy-start(bf16[1,128,32,128]{3,2,1,0:T(8,128)(2,1)} %param.8) | copy-start | bytes 3145732
  2.0 19.7 %copy-start.3 = (bf16[9,128,128]{2,1,0:T(8,128)(2,1)S(1)}, bf16[9,128,128]{2,1,0:T(8,128)(2,1)}, u32[]{:S(2)}) copy-start(bf16[9,128,128]{2,1,0:T(8,128)(2,1)} %refs_0_.1) | copy-start | bytes 884740
  5.2 12.2 %all-to-all-start = ((f32[8,40,128]{2,1,0:T(8,128)}), f32[8,40,128]{2,1,0:T(8,128)S(1)}, u32[]{:S(2)}, u32[]{:S(2)}) async-start(f32[8,40,128]{2,1,0:T(8,128)} %get-tuple-element.47), calls=%async_computation | async-start | bytes 327680 | tf_op jit(solution)/shard_map/all_to_all | solution.py:381
  11.6 14.5 %collective-permute-start.3 = (bf16[128,2048]{1,0:T(8,128)(2,1)}, bf16[128,2048]{1,0:T(8,128)(2,1)}, u32[]{:S(2)}, u32[]{:S(2)}) collective-permute-start(bf16[128,2048]{1,0:T(8,128)(2,1)} %get-tuple-element.57.grad_ref), channel_id=1, source_target_pairs={{8,16},{16,8},{24,32},{32,24},{40,48},{48,40},{56,64},{64,56},{72,... | collective-permute-start | bytes 1572872 | tf_op jit(solution)/shard_map/ppermute | solution.py:367
  17.4 8.7 %collective-permute-start.2 = (bf16[128,2048]{1,0:T(8,128)(2,1)}, bf16[128,2048]{1,0:T(8,128)(2,1)S(1)}, u32[]{:S(2)}, u32[]{:S(2)}) collective-permute-start(bf16[128,2048]{1,0:T(8,128)(2,1)} %get-tuple-element.57.grad_ref), channel_id=1, source_target_pairs={{0,8},{8,0},{16,24},{24,16},{32,40},{40,32},{48,56},{56,48},{64,72... | collective-permute-start | bytes 1572872 | tf_op jit(solution)/shard_map/ppermute | solution.py:368
  17.4 11.9 %collective-permute-start = (bf16[128,2048]{1,0:T(8,128)(2,1)S(1)}, bf16[128,2048]{1,0:T(8,128)(2,1)S(1)}, u32[]{:S(2)}, u32[]{:S(2)}) collective-permute-start(bf16[128,2048]{1,0:T(8,128)(2,1)S(1)} %get-tuple-element.56.grad_ref), channel_id=1, source_target_pairs={{0,8},{8,0},{16,24},{24,16},{32,40},{40,32},{48,56},{56,48},{64,72... | collective-permute-start | bytes 1572872 | tf_op jit(solution)/shard_map/ppermute | solution.py:368
  17.9 13.0 %collective-permute-start.1 = (bf16[128,2048]{1,0:T(8,128)(2,1)S(1)}, bf16[128,2048]{1,0:T(8,128)(2,1)S(1)}, u32[]{:S(2)}, u32[]{:S(2)}) collective-permute-start(bf16[128,2048]{1,0:T(8,128)(2,1)S(1)} %get-tuple-element.56.grad_ref), channel_id=1, source_target_pairs={{8,16},{16,8},{24,32},{32,24},{40,48},{48,40},{56,64},{64,56},{72,... | collective-permute-start | bytes 1572872 | tf_op jit(solution)/shard_map/ppermute | solution.py:367
  33.5 11.1 %collective-permute-start.4 = (f32[4,192,128]{2,1,0:T(8,128)S(1)}, f32[4,192,128]{2,1,0:T(8,128)S(1)}, u32[]{:S(2)}, u32[]{:S(2)}) collective-permute-start(f32[4,192,128]{2,1,0:T(8,128)S(1)} %get-tuple-element.62), channel_id=1, source_target_pairs={{0,8},{8,0},{16,24},{24,16},{32,40},{40,32},{48,56},{56,48},{64,72... | collective-permute-start | bytes 1179656 | tf_op jit(solution)/shard_map/ppermute | solution.py:368
  42.9 3.9 %collective-permute-start.5 = (f32[64,128]{1,0:T(8,128)S(1)}, f32[64,128]{1,0:T(8,128)S(1)}, u32[]{:S(2)}, u32[]{:S(2)}) collective-permute-start(f32[64,128]{1,0:T(8,128)S(1)} %get-tuple-element.63), channel_id=1, source_target_pairs={{0,1},{1,0},{2,3},{3,2},{4,5},{5,4},{6,7},{7,6},{8,9},{9,8},{10,11... | collective-permute-start | bytes 98312 | tf_op jit(solution)/shard_map/ppermute | solution.py:371
  46.8 10.8 %collective-permute-start.9 = (bf16[128,4096]{1,0:T(8,128)(2,1)S(1)}, bf16[128,4096]{1,0:T(8,128)(2,1)S(1)}, u32[]{:S(2)}, u32[]{:S(2)}) collective-permute-start(bf16[128,4096]{1,0:T(8,128)(2,1)S(1)} %get-tuple-element.76.hidden_ref), channel_id=1, source_target_pairs={{0,8},{8,0},{16,24},{24,16},{32,40},{40,32},{48,56},{56,48},{64,72... | collective-permute-start | bytes 3145736 | tf_op jit(solution)/shard_map/ppermute | solution.py:368
  46.8 10.5 %collective-permute-start.6 = (f32[224,128]{1,0:T(8,128)S(1)}, f32[224,128]{1,0:T(8,128)S(1)}, u32[]{:S(2)}, u32[]{:S(2)}) collective-permute-start(f32[224,128]{1,0:T(8,128)S(1)} %get-tuple-element.89), channel_id=1, source_target_pairs={{0,2},{1,3},{2,0},{3,1},{4,6},{5,7},{6,4},{7,5},{8,10},{9,11},{10,... | collective-permute-start | bytes 344072 | tf_op jit(solution)/shard_map/ppermute | solution.py:371
  48.9 8.6 %collective-permute-start.8 = (f32[224,128]{1,0:T(8,128)S(1)}, f32[224,128]{1,0:T(8,128)S(1)}, u32[]{:S(2)}, u32[]{:S(2)}) collective-permute-start(f32[224,128]{1,0:T(8,128)S(1)} %get-tuple-element.90), channel_id=1, source_target_pairs={{0,6},{1,7},{2,4},{3,5},{4,2},{5,3},{6,0},{7,1},{8,14},{9,15},{10,... | collective-permute-start | bytes 344072 | tf_op jit(solution)/shard_map/ppermute | solution.py:371
  51.0 6.4 %collective-permute-start.7 = (f32[192,128]{1,0:T(8,128)S(1)}, f32[192,128]{1,0:T(8,128)S(1)}, u32[]{:S(2)}, u32[]{:S(2)}) collective-permute-start(f32[192,128]{1,0:T(8,128)S(1)} %get-tuple-element.88), channel_id=1, source_target_pairs={{0,4},{1,5},{2,6},{3,7},{4,0},{5,1},{6,2},{7,3},{8,12},{9,13},{10,... | collective-permute-start | bytes 294920 | tf_op jit(solution)/shard_map/ppermute | solution.py:371
  51.6 37.8 %collective-permute-start.18 = (bf16[128,4096]{1,0:T(8,128)(2,1)S(1)}, bf16[128,4096]{1,0:T(8,128)(2,1)S(1)}, u32[]{:S(2)}, u32[]{:S(2)}) collective-permute-start(bf16[128,4096]{1,0:T(8,128)(2,1)S(1)} %get-tuple-element.76.hidden_ref), channel_id=1, source_target_pairs={{8,16},{16,8},{40,48},{48,40},{72,80},{80,72},{104,112},{112,104},... | collective-permute-start | bytes 3145736 | tf_op jit(solution)/shard_map/ppermute | solution.py:420
  57.6 9.5 %collective-permute-start.10 = (f32[192,128]{1,0:T(8,128)S(1)}, f32[192,128]{1,0:T(8,128)S(1)}, u32[]{:S(2)}, u32[]{:S(2)}) collective-permute-start(f32[192,128]{1,0:T(8,128)S(1)} %fusion), channel_id=1, source_target_pairs={{0,32},{1,33},{2,34},{3,35},{4,36},{5,37},{6,38},{7,39},{8,40},{9,... | collective-permute-start | bytes 294920 | tf_op jit(solution)/shard_map/ppermute | solution.py:371
  57.9 10.2 %collective-permute-start.11 = (f32[192,128]{1,0:T(8,128)S(1)}, f32[192,128]{1,0:T(8,128)S(1)}, u32[]{:S(2)}, u32[]{:S(2)}) collective-permute-start(f32[192,128]{1,0:T(8,128)S(1)} %fusion), channel_id=1, source_target_pairs={{0,64},{1,65},{2,66},{3,67},{4,68},{5,69},{6,70},{7,71},{8,72},{9,... | collective-permute-start | bytes 294920 | tf_op jit(solution)/shard_map/ppermute | solution.py:371
  61.2 8.8 %collective-permute-start.12 = (f32[192,128]{1,0:T(8,128)S(1)}, f32[192,128]{1,0:T(8,128)S(1)}, u32[]{:S(2)}, u32[]{:S(2)}) collective-permute-start(f32[192,128]{1,0:T(8,128)S(1)} %fusion), channel_id=1, source_target_pairs={{0,96},{1,97},{2,98},{3,99},{4,100},{5,101},{6,102},{7,103},{8,104... | collective-permute-start | bytes 294920 | tf_op jit(solution)/shard_map/ppermute | solution.py:371
  70.1 9.7 %collective-permute-start.13 = (f32[192,128]{1,0:T(8,128)S(1)}, f32[192,128]{1,0:T(8,128)S(1)}, u32[]{:S(2)}, u32[]{:S(2)}) collective-permute-start(f32[192,128]{1,0:T(8,128)S(1)} %add_add_fusion.1), channel_id=1, source_target_pairs={{0,128},{1,129},{2,130},{3,131},{4,132},{5,133},{6,134},{7,135},{8... | collective-permute-start | bytes 294920 | tf_op jit(solution)/shard_map/ppermute | solution.py:371
  79.8 7.8 %collective-permute-start.14 = (f32[192,128]{1,0:T(8,128)S(1)}, f32[192,128]{1,0:T(8,128)S(1)}, u32[]{:S(2)}, u32[]{:S(2)}) collective-permute-start(f32[192,128]{1,0:T(8,128)S(1)} %add.54), channel_id=1, source_target_pairs={{0,16},{1,17},{2,18},{3,19},{4,20},{5,21},{6,22},{7,23},{8,24},{9,... | collective-permute-start | bytes 294920 | tf_op jit(solution)/shard_map/ppermute | solution.py:371
  82.7 4.9 %collective-permute-start.15 = (f32[192,128]{1,0:T(8,128)S(1)}, f32[192,128]{1,0:T(8,128)S(1)}, u32[]{:S(2)}, u32[]{:S(2)}) collective-permute-start(f32[192,128]{1,0:T(8,128)S(1)} %add.54), channel_id=1, source_target_pairs={{0,1},{1,0},{2,3},{3,2},{4,5},{5,4},{6,7},{7,6},{8,9},{9,8},{10,11... | collective-permute-start | bytes 294920 | tf_op jit(solution)/shard_map/ppermute | solution.py:371
  83.6 5.8 %collective-permute-start.16 = (f32[192,128]{1,0:T(8,128)S(1)}, f32[192,128]{1,0:T(8,128)S(1)}, u32[]{:S(2)}, u32[]{:S(2)}) collective-permute-start(f32[192,128]{1,0:T(8,128)S(1)} %add.54), channel_id=1, source_target_pairs={{0,17},{1,16},{2,19},{3,18},{4,21},{5,20},{6,23},{7,22},{8,25},{9,... | collective-permute-start | bytes 294920 | tf_op jit(solution)/shard_map/ppermute | solution.py:371
  84.0 3.6 %collective-permute-start.17 = (f32[8,128]{1,0:T(8,128)S(1)}, f32[8,128]{1,0:T(8,128)S(1)}, u32[]{:S(2)}, u32[]{:S(2)}) collective-permute-start(f32[8,128]{1,0:T(8,128)S(1)} %get-tuple-element.75), channel_id=1, source_target_pairs={{0,1},{1,0},{2,3},{3,2},{4,5},{5,4},{6,7},{7,6},{8,9},{9,8},{10,11... | collective-permute-start | bytes 12296 | tf_op jit(solution)/shard_map/ppermute | solution.py:371
  89.4 18.5 %collective-permute-start.19 = (bf16[128,4096]{1,0:T(8,128)(2,1)S(1)}, bf16[128,4096]{1,0:T(8,128)(2,1)S(1)}, u32[]{:S(2)}, u32[]{:S(2)}) collective-permute-start(bf16[128,4096]{1,0:T(8,128)(2,1)S(1)} %get-tuple-element.76.hidden_ref), channel_id=1, source_target_pairs={{24,32},{32,24},{56,64},{64,56},{88,96},{96,88},{120,128},{128,120... | collective-permute-start | bytes 3145736 | tf_op jit(solution)/shard_map/ppermute | solution.py:443
  91.4 4.8 %collective-permute-start.20 = (f32[200,128]{1,0:T(8,128)S(1)}, f32[200,128]{1,0:T(8,128)S(1)}, u32[]{:S(2)}, u32[]{:S(2)}) collective-permute-start(f32[200,128]{1,0:T(8,128)S(1)} %pad_maximum_fusion.2.own_ref.refs_0_), channel_id=1, source_target_pairs={{0,2},{1,3},{2,0},{3,1},{4,6},{5,7},{6,4},{7,5},{8,10},{9,11},{10,... | collective-permute-start | bytes 307208 | tf_op jit(solution)/shard_map/ppermute | solution.py:371
  92.2 6.9 %collective-permute-start.21 = (f32[200,128]{1,0:T(8,128)S(1)}, f32[200,128]{1,0:T(8,128)S(1)}, u32[]{:S(2)}, u32[]{:S(2)}) collective-permute-start(f32[200,128]{1,0:T(8,128)S(1)} %pad_maximum_fusion.2.own_ref.refs_0_), channel_id=1, source_target_pairs={{0,4},{1,5},{2,6},{3,7},{4,0},{5,1},{6,2},{7,3},{8,12},{9,13},{10,... | collective-permute-start | bytes 307208 | tf_op jit(solution)/shard_map/ppermute | solution.py:371
  95.4 5.9 %collective-permute-start.22 = (f32[200,128]{1,0:T(8,128)S(1)}, f32[200,128]{1,0:T(8,128)S(1)}, u32[]{:S(2)}, u32[]{:S(2)}) collective-permute-start(f32[200,128]{1,0:T(8,128)S(1)} %pad_maximum_fusion.2.own_ref.refs_0_), channel_id=1, source_target_pairs={{0,6},{1,7},{2,4},{3,5},{4,2},{5,3},{6,0},{7,1},{8,14},{9,15},{10,... | collective-permute-start | bytes 307208 | tf_op jit(solution)/shard_map/ppermute | solution.py:371
  96.2 7.9 %collective-permute-start.23 = (f32[200,128]{1,0:T(8,128)S(1)}, f32[200,128]{1,0:T(8,128)S(1)}, u32[]{:S(2)}, u32[]{:S(2)}) collective-permute-start(f32[200,128]{1,0:T(8,128)S(1)} %pad_maximum_fusion.2.own_ref.refs_0_), channel_id=1, source_target_pairs={{0,8},{8,0},{16,24},{24,16},{32,40},{40,32},{48,56},{56,48},{64,72... | collective-permute-start | bytes 307208 | tf_op jit(solution)/shard_map/ppermute | solution.py:368
  96.2 7.9 %collective-permute-start.24 = (f32[200,128]{1,0:T(8,128)S(1)}, f32[200,128]{1,0:T(8,128)S(1)}, u32[]{:S(2)}, u32[]{:S(2)}) collective-permute-start(f32[200,128]{1,0:T(8,128)S(1)} %collective-permute-done.20.one_ref.refs_1_), channel_id=1, source_target_pairs={{0,8},{8,0},{16,24},{24,16},{32,40},{40,32},{48,56},{56,48},{64,72... | collective-permute-start | bytes 307208 | tf_op jit(solution)/shard_map/ppermute | solution.py:368
  99.2 4.9 %collective-permute-start.25 = (f32[200,128]{1,0:T(8,128)S(1)}, f32[200,128]{1,0:T(8,128)S(1)}, u32[]{:S(2)}, u32[]{:S(2)}) collective-permute-start(f32[200,128]{1,0:T(8,128)S(1)} %collective-permute-done.21.two_ref.refs_2_), channel_id=1, source_target_pairs={{0,8},{8,0},{16,24},{24,16},{32,40},{40,32},{48,56},{56,48},{64,72... | collective-permute-start | bytes 307208 | tf_op jit(solution)/shard_map/ppermute | solution.py:368
  101.3 2.7 %collective-permute-start.26 = (f32[200,128]{1,0:T(8,128)S(1)}, f32[200,128]{1,0:T(8,128)S(1)}, u32[]{:S(2)}, u32[]{:S(2)}) collective-permute-start(f32[200,128]{1,0:T(8,128)S(1)} %collective-permute-done.22.three_ref.refs_3_), channel_id=1, source_target_pairs={{0,8},{8,0},{16,24},{24,16},{32,40},{40,32},{48,56},{56,48},{64,72... | collective-permute-start | bytes 307208 | tf_op jit(solution)/shard_map/ppermute | solution.py:368
  101.3 6.7 %copy-start.1 = (bf16[1,128,32,128]{3,2,1,0:T(8,128)(2,1)S(1)}, bf16[1,128,32,128]{3,2,1,0:T(8,128)(2,1)}, u32[]{:S(2)}) copy-start(bf16[1,128,32,128]{3,2,1,0:T(8,128)(2,1)} %param.7) | copy-start | bytes 3145732
  (1 other events, 1.2 us)

commit v2 on v1

--- a/solution.py
+++ b/solution.py
@@ -36,7 +36,7 @@
     return pairs
 
 
-def call(kernel, outs, ins, scratch=(), cost=(0, 0), limit=24):
+def call(kernel, outs, ins, scratch=(), cost=(0, 0), limit=24, place=pltpu.VMEM):
     smem = pl.BlockSpec(memory_space=pltpu.SMEM)
     vmem = pl.BlockSpec(memory_space=pltpu.VMEM)
     is_place = lambda v: v.dtype == jnp.int32
@@ -45,7 +45,7 @@
         kernel,
         out_shape=[jax.ShapeDtypeStruct(s, d) for s, d in outs],
         in_specs=[smem if is_place(v) else vmem for v in ins],
-        out_specs=[vmem] * len(outs),
+        out_specs=[pl.BlockSpec(memory_space=place)] * len(outs),
         scratch_shapes=list(scratch),
         cost_estimate=pl.CostEstimate(flops=flops, bytes_accessed=moved, transcendentals=0),
         compiler_params=pltpu.CompilerParams(vmem_limit_bytes=limit * MIB),
@@ -295,28 +295,54 @@
     sums_ref[...] = jnp.where(lane == 0, plain, jnp.where(lane == 1, crossed, 0.0)).T[0:8]
 
 
-def output_kernel(me_ref, hidden_ref, mate_ref, inside_ref, outside_ref, weight_ref, raw_ref, out_ref, flat):
+def partial_kernel(me_ref, hidden_ref, mate_ref, inside_ref, weight_ref, raw_ref, out_ref, flat):
     channels, rows, _ = raw_ref.shape
-    inside = me_ref[3] == 1
     even = me_ref[1] == 0
     pick = lambda a, b: jnp.where(even, weight_ref[a].astype(F32), weight_ref[b].astype(F32)).astype(BF16)
     weights = jnp.concatenate([weight_ref[1], pick(2, 0), pick(0, 2)], axis=1)
     each = TILE // LANES
-
-    def step(n, carry):
-        across = jnp.where(inside, inside_ref[:, tile_at(n)], outside_ref[:, tile_at(n)])
-        frames = jnp.concatenate([hidden_ref[:, tile_at(n)], mate_ref[:, tile_at(n)], across], axis=0)
+    for n in range(rows // each):
+        at = span(n * each, each)
+        frames = jnp.concatenate([ref[:, at] for ref in (hidden_ref, mate_ref, inside_ref)], axis=0)
         mixed = jnp.dot(weights, frames, preferred_element_type=F32)
         for i in range(each):
-            flat[n * each + i] = mixed[:, i * LANES : (i + 1) * LANES]
-        return carry
-
-    lax.fori_loop(0, rows // each, step, 0, unroll=2)
+            flat[n * each + i] = mixed[:, span(i, 1)]
     for c in range(0, channels, 16):
-        out_ref[c : c + 16] = (raw_ref[c : c + 16].astype(F32) + turn(flat[:, c : c + 16, :])).astype(BF16)
-
-
-def final_kernel(own_ref, one_ref, two_ref, three_ref, scaled_ref, plane_ref, columns_ref, raw_ref, out_ref, flat):
+        out_ref[c : c + 16] = raw_ref[c : c + 16].astype(F32) + turn(flat[:, c : c + 16, :])
+
+
+def close_kernel(me_ref, *refs):
+    partial_ref, outside_ref, weight_ref, spatial_ref, temporal_ref, out_ref, whole, flat, staged, sems = refs[8:]
+    core, spot = me_ref[1], me_ref[2]
+    channels, rows, _ = partial_ref.shape
+    part = whole.shape[1]
+    for slot in range(4):
+        at = 2 * (slot ^ spot)
+        whole[at + core] = refs[slot][0:part]
+        whole[at + 1 - core] = refs[4 + slot][0:part]
+    split, blocks = spatial_ref.shape[0], channels // 16
+    copies = [
+        pltpu.make_async_copy(whole.at[0:split], spatial_ref, sems.at[blocks]),
+        pltpu.make_async_copy(whole.at[split:], temporal_ref, sems.at[blocks + 1]),
+    ]
+    for copy in copies:
+        copy.start()
+    weight = jnp.where(core == 0, weight_ref[0].astype(F32), weight_ref[2].astype(F32)).astype(BF16)
+    each = TILE // LANES
+    for n in range(rows // each):
+        mixed = jnp.dot(weight, outside_ref[:, span(n * each, each)], preferred_element_type=F32)
+        for i in range(each):
+            flat[n * each + i] = mixed[:, span(i, 1)]
+    for i in range(blocks):
+        at = slice(16 * i, 16 * i + 16)
+        staged[at] = (partial_ref[at] + turn(flat[:, at, :])).astype(BF16)
+        copies.append(pltpu.make_async_copy(staged.at[at], out_ref.at[at], sems.at[i]))
+        copies[-1].start()
+    for copy in copies:
+        copy.wait()
+
+
+def final_kernel(own_ref, one_ref, two_ref, three_ref, scaled_ref, plane_ref, columns_ref, raw_ref, out_ref, flat, staged, sems):
     channels, rows, _ = raw_ref.shape
     count = (channels // GROUPS) * rows * LANES * 8
     at = own_ref.shape[0] - 8
@@ -334,21 +360,14 @@
         return carry
 
     lax.fori_loop(0, rows, step, 0, unroll=2)
-    for c in range(0, channels, 16):
-        out_ref[c : c + 16] = (raw_ref[c : c + 16].astype(F32) + turn(flat[:, c : c + 16, :])).astype(BF16)
-
-
-def place_kernel(me_ref, *refs):
-    spatial_ref, temporal_ref, whole = refs[8:]
-    core, spot = me_ref[1], me_ref[2]
-    part = whole.shape[1]
-    for slot in range(4):
-        at = 2 * (slot ^ spot)
-        whole[at + core] = refs[slot][0:part]
-        whole[at + 1 - core] = refs[4 + slot][0:part]
-    split = spatial_ref.shape[0] // part
-    spatial_ref[...] = whole[0:split].reshape(spatial_ref.shape)
-    temporal_ref[...] = whole[split:].reshape(temporal_ref.shape)
+    copies = []
+    for i in range(channels // 16):
+        at = slice(16 * i, 16 * i + 16)
+        staged[at] = (raw_ref[at].astype(F32) + turn(flat[:, at, :])).astype(BF16)
+        copies.append(pltpu.make_async_copy(staged.at[at], out_ref.at[at], sems.at[i]))
+        copies[-1].start()
+    for copy in copies:
+        copy.wait()
 
 
 def body(inputs, cotangent, spatial_weight, temporal_weight, norm_gain, norm_shift, spatial_bias):
@@ -363,6 +382,7 @@
     at = lax.axis_index("frame")
     place = jnp.stack([me, core, me // 2, (at // 2 % 2) ^ core]).astype(jnp.int32)
     table = jnp.concatenate([v[None] for v in (norm_gain, norm_shift, spatial_bias)])
+    place, table = tied((place, table))
     raw_in, raw_grad = inputs[0], cotangent[0]
     cross = lambda v: lax.ppermute(v, "frame", neighbour(frames))
     mate = lambda v: lax.ppermute(v, "frame", partner(1, frames))
@@ -377,7 +397,7 @@
     turned, payload = call(
         sums_kernel, [(plane, BF16), ((peers, 8 + rows, channels), F32)], [place, raw_in], cost=(0, 2 * MIB), limit=8
     )
-    payload, later_grad, table = tied((payload, raw_grad, table))
+    payload, later_grad = tied((payload, raw_grad))
     received = lax.all_to_all(payload, "chan", 0, 0, tiled=True)
     early_grad, late_grad = call(turn_kernel, [(half, BF16)] * 2, [later_grad], cost=(0, 1000), limit=8)
     crossed = [cross(early_grad)]
@@ -434,38 +454,43 @@
     )
     piece = total(piece, [(4, 0), (8, 0), (12, 0)])
     piece, sums = tied((piece, sums))
-    sums = total(sums, [(0, 1)])
-    piece = total(piece, [(16, 0)])
-    piece = total(piece, [(2, 0), (0, 1), (2, 1)])
-    piece, hidden, hidden_inside = tied((jnp.concatenate([piece, sums]), hidden, hidden_inside))
+    piece = total(piece, [(28, 0)])
+    both_x = total(jnp.concatenate([piece, sums]), [(0, 1)])
+    both_x, hidden_inside = tied((both_x, hidden_inside))
+    piece, sums = both_x[:part], both_x[part:]
     flat = pltpu.VMEM((rows, channels, cols), F32)
+    (partial,) = call(
+        partial_kernel,
+        [(raw_in.shape, F32)],
+        [place, hidden, hidden_mate, hidden_inside, temporal_weight, raw_in],
+        [flat],
+        cost=(1, 1),
+        limit=16,
+    )
+    piece = total(piece, [(2, 1)])
+    piece, hidden, partial = tied((jnp.concatenate([piece, sums]), hidden, partial))
     got = [piece] + [meet(piece, 0, 2 * b) for b in (1, 2, 3)]
     hidden_outside = lax.ppermute(hidden, "frame", crossing(frames, False))
     others = [mate(v) for v in got]
+    staged, sems = pltpu.VMEM(raw_in.shape, BF16), pltpu.SemaphoreType.DMA((10,))
     (input_grad,) = call(
         final_kernel,
         [(raw_in.shape, BF16)],
         [*got, scaled, turned, columns, raw_grad],
-        [flat],
+        [flat, staged, sems],
         cost=(1000, MIB),
         limit=16,
-    )
-    spatial_grad, temporal_grad = call(
-        place_kernel,
-        [((9 * channels, channels), F32), ((3 * channels, channels), F32)],
-        [place, *got, *others],
-        [pltpu.VMEM((8, part, channels), F32)],
-        cost=(1000, MIB),
-        limit=8,
-    )
-    hidden_outside, input_grad, spatial_grad = tied((hidden_outside, input_grad, spatial_grad))
-    (output,) = call(
-        output_kernel,
-        [(raw_in.shape, BF16)],
-        [place, hidden, hidden_mate, hidden_inside, hidden_outside, temporal_weight, raw_in],
-        [flat],
+        place=pl.ANY,
+    )
+    hidden_outside, input_grad = tied((hidden_outside, input_grad))
+    spatial_grad, temporal_grad, output = call(
+        close_kernel,
+        [((6, part, channels), F32), ((2, part, channels), F32), (raw_in.shape, BF16)],
+        [place, *got, *others, partial, hidden_outside, temporal_weight],
+        [pltpu.VMEM((8, part, channels), F32), flat, staged, sems],
         cost=(1000, MIB),
         limit=16,
+        place=pl.ANY,
     )
     square = (-1, channels, channels)
     return (output[None], input_grad[None], spatial_grad.reshape(square), temporal_grad.reshape(square))

time: 111 us -> 110 us (level)
  starting transfers between devices: 51.7 us -> 50.1 us
    ppermute x15 -> x13, starting transfers between devices: 26.1 us -> 24.5 us  [meet(): lax.ppermute(v, ('frame', 'chan'), both(frame_bits, chan_bits, frames, pe...]
    ppermute x1, waiting for transfers between devices: 2.42 us -> 4.04 us  [body(): hidden_outside = lax.ppermute(hidden, 'frame', crossing(frames, False))]
    ppermute x15 -> x13, waiting for transfers between devices: 23.5 us -> 22.9 us  [meet(): lax.ppermute(v, ('frame', 'chan'), both(frame_bits, chan_bits, frames, pe...]
  transfers between devices with their start and end apart: 28 -> 26, of which waited for: 13 -> 13; matrix products, arithmetic and copies ran while one was open for 0% -> 0% of each run, Pallas kernels for 16% -> 16%
where the time goes in v2:
time: 110 us
  starting transfers between devices  50.1 us (46%)
  waiting for transfers between devices  31.1 us (28%)
  Pallas kernels  25.3 us (23%)
  local copies, waits for them, and re-layouts  1.27 us (1%)
    pallas_call x9, Pallas kernels, call(): pl.pallas_call(kernel, out_shape=[jax.ShapeDtypeStruct(s, d) for s, d in...  25.3 us
    ppermute x13, starting transfers between devices, meet(): lax.ppermute(v, ('frame', 'chan'), both(frame_bits, chan_bits, frames, pe...  24.5 us
    ppermute x13, waiting for transfers between devices, meet(): lax.ppermute(v, ('frame', 'chan'), both(frame_bits, chan_bits, frames, pe...  22.9 us
    ppermute x8, starting transfers between devices, body(): mate = lambda v: lax.ppermute(v, 'frame', partner(1, frames))  10.4 us
    ppermute x2, starting transfers between devices, body(): cross = lambda v: lax.ppermute(v, 'frame', neighbour(frames))  7.11 us
    all_to_all x1, starting transfers between devices, body(): received = lax.all_to_all(payload, 'chan', 0, 0, tiled=True)  5.4 us
    ppermute x1, waiting for transfers between devices, body(): hidden_outside = lax.ppermute(hidden, 'frame', crossing(frames, False))  4.04 us
    all_to_all x1, waiting for transfers between devices, body(): received = lax.all_to_all(payload, 'chan', 0, 0, tiled=True)  2.52 us
  transfers between devices with their start and end apart: 26, of which 13 were waited for; matrix products, arithmetic and copies ran while one was open for 0% of the time, Pallas kernels for 16%

profile of v2, /device:TPU:32, one launch (start us, length us, event | category | flops | bytes accessed | tf_op | source)
XLA Modules:
  0.0 109.8 jit_solution(8286299899653032948)
XLA Ops:
  2.7 2.5 %shard_map.102 = (bf16[128,4096]{1,0:T(8,128)(2,1)S(1)}, f32[8,40,128]{2,1,0:T(8,128)}) custom-call(s32[4]{0:T(128)S(1)} %pad_add_fusion.me_ref, bf16[128,32,128]{2,1,0:T(8,128)(2,1)S(1)} %bitcast.21), custom_call_target="tpu_custom_call" | custom-call | bytes 2097152 | tf_op jit(solution)/shard_map/pallas_call | solution.py:44
  5.2 5.4 %all-to-all-start = ((f32[8,40,128]{2,1,0:T(8,128)}), f32[8,40,128]{2,1,0:T(8,128)S(1)}, u32[]{:S(2)}, u32[]{:S(2)}) async-start(f32[8,40,128]{2,1,0:T(8,128)} %get-tuple-element.51), calls=%async_computation | async-start | bytes 327680 | tf_op jit(solution)/shard_map/all_to_all | solution.py:401
  11.6 3.3 %collective-permute-start.3 = (bf16[128,2048]{1,0:T(8,128)(2,1)}, bf16[128,2048]{1,0:T(8,128)(2,1)}, u32[]{:S(2)}, u32[]{:S(2)}) collective-permute-start(bf16[128,2048]{1,0:T(8,128)(2,1)} %get-tuple-element.61.grad_ref), channel_id=1, source_target_pairs={{8,16},{16,8},{24,32},{32,24},{40,48},{48,40},{56,64},{64,56},{72,... | collective-permute-start | bytes 1572872 | tf_op jit(solution)/shard_map/ppermute | solution.py:387
  14.9 2.5 %all-to-all-done.received_ref = f32[8,40,128]{2,1,0:T(8,128)S(1)} async-done(((f32[8,40,128]{2,1,0:T(8,128)}), f32[8,40,128]{2,1,0:T(8,128)S(1)}, u32[]{:S(2)}, u32[]{:S(2)}) %all-to-all-start) | async-done | bytes 163872 | tf_op jit(solution)/shard_map/all_to_all | solution.py:401
  17.9 3.8 %collective-permute-start.1 = (bf16[128,2048]{1,0:T(8,128)(2,1)S(1)}, bf16[128,2048]{1,0:T(8,128)(2,1)S(1)}, u32[]{:S(2)}, u32[]{:S(2)}) collective-permute-start(bf16[128,2048]{1,0:T(8,128)(2,1)S(1)} %get-tuple-element.60.grad_ref), channel_id=1, source_target_pairs={{8,16},{16,8},{24,32},{32,24},{40,48},{48,40},{56,64},{64,56},{72,... | collective-permute-start | bytes 1572872 | tf_op jit(solution)/shard_map/ppermute | solution.py:387
  21.7 4.3 %shard_map.104 = (bf16[384,4352]{1,0:T(8,128)(2,1)S(1)}, bf16[128,4096]{1,0:T(8,128)(2,1)S(1)}, f32[128,4096]{1,0:T(8,128)S(1)}, f32[128,128]{1,0:T(8,128)S(1)}) custom-call(s32[4]{0:T(128)S(1)} %pad_add_fusion.me_ref, bf16[128,4096]{1,0:T(8,128)(2,1)S(1)} %get-tuple-element.49.plane_ref.refs_1_, f32[8,40,128]{2,1,0:T(8,128)S(1)} %all-to-all-done.received_ref, ...), custom_call_target="tpu_custom_call" | custom-call | flops 1000 | bytes 1048576 | tf_op jit(solution)/shard_map/pallas_call | solution.py:44
  26.1 3.2 %shard_map.105 = (bf16[128,2048]{1,0:T(8,128)(2,1)S(1)}, f32[384,128]{1,0:T(8,128)S(1)}, f32[384,384]{1,0:T(8,128)S(1)}, f32[128,128]{1,0:T(8,128)S(1)}) custom-call(s32[4]{0:T(128)S(1)} %pad_add_fusion.me_ref, bf16[384,4352]{1,0:T(8,128)(2,1)S(1)} %get-tuple-element.57.act_ref, bf16[128,4096]{1,0:T(8,128)(2,1)S(1)} %get-tuple-element.85.hidden_ref, ...), custom_call_target="tpu_custom_call" | custom-call | flops 1000 | bytes 1048576 | tf_op jit(solution)/shard_map/pallas_call | solution.py:44
  29.3 1.6 %collective-permute-done.1.cross_ref = bf16[128,2048]{1,0:T(8,128)(2,1)S(1)} collective-permute-done((bf16[128,2048]{1,0:T(8,128)(2,1)S(1)}, bf16[128,2048]{1,0:T(8,128)(2,1)S(1)}, u32[]{:S(2)}, u32[]{:S(2)}) %collective-permute-start.1) | collective-permute-done | bytes 524320 | tf_op jit(solution)/shard_map/ppermute | solution.py:387
  30.9 2.6 %shard_map.106 = (bf16[128,2048]{1,0:T(8,128)(2,1)S(1)}, f32[4,192,128]{2,1,0:T(8,128)S(1)}, f32[4,192,128]{2,1,0:T(8,128)S(1)}, f32[64,128]{1,0:T(8,128)S(1)}) custom-call(s32[4]{0:T(128)S(1)} %pad_add_fusion.me_ref, bf16[384,4352]{1,0:T(8,128)(2,1)S(1)} %get-tuple-element.57.act_ref, bf16[128,4096]{1,0:T(8,128)(2,1)S(1)} %get-tuple-element.85.hidden_ref, ...), custom_call_target="tpu_custom_call" | custom-call | flops 1000 | bytes 1048576 | tf_op jit(solution)/shard_map/pallas_call | solution.py:44
  33.5 9.4 %collective-permute-start.4 = (f32[4,192,128]{2,1,0:T(8,128)S(1)}, f32[4,192,128]{2,1,0:T(8,128)S(1)}, u32[]{:S(2)}, u32[]{:S(2)}) collective-permute-start(f32[4,192,128]{2,1,0:T(8,128)S(1)} %get-tuple-element.66), channel_id=1, source_target_pairs={{0,8},{8,0},{16,24},{24,16},{32,40},{40,32},{48,56},{56,48},{64,72... | collective-permute-start | bytes 1179656 | tf_op jit(solution)/shard_map/ppermute | solution.py:388
  42.9 1.7 %collective-permute-start.5 = (f32[64,128]{1,0:T(8,128)S(1)}, f32[64,128]{1,0:T(8,128)S(1)}, u32[]{:S(2)}, u32[]{:S(2)}) collective-permute-start(f32[64,128]{1,0:T(8,128)S(1)} %get-tuple-element.67), channel_id=1, source_target_pairs={{0,1},{1,0},{2,3},{3,2},{4,5},{5,4},{6,7},{7,6},{8,9},{9,8},{10,11... | collective-permute-start | bytes 98312 | tf_op jit(solution)/shard_map/ppermute | solution.py:391
  44.6 2.2 %collective-permute-done.5.near_ref = f32[64,128]{1,0:T(8,128)S(1)} collective-permute-done((f32[64,128]{1,0:T(8,128)S(1)}, f32[64,128]{1,0:T(8,128)S(1)}, u32[]{:S(2)}, u32[]{:S(2)}) %collective-permute-start.5) | collective-permute-done | bytes 32800 | tf_op jit(solution)/shard_map/ppermute | solution.py:391
  46.8 2.1 %collective-permute-start.6 = (f32[224,128]{1,0:T(8,128)S(1)}, f32[224,128]{1,0:T(8,128)S(1)}, u32[]{:S(2)}, u32[]{:S(2)}) collective-permute-start(f32[224,128]{1,0:T(8,128)S(1)} %get-tuple-element.95), channel_id=1, source_target_pairs={{0,2},{1,3},{2,0},{3,1},{4,6},{5,7},{6,4},{7,5},{8,10},{9,11},{10,... | collective-permute-start | bytes 344072 | tf_op jit(solution)/shard_map/ppermute | solution.py:391
  48.9 2.1 %collective-permute-start.8 = (f32[224,128]{1,0:T(8,128)S(1)}, f32[224,128]{1,0:T(8,128)S(1)}, u32[]{:S(2)}, u32[]{:S(2)}) collective-permute-start(f32[224,128]{1,0:T(8,128)S(1)} %get-tuple-element.96), channel_id=1, source_target_pairs={{0,6},{1,7},{2,4},{3,5},{4,2},{5,3},{6,0},{7,1},{8,14},{9,15},{10,... | collective-permute-start | bytes 344072 | tf_op jit(solution)/shard_map/ppermute | solution.py:391
  52.4 5.0 %collective-permute-done.7 = f32[192,128]{1,0:T(8,128)S(1)} collective-permute-done((f32[192,128]{1,0:T(8,128)S(1)}, f32[192,128]{1,0:T(8,128)S(1)}, u32[]{:S(2)}, u32[]{:S(2)}) %collective-permute-start.7) | collective-permute-done | bytes 98336 | tf_op jit(solution)/shard_map/ppermute | solution.py:391
  57.9 3.4 %collective-permute-start.11 = (f32[192,128]{1,0:T(8,128)S(1)}, f32[192,128]{1,0:T(8,128)S(1)}, u32[]{:S(2)}, u32[]{:S(2)}) collective-permute-start(f32[192,128]{1,0:T(8,128)S(1)} %fusion), channel_id=1, source_target_pairs={{0,64},{1,65},{2,66},{3,67},{4,68},{5,69},{6,70},{7,71},{8,72},{9,... | collective-permute-start | bytes 294920 | tf_op jit(solution)/shard_map/ppermute | solution.py:391
  61.7 5.3 %shard_map.107 = (f32[128,4096]{1,0:T(8,128)S(1)}, f32[8,128]{1,0:T(8,128)S(1)}) custom-call(s32[4]{0:T(128)S(1)} %pad_add_fusion.me_ref, bf16[128,2048]{1,0:T(8,128)(2,1)S(1)} %get-tuple-element.72.early_ref, bf16[128,2048]{1,0:T(8,128)(2,1)S(1)} %get-tuple-element.73.late_ref, f32[64,128]{1,0:T(8,128)S(1)} %collective-permute-done.5.near_ref, ...), custom_call_target="tpu_custom_call" | custom-call | flops 1000 | bytes 1048576 | tf_op jit(solution)/shard_map/pallas_call | solution.py:44
  68.1 2.0 %collective-permute-done.12 = f32[192,128]{1,0:T(8,128)S(1)} collective-permute-done((f32[192,128]{1,0:T(8,128)S(1)}, f32[192,128]{1,0:T(8,128)S(1)}, u32[]{:S(2)}, u32[]{:S(2)}) %collective-permute-start.12) | collective-permute-done | bytes 98336 | tf_op jit(solution)/shard_map/ppermute | solution.py:391
  70.1 5.3 %collective-permute-start.13 = (f32[192,128]{1,0:T(8,128)S(1)}, f32[192,128]{1,0:T(8,128)S(1)}, u32[]{:S(2)}, u32[]{:S(2)}) collective-permute-start(f32[192,128]{1,0:T(8,128)S(1)} %add_add_fusion), channel_id=1, source_target_pairs={{0,224},{1,225},{2,226},{3,227},{4,228},{5,229},{6,230},{7,231},{8... | collective-permute-start | bytes 294920 | tf_op jit(solution)/shard_map/ppermute | solution.py:391
  75.4 2.7 %collective-permute-done.13 = f32[192,128]{1,0:T(8,128)S(1)} collective-permute-done((f32[192,128]{1,0:T(8,128)S(1)}, f32[192,128]{1,0:T(8,128)S(1)}, u32[]{:S(2)}, u32[]{:S(2)}) %collective-permute-start.13) | collective-permute-done | bytes 98336 | tf_op jit(solution)/shard_map/ppermute | solution.py:391
  79.0 3.8 %collective-permute-done.14 = f32[200,128]{1,0:T(8,128)S(1)} collective-permute-done((f32[200,128]{1,0:T(8,128)S(1)}, f32[200,128]{1,0:T(8,128)S(1)}, u32[]{:S(2)}, u32[]{:S(2)}) %collective-permute-start.14) | collective-permute-done | bytes 102432 | tf_op jit(solution)/shard_map/ppermute | solution.py:391
  82.8 2.9 %collective-permute-start.16 = (f32[192,128]{1,0:T(8,128)S(1)}, f32[192,128]{1,0:T(8,128)S(1)}, u32[]{:S(2)}, u32[]{:S(2)}) collective-permute-start(f32[192,128]{1,0:T(8,128)S(1)} %slice.34), channel_id=1, source_target_pairs={{0,17},{1,16},{2,19},{3,18},{4,21},{5,20},{6,23},{7,22},{8,25},{9,... | collective-permute-start | bytes 294920 | tf_op jit(solution)/shard_map/ppermute | solution.py:391
  85.7 1.7 %shard_map.108.refs_8_ = f32[128,32,128]{2,1,0:T(8,128)S(1)} custom-call(s32[4]{0:T(128)S(1)} %pad_add_fusion.me_ref, bf16[128,4096]{1,0:T(8,128)(2,1)S(1)} %get-tuple-element.85.hidden_ref, bf16[128,4096]{1,0:T(8,128)(2,1)S(1)} %collective-permute-done.9.mate_ref, bf16[128,4096]{1,0:T(8,128)(2,1)S(1)} %collective-permute-done.15.inside_ref, ...), custom_call_target="tpu_custom_call" | custom-call | flops 1 | bytes 1 | tf_op jit(solution)/shard_map/pallas_call | solution.py:44
  87.4 1.3 %collective-permute-done.16 = f32[192,128]{1,0:T(8,128)S(1)} collective-permute-done((f32[192,128]{1,0:T(8,128)S(1)}, f32[192,128]{1,0:T(8,128)S(1)}, u32[]{:S(2)}, u32[]{:S(2)}) %collective-permute-start.16) | collective-permute-done | bytes 98336 | tf_op jit(solution)/shard_map/ppermute | solution.py:391
  88.8 1.9 %collective-permute-start.24 = (bf16[128,4096]{1,0:T(8,128)(2,1)S(1)}, bf16[128,4096]{1,0:T(8,128)(2,1)S(1)}, u32[]{:S(2)}, u32[]{:S(2)}) collective-permute-start(bf16[128,4096]{1,0:T(8,128)(2,1)S(1)} %get-tuple-element.85.hidden_ref), channel_id=1, source_target_pairs={{24,32},{32,24},{56,64},{64,56},{88,96},{96,88},{120,128},{128,120... | collective-permute-start | bytes 3145736 | tf_op jit(solution)/shard_map/ppermute | solution.py:473
  90.7 1.5 %collective-permute-start.17 = (f32[200,128]{1,0:T(8,128)S(1)}, f32[200,128]{1,0:T(8,128)S(1)}, u32[]{:S(2)}, u32[]{:S(2)}) collective-permute-start(f32[200,128]{1,0:T(8,128)S(1)} %pad_maximum_fusion.3.own_ref.refs_0_), channel_id=1, source_target_pairs={{0,2},{1,3},{2,0},{3,1},{4,6},{5,7},{6,4},{7,5},{8,10},{9,11},{10,... | collective-permute-start | bytes 307208 | tf_op jit(solution)/shard_map/ppermute | solution.py:391
  92.2 2.7 %collective-permute-start.18 = (f32[200,128]{1,0:T(8,128)S(1)}, f32[200,128]{1,0:T(8,128)S(1)}, u32[]{:S(2)}, u32[]{:S(2)}) collective-permute-start(f32[200,128]{1,0:T(8,128)S(1)} %pad_maximum_fusion.3.own_ref.refs_0_), channel_id=1, source_target_pairs={{0,4},{1,5},{2,6},{3,7},{4,0},{5,1},{6,2},{7,3},{8,12},{9,13},{10,... | collective-permute-start | bytes 307208 | tf_op jit(solution)/shard_map/ppermute | solution.py:391
  96.0 2.6 %collective-permute-done.18.two_ref.refs_2_ = f32[200,128]{1,0:T(8,128)S(1)} collective-permute-done((f32[200,128]{1,0:T(8,128)S(1)}, f32[200,128]{1,0:T(8,128)S(1)}, u32[]{:S(2)}, u32[]{:S(2)}) %collective-permute-start.18) | collective-permute-done | bytes 102432 | tf_op jit(solution)/shard_map/ppermute | solution.py:391
  98.6 2.1 %collective-permute-done.19.three_ref.refs_3_ = f32[200,128]{1,0:T(8,128)S(1)} collective-permute-done((f32[200,128]{1,0:T(8,128)S(1)}, f32[200,128]{1,0:T(8,128)S(1)}, u32[]{:S(2)}, u32[]{:S(2)}) %collective-permute-start.19) | collective-permute-done | bytes 102432 | tf_op jit(solution)/shard_map/ppermute | solution.py:391
  100.8 2.5 %shard_map.109 = bf16[128,32,128]{2,1,0:T(8,128)(2,1)} custom-call(f32[200,128]{1,0:T(8,128)S(1)} %pad_maximum_fusion.3.own_ref.refs_0_, f32[200,128]{1,0:T(8,128)S(1)} %collective-permute-done.17.one_ref.refs_1_, f32[200,128]{1,0:T(8,128)S(1)} %collective-permute-done.18.two_ref.refs_2_, f32[200,128]{1,0:T(8,128)S(1)} %collective-permute-done.19.three_ref.refs_3_, ...), custom_call_target="tpu_custom_call" | custom-call | flops 1000 | bytes 1048576 | tf_op jit(solution)/shard_map/pallas_call | solution.py:44
  103.3 4.0 %collective-permute-done.24.refs_9_ = bf16[128,4096]{1,0:T(8,128)(2,1)S(1)} collective-permute-done((bf16[128,4096]{1,0:T(8,128)(2,1)S(1)}, bf16[128,4096]{1,0:T(8,128)(2,1)S(1)}, u32[]{:S(2)}, u32[]{:S(2)}) %collective-permute-start.24) | collective-permute-done | bytes 1048608 | tf_op jit(solution)/shard_map/ppermute | solution.py:473
  107.3 2.3 %shard_map.110 = (f32[6,192,128]{2,1,0:T(8,128)}, f32[2,192,128]{2,1,0:T(8,128)}, bf16[128,32,128]{2,1,0:T(8,128)(2,1)}) custom-call(s32[4]{0:T(128)S(1)} %pad_add_fusion.me_ref, f32[200,128]{1,0:T(8,128)S(1)} %pad_maximum_fusion.3.own_ref.refs_0_, f32[200,128]{1,0:T(8,128)S(1)} %collective-permute-done.17.one_ref.refs_1_, ...), custom_call_target="tpu_custom_call" | custom-call | flops 1000 | bytes 1048576 | tf_op jit(solution)/shard_map/pallas_call | solution.py:44
  (54 shorter events, 9.1 us)
Async XLA Ops:
  0.6 25.5 %copy-start.3 = (bf16[3,128,128]{2,1,0:T(8,128)(2,1)S(1)}, bf16[3,128,128]{2,1,0:T(8,128)(2,1)}, u32[]{:S(2)}) copy-start(bf16[3,128,128]{2,1,0:T(8,128)(2,1)} %refs_10_.1) | copy-start | bytes 294916
  1.5 1.2 %copy-start = (bf16[1,128,32,128]{3,2,1,0:T(8,128)(2,1)S(1)}, bf16[1,128,32,128]{3,2,1,0:T(8,128)(2,1)}, u32[]{:S(2)}) copy-start(bf16[1,128,32,128]{3,2,1,0:T(8,128)(2,1)} %param.7) | copy-start | bytes 3145732
  2.7 7.9 %copy-start.2 = (bf16[1,128,32,128]{3,2,1,0:T(8,128)(2,1)S(1)}, bf16[1,128,32,128]{3,2,1,0:T(8,128)(2,1)}, u32[]{:S(2)}) copy-start(bf16[1,128,32,128]{3,2,1,0:T(8,128)(2,1)} %param.8) | copy-start | bytes 3145732
  2.7 19.0 %copy-start.4 = (bf16[9,128,128]{2,1,0:T(8,128)(2,1)S(1)}, bf16[9,128,128]{2,1,0:T(8,128)(2,1)}, u32[]{:S(2)}) copy-start(bf16[9,128,128]{2,1,0:T(8,128)(2,1)} %refs_0_.1) | copy-start | bytes 884740
  5.2 12.2 %all-to-all-start = ((f32[8,40,128]{2,1,0:T(8,128)}), f32[8,40,128]{2,1,0:T(8,128)S(1)}, u32[]{:S(2)}, u32[]{:S(2)}) async-start(f32[8,40,128]{2,1,0:T(8,128)} %get-tuple-element.51), calls=%async_computation | async-start | bytes 327680 | tf_op jit(solution)/shard_map/all_to_all | solution.py:401
  11.6 14.5 %collective-permute-start.3 = (bf16[128,2048]{1,0:T(8,128)(2,1)}, bf16[128,2048]{1,0:T(8,128)(2,1)}, u32[]{:S(2)}, u32[]{:S(2)}) collective-permute-start(bf16[128,2048]{1,0:T(8,128)(2,1)} %get-tuple-element.61.grad_ref), channel_id=1, source_target_pairs={{8,16},{16,8},{24,32},{32,24},{40,48},{48,40},{56,64},{64,56},{72,... | collective-permute-start | bytes 1572872 | tf_op jit(solution)/shard_map/ppermute | solution.py:387
  17.4 8.7 %collective-permute-start.2 = (bf16[128,2048]{1,0:T(8,128)(2,1)}, bf16[128,2048]{1,0:T(8,128)(2,1)S(1)}, u32[]{:S(2)}, u32[]{:S(2)}) collective-permute-start(bf16[128,2048]{1,0:T(8,128)(2,1)} %get-tuple-element.61.grad_ref), channel_id=1, source_target_pairs={{0,8},{8,0},{16,24},{24,16},{32,40},{40,32},{48,56},{56,48},{64,72... | collective-permute-start | bytes 1572872 | tf_op jit(solution)/shard_map/ppermute | solution.py:388
  17.4 11.9 %collective-permute-start = (bf16[128,2048]{1,0:T(8,128)(2,1)S(1)}, bf16[128,2048]{1,0:T(8,128)(2,1)S(1)}, u32[]{:S(2)}, u32[]{:S(2)}) collective-permute-start(bf16[128,2048]{1,0:T(8,128)(2,1)S(1)} %get-tuple-element.60.grad_ref), channel_id=1, source_target_pairs={{0,8},{8,0},{16,24},{24,16},{32,40},{40,32},{48,56},{56,48},{64,72... | collective-permute-start | bytes 1572872 | tf_op jit(solution)/shard_map/ppermute | solution.py:388
  17.9 13.0 %collective-permute-start.1 = (bf16[128,2048]{1,0:T(8,128)(2,1)S(1)}, bf16[128,2048]{1,0:T(8,128)(2,1)S(1)}, u32[]{:S(2)}, u32[]{:S(2)}) collective-permute-start(bf16[128,2048]{1,0:T(8,128)(2,1)S(1)} %get-tuple-element.60.grad_ref), channel_id=1, source_target_pairs={{8,16},{16,8},{24,32},{32,24},{40,48},{48,40},{56,64},{64,56},{72,... | collective-permute-start | bytes 1572872 | tf_op jit(solution)/shard_map/ppermute | solution.py:387
  33.5 11.1 %collective-permute-start.4 = (f32[4,192,128]{2,1,0:T(8,128)S(1)}, f32[4,192,128]{2,1,0:T(8,128)S(1)}, u32[]{:S(2)}, u32[]{:S(2)}) collective-permute-start(f32[4,192,128]{2,1,0:T(8,128)S(1)} %get-tuple-element.66), channel_id=1, source_target_pairs={{0,8},{8,0},{16,24},{24,16},{32,40},{40,32},{48,56},{56,48},{64,72... | collective-permute-start | bytes 1179656 | tf_op jit(solution)/shard_map/ppermute | solution.py:388
  42.9 3.9 %collective-permute-start.5 = (f32[64,128]{1,0:T(8,128)S(1)}, f32[64,128]{1,0:T(8,128)S(1)}, u32[]{:S(2)}, u32[]{:S(2)}) collective-permute-start(f32[64,128]{1,0:T(8,128)S(1)} %get-tuple-element.67), channel_id=1, source_target_pairs={{0,1},{1,0},{2,3},{3,2},{4,5},{5,4},{6,7},{7,6},{8,9},{9,8},{10,11... | collective-permute-start | bytes 98312 | tf_op jit(solution)/shard_map/ppermute | solution.py:391
  46.8 10.8 %collective-permute-start.9 = (bf16[128,4096]{1,0:T(8,128)(2,1)S(1)}, bf16[128,4096]{1,0:T(8,128)(2,1)S(1)}, u32[]{:S(2)}, u32[]{:S(2)}) collective-permute-start(bf16[128,4096]{1,0:T(8,128)(2,1)S(1)} %get-tuple-element.85.hidden_ref), channel_id=1, source_target_pairs={{0,8},{8,0},{16,24},{24,16},{32,40},{40,32},{48,56},{56,48},{64,72... | collective-permute-start | bytes 3145736 | tf_op jit(solution)/shard_map/ppermute | solution.py:388
  46.8 10.5 %collective-permute-start.6 = (f32[224,128]{1,0:T(8,128)S(1)}, f32[224,128]{1,0:T(8,128)S(1)}, u32[]{:S(2)}, u32[]{:S(2)}) collective-permute-start(f32[224,128]{1,0:T(8,128)S(1)} %get-tuple-element.95), channel_id=1, source_target_pairs={{0,2},{1,3},{2,0},{3,1},{4,6},{5,7},{6,4},{7,5},{8,10},{9,11},{10,... | collective-permute-start | bytes 344072 | tf_op jit(solution)/shard_map/ppermute | solution.py:391
  48.9 8.6 %collective-permute-start.8 = (f32[224,128]{1,0:T(8,128)S(1)}, f32[224,128]{1,0:T(8,128)S(1)}, u32[]{:S(2)}, u32[]{:S(2)}) collective-permute-start(f32[224,128]{1,0:T(8,128)S(1)} %get-tuple-element.96), channel_id=1, source_target_pairs={{0,6},{1,7},{2,4},{3,5},{4,2},{5,3},{6,0},{7,1},{8,14},{9,15},{10,... | collective-permute-start | bytes 344072 | tf_op jit(solution)/shard_map/ppermute | solution.py:391
  51.0 6.3 %collective-permute-start.7 = (f32[192,128]{1,0:T(8,128)S(1)}, f32[192,128]{1,0:T(8,128)S(1)}, u32[]{:S(2)}, u32[]{:S(2)}) collective-permute-start(f32[192,128]{1,0:T(8,128)S(1)} %get-tuple-element.94), channel_id=1, source_target_pairs={{0,4},{1,5},{2,6},{3,7},{4,0},{5,1},{6,2},{7,3},{8,12},{9,13},{10,... | collective-permute-start | bytes 294920 | tf_op jit(solution)/shard_map/ppermute | solution.py:391
  51.6 31.2 %collective-permute-start.15 = (bf16[128,4096]{1,0:T(8,128)(2,1)S(1)}, bf16[128,4096]{1,0:T(8,128)(2,1)S(1)}, u32[]{:S(2)}, u32[]{:S(2)}) collective-permute-start(bf16[128,4096]{1,0:T(8,128)(2,1)S(1)} %get-tuple-element.85.hidden_ref), channel_id=1, source_target_pairs={{8,16},{16,8},{40,48},{48,40},{72,80},{80,72},{104,112},{112,104},... | collective-permute-start | bytes 3145736 | tf_op jit(solution)/shard_map/ppermute | solution.py:440
  57.6 9.5 %collective-permute-start.10 = (f32[192,128]{1,0:T(8,128)S(1)}, f32[192,128]{1,0:T(8,128)S(1)}, u32[]{:S(2)}, u32[]{:S(2)}) collective-permute-start(f32[192,128]{1,0:T(8,128)S(1)} %fusion), channel_id=1, source_target_pairs={{0,32},{1,33},{2,34},{3,35},{4,36},{5,37},{6,38},{7,39},{8,40},{9,... | collective-permute-start | bytes 294920 | tf_op jit(solution)/shard_map/ppermute | solution.py:391
  57.9 10.2 %collective-permute-start.11 = (f32[192,128]{1,0:T(8,128)S(1)}, f32[192,128]{1,0:T(8,128)S(1)}, u32[]{:S(2)}, u32[]{:S(2)}) collective-permute-start(f32[192,128]{1,0:T(8,128)S(1)} %fusion), channel_id=1, source_target_pairs={{0,64},{1,65},{2,66},{3,67},{4,68},{5,69},{6,70},{7,71},{8,72},{9,... | collective-permute-start | bytes 294920 | tf_op jit(solution)/shard_map/ppermute | solution.py:391
  61.2 8.8 %collective-permute-start.12 = (f32[192,128]{1,0:T(8,128)S(1)}, f32[192,128]{1,0:T(8,128)S(1)}, u32[]{:S(2)}, u32[]{:S(2)}) collective-permute-start(f32[192,128]{1,0:T(8,128)S(1)} %fusion), channel_id=1, source_target_pairs={{0,96},{1,97},{2,98},{3,99},{4,100},{5,101},{6,102},{7,103},{8,104... | collective-permute-start | bytes 294920 | tf_op jit(solution)/shard_map/ppermute | solution.py:391
  61.7 24.1 %copy-start.1 = (bf16[1,128,32,128]{3,2,1,0:T(8,128)(2,1)S(1)}, bf16[1,128,32,128]{3,2,1,0:T(8,128)(2,1)}, u32[]{:S(2)}) copy-start(bf16[1,128,32,128]{3,2,1,0:T(8,128)(2,1)} %param.7) | copy-start | bytes 3145732
  70.1 8.0 %collective-permute-start.13 = (f32[192,128]{1,0:T(8,128)S(1)}, f32[192,128]{1,0:T(8,128)S(1)}, u32[]{:S(2)}, u32[]{:S(2)}) collective-permute-start(f32[192,128]{1,0:T(8,128)S(1)} %add_add_fusion), channel_id=1, source_target_pairs={{0,224},{1,225},{2,226},{3,227},{4,228},{5,229},{6,230},{7,231},{8... | collective-permute-start | bytes 294920 | tf_op jit(solution)/shard_map/ppermute | solution.py:391
  78.1 4.7 %collective-permute-start.14 = (f32[200,128]{1,0:T(8,128)S(1)}, f32[200,128]{1,0:T(8,128)S(1)}, u32[]{:S(2)}, u32[]{:S(2)}) collective-permute-start(f32[200,128]{1,0:T(8,128)S(1)} %pad_maximum_fusion.2), channel_id=1, source_target_pairs={{0,1},{1,0},{2,3},{3,2},{4,5},{5,4},{6,7},{7,6},{8,9},{9,8},{10,11... | collective-permute-start | bytes 307208 | tf_op jit(solution)/shard_map/ppermute | solution.py:391
  82.8 5.9 %collective-permute-start.16 = (f32[192,128]{1,0:T(8,128)S(1)}, f32[192,128]{1,0:T(8,128)S(1)}, u32[]{:S(2)}, u32[]{:S(2)}) collective-permute-start(f32[192,128]{1,0:T(8,128)S(1)} %slice.34), channel_id=1, source_target_pairs={{0,17},{1,16},{2,19},{3,18},{4,21},{5,20},{6,23},{7,22},{8,25},{9,... | collective-permute-start | bytes 294920 | tf_op jit(solution)/shard_map/ppermute | solution.py:391
  88.8 18.5 %collective-permute-start.24 = (bf16[128,4096]{1,0:T(8,128)(2,1)S(1)}, bf16[128,4096]{1,0:T(8,128)(2,1)S(1)}, u32[]{:S(2)}, u32[]{:S(2)}) collective-permute-start(bf16[128,4096]{1,0:T(8,128)(2,1)S(1)} %get-tuple-element.85.hidden_ref), channel_id=1, source_target_pairs={{24,32},{32,24},{56,64},{64,56},{88,96},{96,88},{120,128},{128,120... | collective-permute-start | bytes 3145736 | tf_op jit(solution)/shard_map/ppermute | solution.py:473
  90.7 4.8 %collective-permute-start.17 = (f32[200,128]{1,0:T(8,128)S(1)}, f32[200,128]{1,0:T(8,128)S(1)}, u32[]{:S(2)}, u32[]{:S(2)}) collective-permute-start(f32[200,128]{1,0:T(8,128)S(1)} %pad_maximum_fusion.3.own_ref.refs_0_), channel_id=1, source_target_pairs={{0,2},{1,3},{2,0},{3,1},{4,6},{5,7},{6,4},{7,5},{8,10},{9,11},{10,... | collective-permute-start | bytes 307208 | tf_op jit(solution)/shard_map/ppermute | solution.py:391
  92.2 6.4 %collective-permute-start.18 = (f32[200,128]{1,0:T(8,128)S(1)}, f32[200,128]{1,0:T(8,128)S(1)}, u32[]{:S(2)}, u32[]{:S(2)}) collective-permute-start(f32[200,128]{1,0:T(8,128)S(1)} %pad_maximum_fusion.3.own_ref.refs_0_), channel_id=1, source_target_pairs={{0,4},{1,5},{2,6},{3,7},{4,0},{5,1},{6,2},{7,3},{8,12},{9,13},{10,... | collective-permute-start | bytes 307208 | tf_op jit(solution)/shard_map/ppermute | solution.py:391
  94.9 5.9 %collective-permute-start.19 = (f32[200,128]{1,0:T(8,128)S(1)}, f32[200,128]{1,0:T(8,128)S(1)}, u32[]{:S(2)}, u32[]{:S(2)}) collective-permute-start(f32[200,128]{1,0:T(8,128)S(1)} %pad_maximum_fusion.3.own_ref.refs_0_), channel_id=1, source_target_pairs={{0,6},{1,7},{2,4},{3,5},{4,2},{5,3},{6,0},{7,1},{8,14},{9,15},{10,... | collective-permute-start | bytes 307208 | tf_op jit(solution)/shard_map/ppermute | solution.py:391
  95.5 11.8 %collective-permute-start.20 = (f32[200,128]{1,0:T(8,128)S(1)}, f32[200,128]{1,0:T(8,128)S(1)}, u32[]{:S(2)}, u32[]{:S(2)}) collective-permute-start(f32[200,128]{1,0:T(8,128)S(1)} %pad_maximum_fusion.3.own_ref.refs_0_), channel_id=1, source_target_pairs={{0,8},{8,0},{16,24},{24,16},{32,40},{40,32},{48,56},{56,48},{64,72... | collective-permute-start | bytes 307208 | tf_op jit(solution)/shard_map/ppermute | solution.py:388
  95.5 11.8 %collective-permute-start.21 = (f32[200,128]{1,0:T(8,128)S(1)}, f32[200,128]{1,0:T(8,128)S(1)}, u32[]{:S(2)}, u32[]{:S(2)}) collective-permute-start(f32[200,128]{1,0:T(8,128)S(1)} %collective-permute-done.17.one_ref.refs_1_), channel_id=1, source_target_pairs={{0,8},{8,0},{16,24},{24,16},{32,40},{40,32},{48,56},{56,48},{64,72... | collective-permute-start | bytes 307208 | tf_op jit(solution)/shard_map/ppermute | solution.py:388
  98.6 8.7 %collective-permute-start.22 = (f32[200,128]{1,0:T(8,128)S(1)}, f32[200,128]{1,0:T(8,128)S(1)}, u32[]{:S(2)}, u32[]{:S(2)}) collective-permute-start(f32[200,128]{1,0:T(8,128)S(1)} %collective-permute-done.18.two_ref.refs_2_), channel_id=1, source_target_pairs={{0,8},{8,0},{16,24},{24,16},{32,40},{40,32},{48,56},{56,48},{64,72... | collective-permute-start | bytes 307208 | tf_op jit(solution)/shard_map/ppermute | solution.py:388
  100.8 6.6 %collective-permute-start.23 = (f32[200,128]{1,0:T(8,128)S(1)}, f32[200,128]{1,0:T(8,128)S(1)}, u32[]{:S(2)}, u32[]{:S(2)}) collective-permute-start(f32[200,128]{1,0:T(8,128)S(1)} %collective-permute-done.19.three_ref.refs_3_), channel_id=1, source_target_pairs={{0,8},{8,0},{16,24},{24,16},{32,40},{40,32},{48,56},{56,48},{64,72... | collective-permute-start | bytes 307208 | tf_op jit(solution)/shard_map/ppermute | solution.py:388

commit v3 on v2

--- a/solution.py
+++ b/solution.py
@@ -189,7 +189,8 @@
 
 def backward_kernel(last, me_ref, act_ref, hidden_ref, slope_ref, grad_ref, mate_ref, cross_ref, *rest):
     if last:
-        weight_ref, early_in, late_in, packed_in, *rest = rest
+        inside_ref, weight_ref, early_in, late_in, packed_in, *rest = rest
+        inside = me_ref[3] == 1
         pre_ref, keep_ref, send_ref, edges_ref, early, late, shifted = rest
     else:
         weight_ref, pre_ref, early, late, packed_ref, shifted = rest
@@ -211,7 +212,10 @@
     packed = jnp.zeros((LANES, channels), F32)
     for n in range(own_rows // each):
         at, whole = span(n * each, each), span(n * each + start, each)
-        grads = jnp.concatenate([ref[:, at] for ref in (grad_ref, mate_ref, cross_ref)], axis=0)
+        across = cross_ref[:, at]
+        if last:
+            across = jnp.where(inside, inside_ref[:, at], across)
+        grads = jnp.concatenate([grad_ref[:, at], mate_ref[:, at], across], axis=0)
         back = jnp.dot(weights, grads, preferred_element_type=F32)
         pre = (back * slope_ref[:, whole]).astype(BF16)
         pre_ref[:, at] = pre
@@ -403,7 +407,7 @@
     crossed = [cross(early_grad)]
     received, early_grad, late_grad = tied((received, early_grad, late_grad))
     grads = [early_grad, late_grad]
-    crossed.append(cross(late_grad))
+    inside_grad = lax.ppermute(late_grad, "frame", crossing(frames, True))
     mates = [mate(v) for v in grads]
 
     padded = (3 * channels, pixels + 2 * cols)
@@ -414,6 +418,8 @@
         cost=(1000, MIB),
         limit=16,
     )
+    slope, late_grad = tied((slope, grads[1]))
+    outside_grad = lax.ppermute(late_grad, "frame", crossing(frames, False))
     early_shape, late_shape = (3 * channels, channels), (3 * channels, 3 * channels)
     shifted = pltpu.VMEM((channels, pixels // 2 + 4 * cols), BF16)
     pre_early, *sums = call(
@@ -429,7 +435,7 @@
     pre_late, keep, send, edges = call(
         functools.partial(backward_kernel, True),
         [(half, BF16), slots, slots, ((2 * rows, channels), F32)],
-        [place, act, hidden, slope, grads[1], mates[1], crossed[1], temporal_weight, *sums],
+        [place, act, hidden, slope, grads[1], mates[1], outside_grad, inside_grad, temporal_weight, *sums],
         [pltpu.VMEM(early_shape, F32), pltpu.VMEM(late_shape, F32), shifted],
         cost=(1000, MIB),
         limit=20,

time: 110 us -> 110 us (level); the launches traced: 110 us -> 108 us
  starting transfers between devices: 50.1 us -> 43.1 us
  waiting for transfers between devices: 31.1 us -> 36.7 us
    ppermute x0 -> x2, waiting for transfers between devices: none -> 7.84 us  [the longest x1 7.83 us: body(): outside_grad = lax.ppermute(late_grad, 'frame', crossing(frames, False))]
    ppermute x8, starting transfers between devices: 10.4 us -> 5.36 us  [body(): mate = lambda v: lax.ppermute(v, 'frame', partner(1, frames))]
    ppermute x2 -> x1, starting transfers between devices: 7.11 us -> 3.33 us  [body(): cross = lambda v: lax.ppermute(v, 'frame', neighbour(frames))]
    ppermute x0 -> x2, starting transfers between devices: none -> 2.6 us  [the longest x1 1.92 us: body(): outside_grad = lax.ppermute(late_grad, 'frame', crossing(frames, False))]
    ppermute x2 -> x1, waiting for transfers between devices: 1.61 us -> 0.01 us  [body(): cross = lambda v: lax.ppermute(v, 'frame', neighbour(frames))]
    ppermute x13, waiting for transfers between devices: 22.9 us -> 21.6 us  [meet(): lax.ppermute(v, ('frame', 'chan'), both(frame_bits, chan_bits, frames, pe...]
  transfers between devices with their start and end apart: 26 -> 27, of which waited for: 13 -> 13; matrix products, arithmetic and copies ran while one was open for 0% -> 0% of each run, Pallas kernels for 16% -> 17%
where the time goes in v3:
time: 110 us; the launch traced here: 108 us
  starting transfers between devices  43.1 us (39%)
  waiting for transfers between devices  36.7 us (33%)
  Pallas kernels  25.3 us (23%)
  local copies, waits for them, and re-layouts  1.27 us (1%)
    pallas_call x9, Pallas kernels, call(): pl.pallas_call(kernel, out_shape=[jax.ShapeDtypeStruct(s, d) for s, d in...  25.3 us
    ppermute x13, starting transfers between devices, meet(): lax.ppermute(v, ('frame', 'chan'), both(frame_bits, chan_bits, frames, pe...  23.8 us
    ppermute x13, waiting for transfers between devices, meet(): lax.ppermute(v, ('frame', 'chan'), both(frame_bits, chan_bits, frames, pe...  21.6 us
    ppermute x1, waiting for transfers between devices, body(): outside_grad = lax.ppermute(late_grad, 'frame', crossing(frames, False))  7.83 us
    all_to_all x1, starting transfers between devices, body(): received = lax.all_to_all(payload, 'chan', 0, 0, tiled=True)  5.4 us
    ppermute x8, starting transfers between devices, body(): mate = lambda v: lax.ppermute(v, 'frame', partner(1, frames))  5.36 us
    ppermute x1, waiting for transfers between devices, body(): hidden_outside = lax.ppermute(hidden, 'frame', crossing(frames, False))  4.7 us
    ppermute x1, starting transfers between devices, body(): cross = lambda v: lax.ppermute(v, 'frame', neighbour(frames))  3.33 us
  transfers between devices with their start and end apart: 27, of which 13 were waited for; matrix products, arithmetic and copies ran while one was open for 0% of the time, Pallas kernels for 17%

profile of v3, /device:TPU:32, one launch (start us, length us, event | category | flops | bytes accessed | tf_op | source)
XLA Modules:
  0.0 108.4 jit_solution(17185409662140383802)
XLA Ops:
  2.7 2.5 %shard_map.102 = (bf16[128,4096]{1,0:T(8,128)(2,1)S(1)}, f32[8,40,128]{2,1,0:T(8,128)}) custom-call(s32[4]{0:T(128)S(1)} %pad_add_fusion.me_ref, bf16[128,32,128]{2,1,0:T(8,128)(2,1)S(1)} %bitcast.21), custom_call_target="tpu_custom_call" | custom-call | bytes 2097152 | tf_op jit(solution)/shard_map/pallas_call | solution.py:44
  5.2 5.4 %all-to-all-start = ((f32[8,40,128]{2,1,0:T(8,128)}), f32[8,40,128]{2,1,0:T(8,128)S(1)}, u32[]{:S(2)}, u32[]{:S(2)}) async-start(f32[8,40,128]{2,1,0:T(8,128)} %get-tuple-element.53), calls=%async_computation | async-start | bytes 327680 | tf_op jit(solution)/shard_map/all_to_all | solution.py:405
  11.6 3.3 %collective-permute-start.4 = (bf16[128,2048]{1,0:T(8,128)(2,1)}, bf16[128,2048]{1,0:T(8,128)(2,1)}, u32[]{:S(2)}, u32[]{:S(2)}) collective-permute-start(bf16[128,2048]{1,0:T(8,128)(2,1)} %get-tuple-element.65.grad_ref), channel_id=1, source_target_pairs={{8,16},{16,8},{24,32},{32,24},{40,48},{48,40},{56,64},{64,56},{72,... | collective-permute-start | bytes 1572872 | tf_op jit(solution)/shard_map/ppermute | solution.py:391
  14.9 2.5 %all-to-all-done.received_ref = f32[8,40,128]{2,1,0:T(8,128)S(1)} async-done(((f32[8,40,128]{2,1,0:T(8,128)}), f32[8,40,128]{2,1,0:T(8,128)S(1)}, u32[]{:S(2)}, u32[]{:S(2)}) %all-to-all-start) | async-done | bytes 163872 | tf_op jit(solution)/shard_map/all_to_all | solution.py:405
  18.1 4.1 %collective-permute-start = (bf16[128,2048]{1,0:T(8,128)(2,1)S(1)}, bf16[128,2048]{1,0:T(8,128)(2,1)S(1)}, u32[]{:S(2)}, u32[]{:S(2)}) collective-permute-start(bf16[128,2048]{1,0:T(8,128)(2,1)S(1)} %get-tuple-element.64.grad_ref), channel_id=1, source_target_pairs={{0,8},{8,0},{16,24},{24,16},{32,40},{40,32},{48,56},{56,48},{64,72... | collective-permute-start | bytes 1572872 | tf_op jit(solution)/shard_map/ppermute | solution.py:392
  22.4 4.3 %shard_map.104 = (bf16[384,4352]{1,0:T(8,128)(2,1)S(1)}, bf16[128,4096]{1,0:T(8,128)(2,1)S(1)}, f32[128,4096]{1,0:T(8,128)S(1)}, f32[128,128]{1,0:T(8,128)S(1)}) custom-call(s32[4]{0:T(128)S(1)} %pad_add_fusion.me_ref, bf16[128,4096]{1,0:T(8,128)(2,1)S(1)} %get-tuple-element.51.plane_ref.refs_1_, f32[8,40,128]{2,1,0:T(8,128)S(1)} %all-to-all-done.received_ref, ...), custom_call_target="tpu_custom_call" | custom-call | flops 1000 | bytes 1048576 | tf_op jit(solution)/shard_map/pallas_call | solution.py:44
  26.7 1.9 %collective-permute-start.1 = (bf16[128,2048]{1,0:T(8,128)(2,1)S(1)}, bf16[128,2048]{1,0:T(8,128)(2,1)S(1)}, u32[]{:S(2)}, u32[]{:S(2)}) collective-permute-start(bf16[128,2048]{1,0:T(8,128)(2,1)S(1)} %get-tuple-element.64.grad_ref), channel_id=1, source_target_pairs={{24,32},{32,24},{56,64},{64,56},{88,96},{96,88},{120,128},{128,120... | collective-permute-start | bytes 1572872 | tf_op jit(solution)/shard_map/ppermute | solution.py:422
  28.7 3.2 %shard_map.105 = (bf16[128,2048]{1,0:T(8,128)(2,1)S(1)}, f32[384,128]{1,0:T(8,128)S(1)}, f32[384,384]{1,0:T(8,128)S(1)}, f32[128,128]{1,0:T(8,128)S(1)}) custom-call(s32[4]{0:T(128)S(1)} %pad_add_fusion.me_ref, bf16[384,4352]{1,0:T(8,128)(2,1)S(1)} %get-tuple-element.59.act_ref, bf16[128,4096]{1,0:T(8,128)(2,1)S(1)} %get-tuple-element.89.hidden_ref, ...), custom_call_target="tpu_custom_call" | custom-call | flops 1000 | bytes 1048576 | tf_op jit(solution)/shard_map/pallas_call | solution.py:44
  31.9 7.8 %collective-permute-done.1.cross_ref = bf16[128,2048]{1,0:T(8,128)(2,1)S(1)} collective-permute-done((bf16[128,2048]{1,0:T(8,128)(2,1)S(1)}, bf16[128,2048]{1,0:T(8,128)(2,1)S(1)}, u32[]{:S(2)}, u32[]{:S(2)}) %collective-permute-start.1) | collective-permute-done | bytes 524320 | tf_op jit(solution)/shard_map/ppermute | solution.py:422
  39.7 2.6 %shard_map.106 = (bf16[128,2048]{1,0:T(8,128)(2,1)S(1)}, f32[4,192,128]{2,1,0:T(8,128)S(1)}, f32[4,192,128]{2,1,0:T(8,128)S(1)}, f32[64,128]{1,0:T(8,128)S(1)}) custom-call(s32[4]{0:T(128)S(1)} %pad_add_fusion.me_ref, bf16[384,4352]{1,0:T(8,128)(2,1)S(1)} %get-tuple-element.59.act_ref, bf16[128,4096]{1,0:T(8,128)(2,1)S(1)} %get-tuple-element.89.hidden_ref, ...), custom_call_target="tpu_custom_call" | custom-call | flops 1000 | bytes 1048576 | tf_op jit(solution)/shard_map/pallas_call | solution.py:44
  42.9 1.7 %collective-permute-start.6 = (f32[64,128]{1,0:T(8,128)S(1)}, f32[64,128]{1,0:T(8,128)S(1)}, u32[]{:S(2)}, u32[]{:S(2)}) collective-permute-start(f32[64,128]{1,0:T(8,128)S(1)} %get-tuple-element.71), channel_id=1, source_target_pairs={{0,1},{1,0},{2,3},{3,2},{4,5},{5,4},{6,7},{7,6},{8,9},{9,8},{10,11... | collective-permute-start | bytes 98312 | tf_op jit(solution)/shard_map/ppermute | solution.py:395
  44.6 2.2 %collective-permute-done.6.near_ref = f32[64,128]{1,0:T(8,128)S(1)} collective-permute-done((f32[64,128]{1,0:T(8,128)S(1)}, f32[64,128]{1,0:T(8,128)S(1)}, u32[]{:S(2)}, u32[]{:S(2)}) %collective-permute-start.6) | collective-permute-done | bytes 32800 | tf_op jit(solution)/shard_map/ppermute | solution.py:395
  46.8 2.1 %collective-permute-start.7 = (f32[224,128]{1,0:T(8,128)S(1)}, f32[224,128]{1,0:T(8,128)S(1)}, u32[]{:S(2)}, u32[]{:S(2)}) collective-permute-start(f32[224,128]{1,0:T(8,128)S(1)} %get-tuple-element.99), channel_id=1, source_target_pairs={{0,2},{1,3},{2,0},{3,1},{4,6},{5,7},{6,4},{7,5},{8,10},{9,11},{10,... | collective-permute-start | bytes 344072 | tf_op jit(solution)/shard_map/ppermute | solution.py:395
  49.0 2.1 %collective-permute-start.9 = (f32[224,128]{1,0:T(8,128)S(1)}, f32[224,128]{1,0:T(8,128)S(1)}, u32[]{:S(2)}, u32[]{:S(2)}) collective-permute-start(f32[224,128]{1,0:T(8,128)S(1)} %get-tuple-element.100), channel_id=1, source_target_pairs={{0,6},{1,7},{2,4},{3,5},{4,2},{5,3},{6,0},{7,1},{8,14},{9,15},{10,... | collective-permute-start | bytes 344072 | tf_op jit(solution)/shard_map/ppermute | solution.py:395
  52.4 5.0 %collective-permute-done.8 = f32[192,128]{1,0:T(8,128)S(1)} collective-permute-done((f32[192,128]{1,0:T(8,128)S(1)}, f32[192,128]{1,0:T(8,128)S(1)}, u32[]{:S(2)}, u32[]{:S(2)}) %collective-permute-start.8) | collective-permute-done | bytes 98336 | tf_op jit(solution)/shard_map/ppermute | solution.py:395
  57.6 2.2 %collective-permute-start.13 = (f32[192,128]{1,0:T(8,128)S(1)}, f32[192,128]{1,0:T(8,128)S(1)}, u32[]{:S(2)}, u32[]{:S(2)}) collective-permute-start(f32[192,128]{1,0:T(8,128)S(1)} %fusion), channel_id=1, source_target_pairs={{0,96},{1,97},{2,98},{3,99},{4,100},{5,101},{6,102},{7,103},{8,104... | collective-permute-start | bytes 294920 | tf_op jit(solution)/shard_map/ppermute | solution.py:395
  59.8 1.5 %collective-permute-start.12 = (f32[192,128]{1,0:T(8,128)S(1)}, f32[192,128]{1,0:T(8,128)S(1)}, u32[]{:S(2)}, u32[]{:S(2)}) collective-permute-start(f32[192,128]{1,0:T(8,128)S(1)} %fusion), channel_id=1, source_target_pairs={{0,64},{1,65},{2,66},{3,67},{4,68},{5,69},{6,70},{7,71},{8,72},{9,... | collective-permute-start | bytes 294920 | tf_op jit(solution)/shard_map/ppermute | solution.py:395
  61.2 1.4 %collective-permute-start.11 = (f32[192,128]{1,0:T(8,128)S(1)}, f32[192,128]{1,0:T(8,128)S(1)}, u32[]{:S(2)}, u32[]{:S(2)}) collective-permute-start(f32[192,128]{1,0:T(8,128)S(1)} %fusion), channel_id=1, source_target_pairs={{0,32},{1,33},{2,34},{3,35},{4,36},{5,37},{6,38},{7,39},{8,40},{9,... | collective-permute-start | bytes 294920 | tf_op jit(solution)/shard_map/ppermute | solution.py:395
  62.6 5.3 %shard_map.107 = (f32[128,4096]{1,0:T(8,128)S(1)}, f32[8,128]{1,0:T(8,128)S(1)}) custom-call(s32[4]{0:T(128)S(1)} %pad_add_fusion.me_ref, bf16[128,2048]{1,0:T(8,128)(2,1)S(1)} %get-tuple-element.76.early_ref, bf16[128,2048]{1,0:T(8,128)(2,1)S(1)} %get-tuple-element.77.late_ref, f32[64,128]{1,0:T(8,128)S(1)} %collective-permute-done.6.near_ref, ...), custom_call_target="tpu_custom_call" | custom-call | flops 1000 | bytes 1048576 | tf_op jit(solution)/shard_map/pallas_call | solution.py:44
  68.9 4.2 %collective-permute-start.14 = (f32[192,128]{1,0:T(8,128)S(1)}, f32[192,128]{1,0:T(8,128)S(1)}, u32[]{:S(2)}, u32[]{:S(2)}) collective-permute-start(f32[192,128]{1,0:T(8,128)S(1)} %add_add_fusion), channel_id=1, source_target_pairs={{0,224},{1,225},{2,226},{3,227},{4,228},{5,229},{6,230},{7,231},{8... | collective-permute-start | bytes 294920 | tf_op jit(solution)/shard_map/ppermute | solution.py:395
  73.1 3.5 %collective-permute-done.14 = f32[192,128]{1,0:T(8,128)S(1)} collective-permute-done((f32[192,128]{1,0:T(8,128)S(1)}, f32[192,128]{1,0:T(8,128)S(1)}, u32[]{:S(2)}, u32[]{:S(2)}) %collective-permute-start.14) | collective-permute-done | bytes 98336 | tf_op jit(solution)/shard_map/ppermute | solution.py:395
  77.7 3.8 %collective-permute-done.15 = f32[200,128]{1,0:T(8,128)S(1)} collective-permute-done((f32[200,128]{1,0:T(8,128)S(1)}, f32[200,128]{1,0:T(8,128)S(1)}, u32[]{:S(2)}, u32[]{:S(2)}) %collective-permute-start.15) | collective-permute-done | bytes 102432 | tf_op jit(solution)/shard_map/ppermute | solution.py:395
  81.5 3.0 %collective-permute-start.17 = (f32[192,128]{1,0:T(8,128)S(1)}, f32[192,128]{1,0:T(8,128)S(1)}, u32[]{:S(2)}, u32[]{:S(2)}) collective-permute-start(f32[192,128]{1,0:T(8,128)S(1)} %slice.34), channel_id=1, source_target_pairs={{0,17},{1,16},{2,19},{3,18},{4,21},{5,20},{6,23},{7,22},{8,25},{9,... | collective-permute-start | bytes 294920 | tf_op jit(solution)/shard_map/ppermute | solution.py:395
  84.5 1.7 %shard_map.108.refs_8_ = f32[128,32,128]{2,1,0:T(8,128)S(1)} custom-call(s32[4]{0:T(128)S(1)} %pad_add_fusion.me_ref, bf16[128,4096]{1,0:T(8,128)(2,1)S(1)} %get-tuple-element.89.hidden_ref, bf16[128,4096]{1,0:T(8,128)(2,1)S(1)} %collective-permute-done.10.mate_ref, bf16[128,4096]{1,0:T(8,128)(2,1)S(1)} %collective-permute-done.16.inside_ref, ...), custom_call_target="tpu_custom_call" | custom-call | flops 1 | bytes 1 | tf_op jit(solution)/shard_map/pallas_call | solution.py:44
  86.1 1.3 %collective-permute-done.17 = f32[192,128]{1,0:T(8,128)S(1)} collective-permute-done((f32[192,128]{1,0:T(8,128)S(1)}, f32[192,128]{1,0:T(8,128)S(1)}, u32[]{:S(2)}, u32[]{:S(2)}) %collective-permute-start.17) | collective-permute-done | bytes 98336 | tf_op jit(solution)/shard_map/ppermute | solution.py:395
  87.4 1.9 %collective-permute-start.25 = (bf16[128,4096]{1,0:T(8,128)(2,1)S(1)}, bf16[128,4096]{1,0:T(8,128)(2,1)S(1)}, u32[]{:S(2)}, u32[]{:S(2)}) collective-permute-start(bf16[128,4096]{1,0:T(8,128)(2,1)S(1)} %get-tuple-element.89.hidden_ref), channel_id=1, source_target_pairs={{24,32},{32,24},{56,64},{64,56},{88,96},{96,88},{120,128},{128,120... | collective-permute-start | bytes 3145736 | tf_op jit(solution)/shard_map/ppermute | solution.py:479
  89.4 2.7 %collective-permute-start.20 = (f32[200,128]{1,0:T(8,128)S(1)}, f32[200,128]{1,0:T(8,128)S(1)}, u32[]{:S(2)}, u32[]{:S(2)}) collective-permute-start(f32[200,128]{1,0:T(8,128)S(1)} %pad_maximum_fusion.3.own_ref.refs_0_), channel_id=1, source_target_pairs={{0,6},{1,7},{2,4},{3,5},{4,2},{5,3},{6,0},{7,1},{8,14},{9,15},{10,... | collective-permute-start | bytes 307208 | tf_op jit(solution)/shard_map/ppermute | solution.py:395
  93.6 1.8 %collective-permute-done.20.three_ref.refs_3_ = f32[200,128]{1,0:T(8,128)S(1)} collective-permute-done((f32[200,128]{1,0:T(8,128)S(1)}, f32[200,128]{1,0:T(8,128)S(1)}, u32[]{:S(2)}, u32[]{:S(2)}) %collective-permute-start.20) | collective-permute-done | bytes 102432 | tf_op jit(solution)/shard_map/ppermute | solution.py:395
  95.3 2.9 %collective-permute-done.19.two_ref.refs_2_ = f32[200,128]{1,0:T(8,128)S(1)} collective-permute-done((f32[200,128]{1,0:T(8,128)S(1)}, f32[200,128]{1,0:T(8,128)S(1)}, u32[]{:S(2)}, u32[]{:S(2)}) %collective-permute-start.19) | collective-permute-done | bytes 102432 | tf_op jit(solution)/shard_map/ppermute | solution.py:395
  98.8 2.5 %shard_map.109 = bf16[128,32,128]{2,1,0:T(8,128)(2,1)} custom-call(f32[200,128]{1,0:T(8,128)S(1)} %pad_maximum_fusion.3.own_ref.refs_0_, f32[200,128]{1,0:T(8,128)S(1)} %collective-permute-done.18.one_ref.refs_1_, f32[200,128]{1,0:T(8,128)S(1)} %collective-permute-done.19.two_ref.refs_2_, f32[200,128]{1,0:T(8,128)S(1)} %collective-permute-done.20.three_ref.refs_3_, ...), custom_call_target="tpu_custom_call" | custom-call | flops 1000 | bytes 1048576 | tf_op jit(solution)/shard_map/pallas_call | solution.py:44
  101.3 4.7 %collective-permute-done.25.refs_9_ = bf16[128,4096]{1,0:T(8,128)(2,1)S(1)} collective-permute-done((bf16[128,4096]{1,0:T(8,128)(2,1)S(1)}, bf16[128,4096]{1,0:T(8,128)(2,1)S(1)}, u32[]{:S(2)}, u32[]{:S(2)}) %collective-permute-start.25) | collective-permute-done | bytes 1048608 | tf_op jit(solution)/shard_map/ppermute | solution.py:479
  106.0 2.3 %shard_map.110 = (f32[6,192,128]{2,1,0:T(8,128)}, f32[2,192,128]{2,1,0:T(8,128)}, bf16[128,32,128]{2,1,0:T(8,128)(2,1)}) custom-call(s32[4]{0:T(128)S(1)} %pad_add_fusion.me_ref, f32[200,128]{1,0:T(8,128)S(1)} %pad_maximum_fusion.3.own_ref.refs_0_, f32[200,128]{1,0:T(8,128)S(1)} %collective-permute-done.18.one_ref.refs_1_, ...), custom_call_target="tpu_custom_call" | custom-call | flops 1000 | bytes 1048576 | tf_op jit(solution)/shard_map/pallas_call | solution.py:44
  (56 shorter events, 10.0 us)
Async XLA Ops:
  0.6 28.0 %copy-start.3 = (bf16[3,128,128]{2,1,0:T(8,128)(2,1)S(1)}, bf16[3,128,128]{2,1,0:T(8,128)(2,1)}, u32[]{:S(2)}) copy-start(bf16[3,128,128]{2,1,0:T(8,128)(2,1)} %refs_10_.1) | copy-start | bytes 294916
  1.5 1.2 %copy-start = (bf16[1,128,32,128]{3,2,1,0:T(8,128)(2,1)S(1)}, bf16[1,128,32,128]{3,2,1,0:T(8,128)(2,1)}, u32[]{:S(2)}) copy-start(bf16[1,128,32,128]{3,2,1,0:T(8,128)(2,1)} %param.7) | copy-start | bytes 3145732
  2.7 7.9 %copy-start.2 = (bf16[1,128,32,128]{3,2,1,0:T(8,128)(2,1)S(1)}, bf16[1,128,32,128]{3,2,1,0:T(8,128)(2,1)}, u32[]{:S(2)}) copy-start(bf16[1,128,32,128]{3,2,1,0:T(8,128)(2,1)} %param.8) | copy-start | bytes 3145732
  2.7 19.7 %copy-start.4 = (bf16[9,128,128]{2,1,0:T(8,128)(2,1)S(1)}, bf16[9,128,128]{2,1,0:T(8,128)(2,1)}, u32[]{:S(2)}) copy-start(bf16[9,128,128]{2,1,0:T(8,128)(2,1)} %refs_0_.1) | copy-start | bytes 884740
  5.2 12.2 %all-to-all-start = ((f32[8,40,128]{2,1,0:T(8,128)}), f32[8,40,128]{2,1,0:T(8,128)S(1)}, u32[]{:S(2)}, u32[]{:S(2)}) async-start(f32[8,40,128]{2,1,0:T(8,128)} %get-tuple-element.53), calls=%async_computation | async-start | bytes 327680 | tf_op jit(solution)/shard_map/all_to_all | solution.py:405
  11.6 17.1 %collective-permute-start.4 = (bf16[128,2048]{1,0:T(8,128)(2,1)}, bf16[128,2048]{1,0:T(8,128)(2,1)}, u32[]{:S(2)}, u32[]{:S(2)}) collective-permute-start(bf16[128,2048]{1,0:T(8,128)(2,1)} %get-tuple-element.65.grad_ref), channel_id=1, source_target_pairs={{8,16},{16,8},{24,32},{32,24},{40,48},{48,40},{56,64},{64,56},{72,... | collective-permute-start | bytes 1572872 | tf_op jit(solution)/shard_map/ppermute | solution.py:391
  17.4 14.4 %collective-permute-start.2 = (bf16[128,2048]{1,0:T(8,128)(2,1)S(1)}, bf16[128,2048]{1,0:T(8,128)(2,1)S(1)}, u32[]{:S(2)}, u32[]{:S(2)}) collective-permute-start(bf16[128,2048]{1,0:T(8,128)(2,1)S(1)} %get-tuple-element.64.grad_ref), channel_id=1, source_target_pairs={{8,16},{16,8},{40,48},{48,40},{72,80},{80,72},{104,112},{112,104},... | collective-permute-start | bytes 1572872 | tf_op jit(solution)/shard_map/ppermute | solution.py:410
  18.1 13.8 %collective-permute-start = (bf16[128,2048]{1,0:T(8,128)(2,1)S(1)}, bf16[128,2048]{1,0:T(8,128)(2,1)S(1)}, u32[]{:S(2)}, u32[]{:S(2)}) collective-permute-start(bf16[128,2048]{1,0:T(8,128)(2,1)S(1)} %get-tuple-element.64.grad_ref), channel_id=1, source_target_pairs={{0,8},{8,0},{16,24},{24,16},{32,40},{40,32},{48,56},{56,48},{64,72... | collective-permute-start | bytes 1572872 | tf_op jit(solution)/shard_map/ppermute | solution.py:392
  22.3 6.4 %collective-permute-start.3 = (bf16[128,2048]{1,0:T(8,128)(2,1)}, bf16[128,2048]{1,0:T(8,128)(2,1)S(1)}, u32[]{:S(2)}, u32[]{:S(2)}) collective-permute-start(bf16[128,2048]{1,0:T(8,128)(2,1)} %get-tuple-element.65.grad_ref), channel_id=1, source_target_pairs={{0,8},{8,0},{16,24},{24,16},{32,40},{40,32},{48,56},{56,48},{64,72... | collective-permute-start | bytes 1572872 | tf_op jit(solution)/shard_map/ppermute | solution.py:392
  26.7 13.0 %collective-permute-start.1 = (bf16[128,2048]{1,0:T(8,128)(2,1)S(1)}, bf16[128,2048]{1,0:T(8,128)(2,1)S(1)}, u32[]{:S(2)}, u32[]{:S(2)}) collective-permute-start(bf16[128,2048]{1,0:T(8,128)(2,1)S(1)} %get-tuple-element.64.grad_ref), channel_id=1, source_target_pairs={{24,32},{32,24},{56,64},{64,56},{88,96},{96,88},{120,128},{128,120... | collective-permute-start | bytes 1572872 | tf_op jit(solution)/shard_map/ppermute | solution.py:422
  42.3 2.3 %collective-permute-start.5 = (f32[4,192,128]{2,1,0:T(8,128)S(1)}, f32[4,192,128]{2,1,0:T(8,128)S(1)}, u32[]{:S(2)}, u32[]{:S(2)}) collective-permute-start(f32[4,192,128]{2,1,0:T(8,128)S(1)} %get-tuple-element.70), channel_id=1, source_target_pairs={{0,8},{8,0},{16,24},{24,16},{32,40},{40,32},{48,56},{56,48},{64,72... | collective-permute-start | bytes 1179656 | tf_op jit(solution)/shard_map/ppermute | solution.py:392
  42.9 3.9 %collective-permute-start.6 = (f32[64,128]{1,0:T(8,128)S(1)}, f32[64,128]{1,0:T(8,128)S(1)}, u32[]{:S(2)}, u32[]{:S(2)}) collective-permute-start(f32[64,128]{1,0:T(8,128)S(1)} %get-tuple-element.71), channel_id=1, source_target_pairs={{0,1},{1,0},{2,3},{3,2},{4,5},{5,4},{6,7},{7,6},{8,9},{9,8},{10,11... | collective-permute-start | bytes 98312 | tf_op jit(solution)/shard_map/ppermute | solution.py:395
  46.8 10.8 %collective-permute-start.10 = (bf16[128,4096]{1,0:T(8,128)(2,1)S(1)}, bf16[128,4096]{1,0:T(8,128)(2,1)S(1)}, u32[]{:S(2)}, u32[]{:S(2)}) collective-permute-start(bf16[128,4096]{1,0:T(8,128)(2,1)S(1)} %get-tuple-element.89.hidden_ref), channel_id=1, source_target_pairs={{0,8},{8,0},{16,24},{24,16},{32,40},{40,32},{48,56},{56,48},{64,72... | collective-permute-start | bytes 3145736 | tf_op jit(solution)/shard_map/ppermute | solution.py:392
  46.8 10.5 %collective-permute-start.7 = (f32[224,128]{1,0:T(8,128)S(1)}, f32[224,128]{1,0:T(8,128)S(1)}, u32[]{:S(2)}, u32[]{:S(2)}) collective-permute-start(f32[224,128]{1,0:T(8,128)S(1)} %get-tuple-element.99), channel_id=1, source_target_pairs={{0,2},{1,3},{2,0},{3,1},{4,6},{5,7},{6,4},{7,5},{8,10},{9,11},{10,... | collective-permute-start | bytes 344072 | tf_op jit(solution)/shard_map/ppermute | solution.py:395
  49.0 8.6 %collective-permute-start.9 = (f32[224,128]{1,0:T(8,128)S(1)}, f32[224,128]{1,0:T(8,128)S(1)}, u32[]{:S(2)}, u32[]{:S(2)}) collective-permute-start(f32[224,128]{1,0:T(8,128)S(1)} %get-tuple-element.100), channel_id=1, source_target_pairs={{0,6},{1,7},{2,4},{3,5},{4,2},{5,3},{6,0},{7,1},{8,14},{9,15},{10,... | collective-permute-start | bytes 344072 | tf_op jit(solution)/shard_map/ppermute | solution.py:395
  51.0 6.4 %collective-permute-start.8 = (f32[192,128]{1,0:T(8,128)S(1)}, f32[192,128]{1,0:T(8,128)S(1)}, u32[]{:S(2)}, u32[]{:S(2)}) collective-permute-start(f32[192,128]{1,0:T(8,128)S(1)} %get-tuple-element.98), channel_id=1, source_target_pairs={{0,4},{1,5},{2,6},{3,7},{4,0},{5,1},{6,2},{7,3},{8,12},{9,13},{10,... | collective-permute-start | bytes 294920 | tf_op jit(solution)/shard_map/ppermute | solution.py:395
  51.6 29.8 %collective-permute-start.16 = (bf16[128,4096]{1,0:T(8,128)(2,1)S(1)}, bf16[128,4096]{1,0:T(8,128)(2,1)S(1)}, u32[]{:S(2)}, u32[]{:S(2)}) collective-permute-start(bf16[128,4096]{1,0:T(8,128)(2,1)S(1)} %get-tuple-element.89.hidden_ref), channel_id=1, source_target_pairs={{8,16},{16,8},{40,48},{48,40},{72,80},{80,72},{104,112},{112,104},... | collective-permute-start | bytes 3145736 | tf_op jit(solution)/shard_map/ppermute | solution.py:446
  57.6 10.3 %collective-permute-start.13 = (f32[192,128]{1,0:T(8,128)S(1)}, f32[192,128]{1,0:T(8,128)S(1)}, u32[]{:S(2)}, u32[]{:S(2)}) collective-permute-start(f32[192,128]{1,0:T(8,128)S(1)} %fusion), channel_id=1, source_target_pairs={{0,96},{1,97},{2,98},{3,99},{4,100},{5,101},{6,102},{7,103},{8,104... | collective-permute-start | bytes 294920 | tf_op jit(solution)/shard_map/ppermute | solution.py:395
  59.8 8.3 %collective-permute-start.12 = (f32[192,128]{1,0:T(8,128)S(1)}, f32[192,128]{1,0:T(8,128)S(1)}, u32[]{:S(2)}, u32[]{:S(2)}) collective-permute-start(f32[192,128]{1,0:T(8,128)S(1)} %fusion), channel_id=1, source_target_pairs={{0,64},{1,65},{2,66},{3,67},{4,68},{5,69},{6,70},{7,71},{8,72},{9,... | collective-permute-start | bytes 294920 | tf_op jit(solution)/shard_map/ppermute | solution.py:395
  61.2 7.7 %collective-permute-start.11 = (f32[192,128]{1,0:T(8,128)S(1)}, f32[192,128]{1,0:T(8,128)S(1)}, u32[]{:S(2)}, u32[]{:S(2)}) collective-permute-start(f32[192,128]{1,0:T(8,128)S(1)} %fusion), channel_id=1, source_target_pairs={{0,32},{1,33},{2,34},{3,35},{4,36},{5,37},{6,38},{7,39},{8,40},{9,... | collective-permute-start | bytes 294920 | tf_op jit(solution)/shard_map/ppermute | solution.py:395
  62.6 21.9 %copy-start.1 = (bf16[1,128,32,128]{3,2,1,0:T(8,128)(2,1)S(1)}, bf16[1,128,32,128]{3,2,1,0:T(8,128)(2,1)}, u32[]{:S(2)}) copy-start(bf16[1,128,32,128]{3,2,1,0:T(8,128)(2,1)} %param.7) | copy-start | bytes 3145732
  68.9 7.8 %collective-permute-start.14 = (f32[192,128]{1,0:T(8,128)S(1)}, f32[192,128]{1,0:T(8,128)S(1)}, u32[]{:S(2)}, u32[]{:S(2)}) collective-permute-start(f32[192,128]{1,0:T(8,128)S(1)} %add_add_fusion), channel_id=1, source_target_pairs={{0,224},{1,225},{2,226},{3,227},{4,228},{5,229},{6,230},{7,231},{8... | collective-permute-start | bytes 294920 | tf_op jit(solution)/shard_map/ppermute | solution.py:395
  76.7 4.7 %collective-permute-start.15 = (f32[200,128]{1,0:T(8,128)S(1)}, f32[200,128]{1,0:T(8,128)S(1)}, u32[]{:S(2)}, u32[]{:S(2)}) collective-permute-start(f32[200,128]{1,0:T(8,128)S(1)} %pad_maximum_fusion.2), channel_id=1, source_target_pairs={{0,1},{1,0},{2,3},{3,2},{4,5},{5,4},{6,7},{7,6},{8,9},{9,8},{10,11... | collective-permute-start | bytes 307208 | tf_op jit(solution)/shard_map/ppermute | solution.py:395
  81.5 5.9 %collective-permute-start.17 = (f32[192,128]{1,0:T(8,128)S(1)}, f32[192,128]{1,0:T(8,128)S(1)}, u32[]{:S(2)}, u32[]{:S(2)}) collective-permute-start(f32[192,128]{1,0:T(8,128)S(1)} %slice.34), channel_id=1, source_target_pairs={{0,17},{1,16},{2,19},{3,18},{4,21},{5,20},{6,23},{7,22},{8,25},{9,... | collective-permute-start | bytes 294920 | tf_op jit(solution)/shard_map/ppermute | solution.py:395
  87.4 18.5 %collective-permute-start.25 = (bf16[128,4096]{1,0:T(8,128)(2,1)S(1)}, bf16[128,4096]{1,0:T(8,128)(2,1)S(1)}, u32[]{:S(2)}, u32[]{:S(2)}) collective-permute-start(bf16[128,4096]{1,0:T(8,128)(2,1)S(1)} %get-tuple-element.89.hidden_ref), channel_id=1, source_target_pairs={{24,32},{32,24},{56,64},{64,56},{88,96},{96,88},{120,128},{128,120... | collective-permute-start | bytes 3145736 | tf_op jit(solution)/shard_map/ppermute | solution.py:479
  89.4 6.0 %collective-permute-start.20 = (f32[200,128]{1,0:T(8,128)S(1)}, f32[200,128]{1,0:T(8,128)S(1)}, u32[]{:S(2)}, u32[]{:S(2)}) collective-permute-start(f32[200,128]{1,0:T(8,128)S(1)} %pad_maximum_fusion.3.own_ref.refs_0_), channel_id=1, source_target_pairs={{0,6},{1,7},{2,4},{3,5},{4,2},{5,3},{6,0},{7,1},{8,14},{9,15},{10,... | collective-permute-start | bytes 307208 | tf_op jit(solution)/shard_map/ppermute | solution.py:395
  92.1 6.2 %collective-permute-start.19 = (f32[200,128]{1,0:T(8,128)S(1)}, f32[200,128]{1,0:T(8,128)S(1)}, u32[]{:S(2)}, u32[]{:S(2)}) collective-permute-start(f32[200,128]{1,0:T(8,128)S(1)} %pad_maximum_fusion.3.own_ref.refs_0_), channel_id=1, source_target_pairs={{0,4},{1,5},{2,6},{3,7},{4,0},{5,1},{6,2},{7,3},{8,12},{9,13},{10,... | collective-permute-start | bytes 307208 | tf_op jit(solution)/shard_map/ppermute | solution.py:395
  93.0 5.3 %collective-permute-start.18 = (f32[200,128]{1,0:T(8,128)S(1)}, f32[200,128]{1,0:T(8,128)S(1)}, u32[]{:S(2)}, u32[]{:S(2)}) collective-permute-start(f32[200,128]{1,0:T(8,128)S(1)} %pad_maximum_fusion.3.own_ref.refs_0_), channel_id=1, source_target_pairs={{0,2},{1,3},{2,0},{3,1},{4,6},{5,7},{6,4},{7,5},{8,10},{9,11},{10,... | collective-permute-start | bytes 307208 | tf_op jit(solution)/shard_map/ppermute | solution.py:395
  93.6 12.4 %collective-permute-start.21 = (f32[200,128]{1,0:T(8,128)S(1)}, f32[200,128]{1,0:T(8,128)S(1)}, u32[]{:S(2)}, u32[]{:S(2)}) collective-permute-start(f32[200,128]{1,0:T(8,128)S(1)} %pad_maximum_fusion.3.own_ref.refs_0_), channel_id=1, source_target_pairs={{0,8},{8,0},{16,24},{24,16},{32,40},{40,32},{48,56},{56,48},{64,72... | collective-permute-start | bytes 307208 | tf_op jit(solution)/shard_map/ppermute | solution.py:392
  95.3 10.6 %collective-permute-start.24 = (f32[200,128]{1,0:T(8,128)S(1)}, f32[200,128]{1,0:T(8,128)S(1)}, u32[]{:S(2)}, u32[]{:S(2)}) collective-permute-start(f32[200,128]{1,0:T(8,128)S(1)} %collective-permute-done.20.three_ref.refs_3_), channel_id=1, source_target_pairs={{0,8},{8,0},{16,24},{24,16},{32,40},{40,32},{48,56},{56,48},{64,72... | collective-permute-start | bytes 307208 | tf_op jit(solution)/shard_map/ppermute | solution.py:392
  98.3 7.7 %collective-permute-start.23 = (f32[200,128]{1,0:T(8,128)S(1)}, f32[200,128]{1,0:T(8,128)S(1)}, u32[]{:S(2)}, u32[]{:S(2)}) collective-permute-start(f32[200,128]{1,0:T(8,128)S(1)} %collective-permute-done.19.two_ref.refs_2_), channel_id=1, source_target_pairs={{0,8},{8,0},{16,24},{24,16},{32,40},{40,32},{48,56},{56,48},{64,72... | collective-permute-start | bytes 307208 | tf_op jit(solution)/shard_map/ppermute | solution.py:392
  98.3 7.7 %collective-permute-start.22 = (f32[200,128]{1,0:T(8,128)S(1)}, f32[200,128]{1,0:T(8,128)S(1)}, u32[]{:S(2)}, u32[]{:S(2)}) collective-permute-start(f32[200,128]{1,0:T(8,128)S(1)} %collective-permute-done.18.one_ref.refs_1_), channel_id=1, source_target_pairs={{0,8},{8,0},{16,24},{24,16},{32,40},{40,32},{48,56},{56,48},{64,72... | collective-permute-start | bytes 307208 | tf_op jit(solution)/shard_map/ppermute | solution.py:392

commit v4 on v3

--- a/solution.py
+++ b/solution.py
@@ -473,10 +473,10 @@
         cost=(1, 1),
         limit=16,
     )
-    piece = total(piece, [(2, 1)])
-    piece, hidden, partial = tied((jnp.concatenate([piece, sums]), hidden, partial))
+    far_sum, sent, partial = tied((meet(piece, 2, 1), hidden, partial))
+    hidden_outside = lax.ppermute(sent, "frame", crossing(frames, False))
+    piece = jnp.concatenate([piece + far_sum, sums])
     got = [piece] + [meet(piece, 0, 2 * b) for b in (1, 2, 3)]
-    hidden_outside = lax.ppermute(hidden, "frame", crossing(frames, False))
     others = [mate(v) for v in got]
     staged, sems = pltpu.VMEM(raw_in.shape, BF16), pltpu.SemaphoreType.DMA((10,))
     (input_grad,) = call(

time: 110 us -> 109 us (level)
  no operation moved by 1% of the time
where the time goes in v4:
time: 109 us; the launch traced here: 108 us
  starting transfers between devices  43.1 us (40%)
  waiting for transfers between devices  36.7 us (34%)
  Pallas kernels  25.3 us (23%)
  local copies, waits for them, and re-layouts  1.27 us (1%)
    pallas_call x9, Pallas kernels, call(): pl.pallas_call(kernel, out_shape=[jax.ShapeDtypeStruct(s, d) for s, d in...  25.3 us
    ppermute x13, starting transfers between devices, meet(): lax.ppermute(v, ('frame', 'chan'), both(frame_bits, chan_bits, frames, pe...  23.8 us
    ppermute x13, waiting for transfers between devices, meet(): lax.ppermute(v, ('frame', 'chan'), both(frame_bits, chan_bits, frames, pe...  21.6 us
    ppermute x1, waiting for transfers between devices, body(): outside_grad = lax.ppermute(late_grad, 'frame', crossing(frames, False))  7.83 us
    all_to_all x1, starting transfers between devices, body(): received = lax.all_to_all(payload, 'chan', 0, 0, tiled=True)  5.4 us
    ppermute x8, starting transfers between devices, body(): mate = lambda v: lax.ppermute(v, 'frame', partner(1, frames))  5.36 us
    ppermute x1, waiting for transfers between devices, body(): hidden_outside = lax.ppermute(sent, 'frame', crossing(frames, False))  4.65 us
    ppermute x1, starting transfers between devices, body(): cross = lambda v: lax.ppermute(v, 'frame', neighbour(frames))  3.33 us
  transfers between devices with their start and end apart: 27, of which 13 were waited for; matrix products, arithmetic and copies ran while one was open for 0% of the time, Pallas kernels for 17%

profile of v4, /device:TPU:32, one launch (start us, length us, event | category | flops | bytes accessed | tf_op | source)
XLA Modules:
  0.0 108.4 jit_solution(13838818041276458809)
XLA Ops:
  2.7 2.5 %shard_map.102 = (bf16[128,4096]{1,0:T(8,128)(2,1)S(1)}, f32[8,40,128]{2,1,0:T(8,128)}) custom-call(s32[4]{0:T(128)S(1)} %pad_add_fusion.me_ref, bf16[128,32,128]{2,1,0:T(8,128)(2,1)S(1)} %bitcast.21), custom_call_target="tpu_custom_call" | custom-call | bytes 2097152 | tf_op jit(solution)/shard_map/pallas_call | solution.py:44
  5.2 5.4 %all-to-all-start = ((f32[8,40,128]{2,1,0:T(8,128)}), f32[8,40,128]{2,1,0:T(8,128)S(1)}, u32[]{:S(2)}, u32[]{:S(2)}) async-start(f32[8,40,128]{2,1,0:T(8,128)} %get-tuple-element.53), calls=%async_computation | async-start | bytes 327680 | tf_op jit(solution)/shard_map/all_to_all | solution.py:405
  11.6 3.3 %collective-permute-start.4 = (bf16[128,2048]{1,0:T(8,128)(2,1)}, bf16[128,2048]{1,0:T(8,128)(2,1)}, u32[]{:S(2)}, u32[]{:S(2)}) collective-permute-start(bf16[128,2048]{1,0:T(8,128)(2,1)} %get-tuple-element.65.grad_ref), channel_id=1, source_target_pairs={{8,16},{16,8},{24,32},{32,24},{40,48},{48,40},{56,64},{64,56},{72,... | collective-permute-start | bytes 1572872 | tf_op jit(solution)/shard_map/ppermute | solution.py:391
  14.9 2.5 %all-to-all-done.received_ref = f32[8,40,128]{2,1,0:T(8,128)S(1)} async-done(((f32[8,40,128]{2,1,0:T(8,128)}), f32[8,40,128]{2,1,0:T(8,128)S(1)}, u32[]{:S(2)}, u32[]{:S(2)}) %all-to-all-start) | async-done | bytes 163872 | tf_op jit(solution)/shard_map/all_to_all | solution.py:405
  18.1 4.1 %collective-permute-start = (bf16[128,2048]{1,0:T(8,128)(2,1)S(1)}, bf16[128,2048]{1,0:T(8,128)(2,1)S(1)}, u32[]{:S(2)}, u32[]{:S(2)}) collective-permute-start(bf16[128,2048]{1,0:T(8,128)(2,1)S(1)} %get-tuple-element.64.grad_ref), channel_id=1, source_target_pairs={{0,8},{8,0},{16,24},{24,16},{32,40},{40,32},{48,56},{56,48},{64,72... | collective-permute-start | bytes 1572872 | tf_op jit(solution)/shard_map/ppermute | solution.py:392
  22.4 4.3 %shard_map.104 = (bf16[384,4352]{1,0:T(8,128)(2,1)S(1)}, bf16[128,4096]{1,0:T(8,128)(2,1)S(1)}, f32[128,4096]{1,0:T(8,128)S(1)}, f32[128,128]{1,0:T(8,128)S(1)}) custom-call(s32[4]{0:T(128)S(1)} %pad_add_fusion.me_ref, bf16[128,4096]{1,0:T(8,128)(2,1)S(1)} %get-tuple-element.51.plane_ref.refs_1_, f32[8,40,128]{2,1,0:T(8,128)S(1)} %all-to-all-done.received_ref, ...), custom_call_target="tpu_custom_call" | custom-call | flops 1000 | bytes 1048576 | tf_op jit(solution)/shard_map/pallas_call | solution.py:44
  26.7 1.9 %collective-permute-start.1 = (bf16[128,2048]{1,0:T(8,128)(2,1)S(1)}, bf16[128,2048]{1,0:T(8,128)(2,1)S(1)}, u32[]{:S(2)}, u32[]{:S(2)}) collective-permute-start(bf16[128,2048]{1,0:T(8,128)(2,1)S(1)} %get-tuple-element.64.grad_ref), channel_id=1, source_target_pairs={{24,32},{32,24},{56,64},{64,56},{88,96},{96,88},{120,128},{128,120... | collective-permute-start | bytes 1572872 | tf_op jit(solution)/shard_map/ppermute | solution.py:422
  28.7 3.2 %shard_map.105 = (bf16[128,2048]{1,0:T(8,128)(2,1)S(1)}, f32[384,128]{1,0:T(8,128)S(1)}, f32[384,384]{1,0:T(8,128)S(1)}, f32[128,128]{1,0:T(8,128)S(1)}) custom-call(s32[4]{0:T(128)S(1)} %pad_add_fusion.me_ref, bf16[384,4352]{1,0:T(8,128)(2,1)S(1)} %get-tuple-element.59.act_ref, bf16[128,4096]{1,0:T(8,128)(2,1)S(1)} %get-tuple-element.89.hidden_ref, ...), custom_call_target="tpu_custom_call" | custom-call | flops 1000 | bytes 1048576 | tf_op jit(solution)/shard_map/pallas_call | solution.py:44
  31.9 7.8 %collective-permute-done.1.cross_ref = bf16[128,2048]{1,0:T(8,128)(2,1)S(1)} collective-permute-done((bf16[128,2048]{1,0:T(8,128)(2,1)S(1)}, bf16[128,2048]{1,0:T(8,128)(2,1)S(1)}, u32[]{:S(2)}, u32[]{:S(2)}) %collective-permute-start.1) | collective-permute-done | bytes 524320 | tf_op jit(solution)/shard_map/ppermute | solution.py:422
  39.7 2.6 %shard_map.106 = (bf16[128,2048]{1,0:T(8,128)(2,1)S(1)}, f32[4,192,128]{2,1,0:T(8,128)S(1)}, f32[4,192,128]{2,1,0:T(8,128)S(1)}, f32[64,128]{1,0:T(8,128)S(1)}) custom-call(s32[4]{0:T(128)S(1)} %pad_add_fusion.me_ref, bf16[384,4352]{1,0:T(8,128)(2,1)S(1)} %get-tuple-element.59.act_ref, bf16[128,4096]{1,0:T(8,128)(2,1)S(1)} %get-tuple-element.89.hidden_ref, ...), custom_call_target="tpu_custom_call" | custom-call | flops 1000 | bytes 1048576 | tf_op jit(solution)/shard_map/pallas_call | solution.py:44
  42.9 1.7 %collective-permute-start.6 = (f32[64,128]{1,0:T(8,128)S(1)}, f32[64,128]{1,0:T(8,128)S(1)}, u32[]{:S(2)}, u32[]{:S(2)}) collective-permute-start(f32[64,128]{1,0:T(8,128)S(1)} %get-tuple-element.71), channel_id=1, source_target_pairs={{0,1},{1,0},{2,3},{3,2},{4,5},{5,4},{6,7},{7,6},{8,9},{9,8},{10,11... | collective-permute-start | bytes 98312 | tf_op jit(solution)/shard_map/ppermute | solution.py:395
  44.6 2.2 %collective-permute-done.6.near_ref = f32[64,128]{1,0:T(8,128)S(1)} collective-permute-done((f32[64,128]{1,0:T(8,128)S(1)}, f32[64,128]{1,0:T(8,128)S(1)}, u32[]{:S(2)}, u32[]{:S(2)}) %collective-permute-start.6) | collective-permute-done | bytes 32800 | tf_op jit(solution)/shard_map/ppermute | solution.py:395
  46.8 2.1 %collective-permute-start.7 = (f32[224,128]{1,0:T(8,128)S(1)}, f32[224,128]{1,0:T(8,128)S(1)}, u32[]{:S(2)}, u32[]{:S(2)}) collective-permute-start(f32[224,128]{1,0:T(8,128)S(1)} %get-tuple-element.99), channel_id=1, source_target_pairs={{0,2},{1,3},{2,0},{3,1},{4,6},{5,7},{6,4},{7,5},{8,10},{9,11},{10,... | collective-permute-start | bytes 344072 | tf_op jit(solution)/shard_map/ppermute | solution.py:395
  49.0 2.1 %collective-permute-start.9 = (f32[224,128]{1,0:T(8,128)S(1)}, f32[224,128]{1,0:T(8,128)S(1)}, u32[]{:S(2)}, u32[]{:S(2)}) collective-permute-start(f32[224,128]{1,0:T(8,128)S(1)} %get-tuple-element.100), channel_id=1, source_target_pairs={{0,6},{1,7},{2,4},{3,5},{4,2},{5,3},{6,0},{7,1},{8,14},{9,15},{10,... | collective-permute-start | bytes 344072 | tf_op jit(solution)/shard_map/ppermute | solution.py:395
  52.4 5.0 %collective-permute-done.8 = f32[192,128]{1,0:T(8,128)S(1)} collective-permute-done((f32[192,128]{1,0:T(8,128)S(1)}, f32[192,128]{1,0:T(8,128)S(1)}, u32[]{:S(2)}, u32[]{:S(2)}) %collective-permute-start.8) | collective-permute-done | bytes 98336 | tf_op jit(solution)/shard_map/ppermute | solution.py:395
  57.6 2.2 %collective-permute-start.13 = (f32[192,128]{1,0:T(8,128)S(1)}, f32[192,128]{1,0:T(8,128)S(1)}, u32[]{:S(2)}, u32[]{:S(2)}) collective-permute-start(f32[192,128]{1,0:T(8,128)S(1)} %fusion), channel_id=1, source_target_pairs={{0,96},{1,97},{2,98},{3,99},{4,100},{5,101},{6,102},{7,103},{8,104... | collective-permute-start | bytes 294920 | tf_op jit(solution)/shard_map/ppermute | solution.py:395
  59.8 1.5 %collective-permute-start.12 = (f32[192,128]{1,0:T(8,128)S(1)}, f32[192,128]{1,0:T(8,128)S(1)}, u32[]{:S(2)}, u32[]{:S(2)}) collective-permute-start(f32[192,128]{1,0:T(8,128)S(1)} %fusion), channel_id=1, source_target_pairs={{0,64},{1,65},{2,66},{3,67},{4,68},{5,69},{6,70},{7,71},{8,72},{9,... | collective-permute-start | bytes 294920 | tf_op jit(solution)/shard_map/ppermute | solution.py:395
  61.2 1.4 %collective-permute-start.11 = (f32[192,128]{1,0:T(8,128)S(1)}, f32[192,128]{1,0:T(8,128)S(1)}, u32[]{:S(2)}, u32[]{:S(2)}) collective-permute-start(f32[192,128]{1,0:T(8,128)S(1)} %fusion), channel_id=1, source_target_pairs={{0,32},{1,33},{2,34},{3,35},{4,36},{5,37},{6,38},{7,39},{8,40},{9,... | collective-permute-start | bytes 294920 | tf_op jit(solution)/shard_map/ppermute | solution.py:395
  62.6 5.3 %shard_map.107 = (f32[128,4096]{1,0:T(8,128)S(1)}, f32[8,128]{1,0:T(8,128)S(1)}) custom-call(s32[4]{0:T(128)S(1)} %pad_add_fusion.me_ref, bf16[128,2048]{1,0:T(8,128)(2,1)S(1)} %get-tuple-element.76.early_ref, bf16[128,2048]{1,0:T(8,128)(2,1)S(1)} %get-tuple-element.77.late_ref, f32[64,128]{1,0:T(8,128)S(1)} %collective-permute-done.6.near_ref, ...), custom_call_target="tpu_custom_call" | custom-call | flops 1000 | bytes 1048576 | tf_op jit(solution)/shard_map/pallas_call | solution.py:44
  68.9 4.2 %collective-permute-start.14 = (f32[192,128]{1,0:T(8,128)S(1)}, f32[192,128]{1,0:T(8,128)S(1)}, u32[]{:S(2)}, u32[]{:S(2)}) collective-permute-start(f32[192,128]{1,0:T(8,128)S(1)} %add_add_fusion), channel_id=1, source_target_pairs={{0,224},{1,225},{2,226},{3,227},{4,228},{5,229},{6,230},{7,231},{8... | collective-permute-start | bytes 294920 | tf_op jit(solution)/shard_map/ppermute | solution.py:395
  73.1 3.5 %collective-permute-done.14 = f32[192,128]{1,0:T(8,128)S(1)} collective-permute-done((f32[192,128]{1,0:T(8,128)S(1)}, f32[192,128]{1,0:T(8,128)S(1)}, u32[]{:S(2)}, u32[]{:S(2)}) %collective-permute-start.14) | collective-permute-done | bytes 98336 | tf_op jit(solution)/shard_map/ppermute | solution.py:395
  77.7 3.8 %collective-permute-done.15 = f32[200,128]{1,0:T(8,128)S(1)} collective-permute-done((f32[200,128]{1,0:T(8,128)S(1)}, f32[200,128]{1,0:T(8,128)S(1)}, u32[]{:S(2)}, u32[]{:S(2)}) %collective-permute-start.15) | collective-permute-done | bytes 102432 | tf_op jit(solution)/shard_map/ppermute | solution.py:395
  81.5 3.0 %collective-permute-start.17 = (f32[192,128]{1,0:T(8,128)S(1)}, f32[192,128]{1,0:T(8,128)S(1)}, u32[]{:S(2)}, u32[]{:S(2)}) collective-permute-start(f32[192,128]{1,0:T(8,128)S(1)} %slice.34), channel_id=1, source_target_pairs={{0,17},{1,16},{2,19},{3,18},{4,21},{5,20},{6,23},{7,22},{8,25},{9,... | collective-permute-start | bytes 294920 | tf_op jit(solution)/shard_map/ppermute | solution.py:395
  84.5 1.7 %shard_map.108.refs_8_ = f32[128,32,128]{2,1,0:T(8,128)S(1)} custom-call(s32[4]{0:T(128)S(1)} %pad_add_fusion.me_ref, bf16[128,4096]{1,0:T(8,128)(2,1)S(1)} %get-tuple-element.89.hidden_ref, bf16[128,4096]{1,0:T(8,128)(2,1)S(1)} %collective-permute-done.10.mate_ref, bf16[128,4096]{1,0:T(8,128)(2,1)S(1)} %collective-permute-done.16.inside_ref, ...), custom_call_target="tpu_custom_call" | custom-call | flops 1 | bytes 1 | tf_op jit(solution)/shard_map/pallas_call | solution.py:44
  86.1 1.3 %collective-permute-done.17 = f32[192,128]{1,0:T(8,128)S(1)} collective-permute-done((f32[192,128]{1,0:T(8,128)S(1)}, f32[192,128]{1,0:T(8,128)S(1)}, u32[]{:S(2)}, u32[]{:S(2)}) %collective-permute-start.17) | collective-permute-done | bytes 98336 | tf_op jit(solution)/shard_map/ppermute | solution.py:395
  87.4 1.9 %collective-permute-start.25 = (bf16[128,4096]{1,0:T(8,128)(2,1)S(1)}, bf16[128,4096]{1,0:T(8,128)(2,1)S(1)}, u32[]{:S(2)}, u32[]{:S(2)}) collective-permute-start(bf16[128,4096]{1,0:T(8,128)(2,1)S(1)} %get-tuple-element.89.hidden_ref), channel_id=1, source_target_pairs={{24,32},{32,24},{56,64},{64,56},{88,96},{96,88},{120,128},{128,120... | collective-permute-start | bytes 3145736 | tf_op jit(solution)/shard_map/ppermute | solution.py:477
  89.4 2.7 %collective-permute-start.20 = (f32[200,128]{1,0:T(8,128)S(1)}, f32[200,128]{1,0:T(8,128)S(1)}, u32[]{:S(2)}, u32[]{:S(2)}) collective-permute-start(f32[200,128]{1,0:T(8,128)S(1)} %pad_maximum_fusion.3.own_ref.refs_0_), channel_id=1, source_target_pairs={{0,6},{1,7},{2,4},{3,5},{4,2},{5,3},{6,0},{7,1},{8,14},{9,15},{10,... | collective-permute-start | bytes 307208 | tf_op jit(solution)/shard_map/ppermute | solution.py:395
  93.6 1.8 %collective-permute-done.20.three_ref.refs_3_ = f32[200,128]{1,0:T(8,128)S(1)} collective-permute-done((f32[200,128]{1,0:T(8,128)S(1)}, f32[200,128]{1,0:T(8,128)S(1)}, u32[]{:S(2)}, u32[]{:S(2)}) %collective-permute-start.20) | collective-permute-done | bytes 102432 | tf_op jit(solution)/shard_map/ppermute | solution.py:395
  95.3 2.9 %collective-permute-done.19.two_ref.refs_2_ = f32[200,128]{1,0:T(8,128)S(1)} collective-permute-done((f32[200,128]{1,0:T(8,128)S(1)}, f32[200,128]{1,0:T(8,128)S(1)}, u32[]{:S(2)}, u32[]{:S(2)}) %collective-permute-start.19) | collective-permute-done | bytes 102432 | tf_op jit(solution)/shard_map/ppermute | solution.py:395
  98.8 2.5 %shard_map.109 = bf16[128,32,128]{2,1,0:T(8,128)(2,1)} custom-call(f32[200,128]{1,0:T(8,128)S(1)} %pad_maximum_fusion.3.own_ref.refs_0_, f32[200,128]{1,0:T(8,128)S(1)} %collective-permute-done.18.one_ref.refs_1_, f32[200,128]{1,0:T(8,128)S(1)} %collective-permute-done.19.two_ref.refs_2_, f32[200,128]{1,0:T(8,128)S(1)} %collective-permute-done.20.three_ref.refs_3_, ...), custom_call_target="tpu_custom_call" | custom-call | flops 1000 | bytes 1048576 | tf_op jit(solution)/shard_map/pallas_call | solution.py:44
  101.3 4.6 %collective-permute-done.25.refs_9_ = bf16[128,4096]{1,0:T(8,128)(2,1)S(1)} collective-permute-done((bf16[128,4096]{1,0:T(8,128)(2,1)S(1)}, bf16[128,4096]{1,0:T(8,128)(2,1)S(1)}, u32[]{:S(2)}, u32[]{:S(2)}) %collective-permute-start.25) | collective-permute-done | bytes 1048608 | tf_op jit(solution)/shard_map/ppermute | solution.py:477
  105.9 2.3 %shard_map.110 = (f32[6,192,128]{2,1,0:T(8,128)}, f32[2,192,128]{2,1,0:T(8,128)}, bf16[128,32,128]{2,1,0:T(8,128)(2,1)}) custom-call(s32[4]{0:T(128)S(1)} %pad_add_fusion.me_ref, f32[200,128]{1,0:T(8,128)S(1)} %pad_maximum_fusion.3.own_ref.refs_0_, f32[200,128]{1,0:T(8,128)S(1)} %collective-permute-done.18.one_ref.refs_1_, ...), custom_call_target="tpu_custom_call" | custom-call | flops 1000 | bytes 1048576 | tf_op jit(solution)/shard_map/pallas_call | solution.py:44
  (56 shorter events, 10.0 us)
Async XLA Ops:
  0.6 28.0 %copy-start.3 = (bf16[3,128,128]{2,1,0:T(8,128)(2,1)S(1)}, bf16[3,128,128]{2,1,0:T(8,128)(2,1)}, u32[]{:S(2)}) copy-start(bf16[3,128,128]{2,1,0:T(8,128)(2,1)} %refs_10_.1) | copy-start | bytes 294916
  1.5 1.2 %copy-start = (bf16[1,128,32,128]{3,2,1,0:T(8,128)(2,1)S(1)}, bf16[1,128,32,128]{3,2,1,0:T(8,128)(2,1)}, u32[]{:S(2)}) copy-start(bf16[1,128,32,128]{3,2,1,0:T(8,128)(2,1)} %param.7) | copy-start | bytes 3145732
  2.7 7.9 %copy-start.2 = (bf16[1,128,32,128]{3,2,1,0:T(8,128)(2,1)S(1)}, bf16[1,128,32,128]{3,2,1,0:T(8,128)(2,1)}, u32[]{:S(2)}) copy-start(bf16[1,128,32,128]{3,2,1,0:T(8,128)(2,1)} %param.8) | copy-start | bytes 3145732
  2.7 19.7 %copy-start.4 = (bf16[9,128,128]{2,1,0:T(8,128)(2,1)S(1)}, bf16[9,128,128]{2,1,0:T(8,128)(2,1)}, u32[]{:S(2)}) copy-start(bf16[9,128,128]{2,1,0:T(8,128)(2,1)} %refs_0_.1) | copy-start | bytes 884740
  5.2 12.2 %all-to-all-start = ((f32[8,40,128]{2,1,0:T(8,128)}), f32[8,40,128]{2,1,0:T(8,128)S(1)}, u32[]{:S(2)}, u32[]{:S(2)}) async-start(f32[8,40,128]{2,1,0:T(8,128)} %get-tuple-element.53), calls=%async_computation | async-start | bytes 327680 | tf_op jit(solution)/shard_map/all_to_all | solution.py:405
  11.6 17.1 %collective-permute-start.4 = (bf16[128,2048]{1,0:T(8,128)(2,1)}, bf16[128,2048]{1,0:T(8,128)(2,1)}, u32[]{:S(2)}, u32[]{:S(2)}) collective-permute-start(bf16[128,2048]{1,0:T(8,128)(2,1)} %get-tuple-element.65.grad_ref), channel_id=1, source_target_pairs={{8,16},{16,8},{24,32},{32,24},{40,48},{48,40},{56,64},{64,56},{72,... | collective-permute-start | bytes 1572872 | tf_op jit(solution)/shard_map/ppermute | solution.py:391
  17.4 14.4 %collective-permute-start.2 = (bf16[128,2048]{1,0:T(8,128)(2,1)S(1)}, bf16[128,2048]{1,0:T(8,128)(2,1)S(1)}, u32[]{:S(2)}, u32[]{:S(2)}) collective-permute-start(bf16[128,2048]{1,0:T(8,128)(2,1)S(1)} %get-tuple-element.64.grad_ref), channel_id=1, source_target_pairs={{8,16},{16,8},{40,48},{48,40},{72,80},{80,72},{104,112},{112,104},... | collective-permute-start | bytes 1572872 | tf_op jit(solution)/shard_map/ppermute | solution.py:410
  18.1 13.8 %collective-permute-start = (bf16[128,2048]{1,0:T(8,128)(2,1)S(1)}, bf16[128,2048]{1,0:T(8,128)(2,1)S(1)}, u32[]{:S(2)}, u32[]{:S(2)}) collective-permute-start(bf16[128,2048]{1,0:T(8,128)(2,1)S(1)} %get-tuple-element.64.grad_ref), channel_id=1, source_target_pairs={{0,8},{8,0},{16,24},{24,16},{32,40},{40,32},{48,56},{56,48},{64,72... | collective-permute-start | bytes 1572872 | tf_op jit(solution)/shard_map/ppermute | solution.py:392
  22.3 6.4 %collective-permute-start.3 = (bf16[128,2048]{1,0:T(8,128)(2,1)}, bf16[128,2048]{1,0:T(8,128)(2,1)S(1)}, u32[]{:S(2)}, u32[]{:S(2)}) collective-permute-start(bf16[128,2048]{1,0:T(8,128)(2,1)} %get-tuple-element.65.grad_ref), channel_id=1, source_target_pairs={{0,8},{8,0},{16,24},{24,16},{32,40},{40,32},{48,56},{56,48},{64,72... | collective-permute-start | bytes 1572872 | tf_op jit(solution)/shard_map/ppermute | solution.py:392
  26.7 13.0 %collective-permute-start.1 = (bf16[128,2048]{1,0:T(8,128)(2,1)S(1)}, bf16[128,2048]{1,0:T(8,128)(2,1)S(1)}, u32[]{:S(2)}, u32[]{:S(2)}) collective-permute-start(bf16[128,2048]{1,0:T(8,128)(2,1)S(1)} %get-tuple-element.64.grad_ref), channel_id=1, source_target_pairs={{24,32},{32,24},{56,64},{64,56},{88,96},{96,88},{120,128},{128,120... | collective-permute-start | bytes 1572872 | tf_op jit(solution)/shard_map/ppermute | solution.py:422
  42.3 2.3 %collective-permute-start.5 = (f32[4,192,128]{2,1,0:T(8,128)S(1)}, f32[4,192,128]{2,1,0:T(8,128)S(1)}, u32[]{:S(2)}, u32[]{:S(2)}) collective-permute-start(f32[4,192,128]{2,1,0:T(8,128)S(1)} %get-tuple-element.70), channel_id=1, source_target_pairs={{0,8},{8,0},{16,24},{24,16},{32,40},{40,32},{48,56},{56,48},{64,72... | collective-permute-start | bytes 1179656 | tf_op jit(solution)/shard_map/ppermute | solution.py:392
  42.9 3.9 %collective-permute-start.6 = (f32[64,128]{1,0:T(8,128)S(1)}, f32[64,128]{1,0:T(8,128)S(1)}, u32[]{:S(2)}, u32[]{:S(2)}) collective-permute-start(f32[64,128]{1,0:T(8,128)S(1)} %get-tuple-element.71), channel_id=1, source_target_pairs={{0,1},{1,0},{2,3},{3,2},{4,5},{5,4},{6,7},{7,6},{8,9},{9,8},{10,11... | collective-permute-start | bytes 98312 | tf_op jit(solution)/shard_map/ppermute | solution.py:395
  46.8 10.8 %collective-permute-start.10 = (bf16[128,4096]{1,0:T(8,128)(2,1)S(1)}, bf16[128,4096]{1,0:T(8,128)(2,1)S(1)}, u32[]{:S(2)}, u32[]{:S(2)}) collective-permute-start(bf16[128,4096]{1,0:T(8,128)(2,1)S(1)} %get-tuple-element.89.hidden_ref), channel_id=1, source_target_pairs={{0,8},{8,0},{16,24},{24,16},{32,40},{40,32},{48,56},{56,48},{64,72... | collective-permute-start | bytes 3145736 | tf_op jit(solution)/shard_map/ppermute | solution.py:392
  46.8 10.5 %collective-permute-start.7 = (f32[224,128]{1,0:T(8,128)S(1)}, f32[224,128]{1,0:T(8,128)S(1)}, u32[]{:S(2)}, u32[]{:S(2)}) collective-permute-start(f32[224,128]{1,0:T(8,128)S(1)} %get-tuple-element.99), channel_id=1, source_target_pairs={{0,2},{1,3},{2,0},{3,1},{4,6},{5,7},{6,4},{7,5},{8,10},{9,11},{10,... | collective-permute-start | bytes 344072 | tf_op jit(solution)/shard_map/ppermute | solution.py:395
  49.0 8.6 %collective-permute-start.9 = (f32[224,128]{1,0:T(8,128)S(1)}, f32[224,128]{1,0:T(8,128)S(1)}, u32[]{:S(2)}, u32[]{:S(2)}) collective-permute-start(f32[224,128]{1,0:T(8,128)S(1)} %get-tuple-element.100), channel_id=1, source_target_pairs={{0,6},{1,7},{2,4},{3,5},{4,2},{5,3},{6,0},{7,1},{8,14},{9,15},{10,... | collective-permute-start | bytes 344072 | tf_op jit(solution)/shard_map/ppermute | solution.py:395
  51.0 6.4 %collective-permute-start.8 = (f32[192,128]{1,0:T(8,128)S(1)}, f32[192,128]{1,0:T(8,128)S(1)}, u32[]{:S(2)}, u32[]{:S(2)}) collective-permute-start(f32[192,128]{1,0:T(8,128)S(1)} %get-tuple-element.98), channel_id=1, source_target_pairs={{0,4},{1,5},{2,6},{3,7},{4,0},{5,1},{6,2},{7,3},{8,12},{9,13},{10,... | collective-permute-start | bytes 294920 | tf_op jit(solution)/shard_map/ppermute | solution.py:395
  51.6 29.8 %collective-permute-start.16 = (bf16[128,4096]{1,0:T(8,128)(2,1)S(1)}, bf16[128,4096]{1,0:T(8,128)(2,1)S(1)}, u32[]{:S(2)}, u32[]{:S(2)}) collective-permute-start(bf16[128,4096]{1,0:T(8,128)(2,1)S(1)} %get-tuple-element.89.hidden_ref), channel_id=1, source_target_pairs={{8,16},{16,8},{40,48},{48,40},{72,80},{80,72},{104,112},{112,104},... | collective-permute-start | bytes 3145736 | tf_op jit(solution)/shard_map/ppermute | solution.py:446
  57.6 10.3 %collective-permute-start.13 = (f32[192,128]{1,0:T(8,128)S(1)}, f32[192,128]{1,0:T(8,128)S(1)}, u32[]{:S(2)}, u32[]{:S(2)}) collective-permute-start(f32[192,128]{1,0:T(8,128)S(1)} %fusion), channel_id=1, source_target_pairs={{0,96},{1,97},{2,98},{3,99},{4,100},{5,101},{6,102},{7,103},{8,104... | collective-permute-start | bytes 294920 | tf_op jit(solution)/shard_map/ppermute | solution.py:395
  59.8 8.3 %collective-permute-start.12 = (f32[192,128]{1,0:T(8,128)S(1)}, f32[192,128]{1,0:T(8,128)S(1)}, u32[]{:S(2)}, u32[]{:S(2)}) collective-permute-start(f32[192,128]{1,0:T(8,128)S(1)} %fusion), channel_id=1, source_target_pairs={{0,64},{1,65},{2,66},{3,67},{4,68},{5,69},{6,70},{7,71},{8,72},{9,... | collective-permute-start | bytes 294920 | tf_op jit(solution)/shard_map/ppermute | solution.py:395
  61.2 7.7 %collective-permute-start.11 = (f32[192,128]{1,0:T(8,128)S(1)}, f32[192,128]{1,0:T(8,128)S(1)}, u32[]{:S(2)}, u32[]{:S(2)}) collective-permute-start(f32[192,128]{1,0:T(8,128)S(1)} %fusion), channel_id=1, source_target_pairs={{0,32},{1,33},{2,34},{3,35},{4,36},{5,37},{6,38},{7,39},{8,40},{9,... | collective-permute-start | bytes 294920 | tf_op jit(solution)/shard_map/ppermute | solution.py:395
  62.6 21.9 %copy-start.1 = (bf16[1,128,32,128]{3,2,1,0:T(8,128)(2,1)S(1)}, bf16[1,128,32,128]{3,2,1,0:T(8,128)(2,1)}, u32[]{:S(2)}) copy-start(bf16[1,128,32,128]{3,2,1,0:T(8,128)(2,1)} %param.7) | copy-start | bytes 3145732
  68.9 7.8 %collective-permute-start.14 = (f32[192,128]{1,0:T(8,128)S(1)}, f32[192,128]{1,0:T(8,128)S(1)}, u32[]{:S(2)}, u32[]{:S(2)}) collective-permute-start(f32[192,128]{1,0:T(8,128)S(1)} %add_add_fusion), channel_id=1, source_target_pairs={{0,224},{1,225},{2,226},{3,227},{4,228},{5,229},{6,230},{7,231},{8... | collective-permute-start | bytes 294920 | tf_op jit(solution)/shard_map/ppermute | solution.py:395
  76.7 4.7 %collective-permute-start.15 = (f32[200,128]{1,0:T(8,128)S(1)}, f32[200,128]{1,0:T(8,128)S(1)}, u32[]{:S(2)}, u32[]{:S(2)}) collective-permute-start(f32[200,128]{1,0:T(8,128)S(1)} %pad_maximum_fusion.2), channel_id=1, source_target_pairs={{0,1},{1,0},{2,3},{3,2},{4,5},{5,4},{6,7},{7,6},{8,9},{9,8},{10,11... | collective-permute-start | bytes 307208 | tf_op jit(solution)/shard_map/ppermute | solution.py:395
  81.5 5.9 %collective-permute-start.17 = (f32[192,128]{1,0:T(8,128)S(1)}, f32[192,128]{1,0:T(8,128)S(1)}, u32[]{:S(2)}, u32[]{:S(2)}) collective-permute-start(f32[192,128]{1,0:T(8,128)S(1)} %slice.34), channel_id=1, source_target_pairs={{0,17},{1,16},{2,19},{3,18},{4,21},{5,20},{6,23},{7,22},{8,25},{9,... | collective-permute-start | bytes 294920 | tf_op jit(solution)/shard_map/ppermute | solution.py:395
  87.4 18.5 %collective-permute-start.25 = (bf16[128,4096]{1,0:T(8,128)(2,1)S(1)}, bf16[128,4096]{1,0:T(8,128)(2,1)S(1)}, u32[]{:S(2)}, u32[]{:S(2)}) collective-permute-start(bf16[128,4096]{1,0:T(8,128)(2,1)S(1)} %get-tuple-element.89.hidden_ref), channel_id=1, source_target_pairs={{24,32},{32,24},{56,64},{64,56},{88,96},{96,88},{120,128},{128,120... | collective-permute-start | bytes 3145736 | tf_op jit(solution)/shard_map/ppermute | solution.py:477
  89.4 6.0 %collective-permute-start.20 = (f32[200,128]{1,0:T(8,128)S(1)}, f32[200,128]{1,0:T(8,128)S(1)}, u32[]{:S(2)}, u32[]{:S(2)}) collective-permute-start(f32[200,128]{1,0:T(8,128)S(1)} %pad_maximum_fusion.3.own_ref.refs_0_), channel_id=1, source_target_pairs={{0,6},{1,7},{2,4},{3,5},{4,2},{5,3},{6,0},{7,1},{8,14},{9,15},{10,... | collective-permute-start | bytes 307208 | tf_op jit(solution)/shard_map/ppermute | solution.py:395
  92.1 6.2 %collective-permute-start.19 = (f32[200,128]{1,0:T(8,128)S(1)}, f32[200,128]{1,0:T(8,128)S(1)}, u32[]{:S(2)}, u32[]{:S(2)}) collective-permute-start(f32[200,128]{1,0:T(8,128)S(1)} %pad_maximum_fusion.3.own_ref.refs_0_), channel_id=1, source_target_pairs={{0,4},{1,5},{2,6},{3,7},{4,0},{5,1},{6,2},{7,3},{8,12},{9,13},{10,... | collective-permute-start | bytes 307208 | tf_op jit(solution)/shard_map/ppermute | solution.py:395
  93.0 5.3 %collective-permute-start.18 = (f32[200,128]{1,0:T(8,128)S(1)}, f32[200,128]{1,0:T(8,128)S(1)}, u32[]{:S(2)}, u32[]{:S(2)}) collective-permute-start(f32[200,128]{1,0:T(8,128)S(1)} %pad_maximum_fusion.3.own_ref.refs_0_), channel_id=1, source_target_pairs={{0,2},{1,3},{2,0},{3,1},{4,6},{5,7},{6,4},{7,5},{8,10},{9,11},{10,... | collective-permute-start | bytes 307208 | tf_op jit(solution)/shard_map/ppermute | solution.py:395
  93.6 12.4 %collective-permute-start.21 = (f32[200,128]{1,0:T(8,128)S(1)}, f32[200,128]{1,0:T(8,128)S(1)}, u32[]{:S(2)}, u32[]{:S(2)}) collective-permute-start(f32[200,128]{1,0:T(8,128)S(1)} %pad_maximum_fusion.3.own_ref.refs_0_), channel_id=1, source_target_pairs={{0,8},{8,0},{16,24},{24,16},{32,40},{40,32},{48,56},{56,48},{64,72... | collective-permute-start | bytes 307208 | tf_op jit(solution)/shard_map/ppermute | solution.py:392
  95.3 10.6 %collective-permute-start.24 = (f32[200,128]{1,0:T(8,128)S(1)}, f32[200,128]{1,0:T(8,128)S(1)}, u32[]{:S(2)}, u32[]{:S(2)}) collective-permute-start(f32[200,128]{1,0:T(8,128)S(1)} %collective-permute-done.20.three_ref.refs_3_), channel_id=1, source_target_pairs={{0,8},{8,0},{16,24},{24,16},{32,40},{40,32},{48,56},{56,48},{64,72... | collective-permute-start | bytes 307208 | tf_op jit(solution)/shard_map/ppermute | solution.py:392
  98.3 7.7 %collective-permute-start.23 = (f32[200,128]{1,0:T(8,128)S(1)}, f32[200,128]{1,0:T(8,128)S(1)}, u32[]{:S(2)}, u32[]{:S(2)}) collective-permute-start(f32[200,128]{1,0:T(8,128)S(1)} %collective-permute-done.19.two_ref.refs_2_), channel_id=1, source_target_pairs={{0,8},{8,0},{16,24},{24,16},{32,40},{40,32},{48,56},{56,48},{64,72... | collective-permute-start | bytes 307208 | tf_op jit(solution)/shard_map/ppermute | solution.py:392
  98.3 7.7 %collective-permute-start.22 = (f32[200,128]{1,0:T(8,128)S(1)}, f32[200,128]{1,0:T(8,128)S(1)}, u32[]{:S(2)}, u32[]{:S(2)}) collective-permute-start(f32[200,128]{1,0:T(8,128)S(1)} %collective-permute-done.18.one_ref.refs_1_), channel_id=1, source_target_pairs={{0,8},{8,0},{16,24},{24,16},{32,40},{40,32},{48,56},{56,48},{64,72... | collective-permute-start | bytes 307208 | tf_op jit(solution)/shard_map/ppermute | solution.py:392
